TPU v7x, 512 devices: a whole 4x8x8 slice. The times are simulated.
512 devices in a mesh: mem: 64 (over x, y, core), tile: 8 (over z).
Axes of the slice: x: 4, y: 8, z: 8, core: 2. Of those that a mesh axis runs over, the one named last changes fastest.
Arguments:
- background_members: bfloat16 [64, 2, 256, 4096], P('mem', None, None, 'tile'), may hold values from -6 to 6
- measured_datum: float32 [2, 64, 8, 64], P(None, 'mem', 'tile'), may hold values from -12 to 12
- measurement_noise_spread: float32 [2, 64, 8, 64], P(None, 'mem', 'tile'), may hold values from 0.1 to 2
- measured_point: int32 [2, 64, 8, 64], P(None, 'mem', 'tile'), may hold values from 0 to 4095
- active_measure_total: int32 [2, 64, 8], P(None, 'mem', 'tile'), may hold values from 1 to 64, as said below
Outputs:
- analysis: bfloat16 [64, 2, 256, 4096], P('mem', None, None, 'tile')
Inputs may be any that keep to these rules, and one draw needn't show every extreme that they name: `measured_point`: cell number within the owning tile, level * 4 * 512 + row in tile * 512 + column in tile. `active_measure_total`: slots from this count on are not live; in every batch some tile has all 64 slots live.
All inputs are finite; a program needn't handle non-finite values.
Results may differ from a plain program's by a relative error of at most 0.001.
Values may be sent and summed in bfloat16 or wider, within the bound.
No kernel may reach another device: no remote copies, remote signals or barrier semaphores. Data moves between devices by JAX's collectives and lax.ppermute only.
A program may use at most 64 MiB of HBM per device.

v0:
```python
import math

import jax
import jax.numpy as jnp
from jax import lax
from jax.sharding import PartitionSpec as P

MEMBER_TOTAL = 64
PATCH_SPAN_NORTH = 4
PATCH_SPAN_EAST = 512
NB = 2


def from_behind(block, axis, distance):
    devices = range(lax.axis_size(axis))
    route = [(i - distance, i) for i in devices if i - distance in devices]
    return lax.ppermute(block, axis, route)


def gaspari(distance, cutoff):
    scaled = distance / (0.5 * cutoff)
    clipped = jnp.maximum(scaled, 1.0)
    inside_part = (
        ((-0.25 * scaled + 0.5) * scaled + 0.625) * scaled - 5.0 / 3.0
    ) * scaled * scaled + 1.0
    outside_part = (
        ((((scaled / 12.0 - 0.5) * scaled + 0.625) * scaled + 5.0 / 3.0) * scaled - 5.0) * scaled
        + 4.0
        - 2.0 / (3.0 * clipped)
    )
    return jnp.where(
        scaled <= 1.0, inside_part, jnp.where(scaled < 2.0, outside_part, jnp.zeros_like(scaled))
    )


def make_packet(columns, obs_values, error_var, live_count, site_ids):
    prior_mean = jnp.mean(columns, axis=0)
    prior_pert = columns - prior_mean
    variance = jnp.sum(prior_pert * prior_pert, axis=0) / (MEMBER_TOTAL - 1)
    denominator = variance + error_var
    live_mask = (jnp.arange(columns.shape[1], dtype=jnp.int32) < live_count).astype(columns.dtype)
    factor = 1.0 / (1.0 + jnp.sqrt(error_var / denominator))
    mean_weight = live_mask * (obs_values - prior_mean) / denominator
    pert_weight = live_mask * factor / denominator
    return jnp.concatenate(
        [prior_pert, mean_weight[None], pert_weight[None], site_ids.astype(columns.dtype)[None]],
        axis=0,
    )


def unpack(neighbours):
    slots = neighbours.shape[3]
    flattened = jnp.transpose(neighbours.reshape(9, MEMBER_TOTAL + 3, slots), (1, 0, 2)).reshape(
        MEMBER_TOTAL + 3, 9 * slots
    )
    perturb = flattened[:MEMBER_TOTAL]
    site_ids = flattened[MEMBER_TOTAL + 2].astype(jnp.int32)
    slot_of = jnp.arange(9 * slots, dtype=jnp.int32) // slots
    row_shift = slot_of // 3 - 1
    col_shift = slot_of % 3 - 1
    obs_row = (
        row_shift * PATCH_SPAN_NORTH
        + site_ids % (PATCH_SPAN_NORTH * PATCH_SPAN_EAST) // PATCH_SPAN_EAST
    ).astype(perturb.dtype)
    obs_col = (col_shift * PATCH_SPAN_EAST + site_ids % PATCH_SPAN_EAST).astype(perturb.dtype)
    obs_level = (site_ids // (PATCH_SPAN_NORTH * PATCH_SPAN_EAST)).astype(perturb.dtype)
    return (
        perturb,
        flattened[MEMBER_TOTAL],
        flattened[MEMBER_TOTAL + 1],
        obs_row,
        obs_col,
        obs_level,
    )


def update_block(block_state, cell_ids, unpacked):
    perturb, mean_weight, pert_weight, obs_row, obs_col, obs_level = unpacked
    kind = block_state.dtype
    cell_mean = jnp.mean(block_state, axis=0)
    cell_pert = block_state - cell_mean
    covariance = lax.dot_general(
        perturb, cell_pert, (((0,), (0,)), ((), ())), precision=lax.Precision.HIGHEST
    ) / (MEMBER_TOTAL - 1)
    cell_level = (cell_ids // (PATCH_SPAN_NORTH * PATCH_SPAN_EAST)).astype(kind)
    cell_row = (cell_ids % (PATCH_SPAN_NORTH * PATCH_SPAN_EAST) // PATCH_SPAN_EAST).astype(kind)
    cell_col = (cell_ids % PATCH_SPAN_EAST).astype(kind)
    row_gap = obs_row[:, None] - cell_row[None, :]
    col_gap = obs_col[:, None] - cell_col[None, :]
    distance = jnp.sqrt(row_gap * row_gap + col_gap * col_gap)
    weight = gaspari(distance, 2 * PATCH_SPAN_NORTH) / (
        1.0 + jnp.abs(obs_level[:, None] - cell_level[None, :])
    )
    gain_terms = weight * covariance
    mean_step = jnp.dot(mean_weight[None, :], gain_terms, precision=lax.Precision.HIGHEST)[0]
    pert_step = jnp.dot(perturb, gain_terms * pert_weight[:, None], precision=lax.Precision.HIGHEST)
    return cell_mean + mean_step + cell_pert - pert_step


def select_columns(values, wanted):
    leading = values.shape[:-1]
    arranged = values.reshape(leading + (3, 3, values.shape[-1] // 9))
    return arranged[..., wanted, :].reshape(leading + (-1,))


def strip_update(member_fields, unpacked):
    member_count, cell_total = member_fields.shape
    span_east = PATCH_SPAN_EAST
    reach = 2 * PATCH_SPAN_NORTH
    line_count = cell_total // span_east
    strip_width = math.gcd(span_east, 128)
    arranged = member_fields.reshape(member_count, line_count, span_east)
    line_start = jnp.arange(line_count, dtype=jnp.int32)[:, None] * span_east
    results = []
    for strip_start in range(0, span_east, strip_width):
        wanted = [1]
        if strip_start < reach:
            wanted = [0] + wanted
        if strip_start + strip_width > span_east - reach:
            wanted = wanted + [2]
        chosen = tuple((select_columns(values, wanted) for values in unpacked))
        strip_state = jnp.transpose(
            arranged[:, :, strip_start : strip_start + strip_width], (1, 0, 2)
        )
        strip_ids = line_start + strip_start + jnp.arange(strip_width, dtype=jnp.int32)[None, :]
        updated = lax.map(
            lambda operands: update_block(operands[0], operands[1], chosen),
            (strip_state, strip_ids),
        )
        results.append(jnp.transpose(updated, (1, 0, 2)))
    return jnp.concatenate(results, axis=2).reshape(member_count, cell_total)


def spread(packet):
    west_side = from_behind(packet, "tile", 1)
    east_side = from_behind(packet, "tile", -1)
    windowed = jnp.concatenate([west_side, packet, east_side], axis=1)
    above_row = from_behind(windowed, "mem", 1)
    below_row = from_behind(windowed, "mem", -1)
    return jnp.concatenate([above_row, windowed, below_row], axis=0)


def on_device(
    background_members,
    measured_datum,
    measurement_noise_spread,
    measured_point,
    active_measure_total,
):
    patch_field_block = lax.all_to_all(
        background_members, "mem", split_axis=2, concat_axis=0, tiled=True
    )
    member_count, level_count, tile_rows, tile_cols = patch_field_block.shape
    member_fields = patch_field_block.astype(jnp.float32).reshape(
        member_count, level_count * tile_rows * tile_cols
    )

    def packet_of(columns, batch_index):
        packet = make_packet(
            columns,
            measured_datum[batch_index, 0, 0],
            measurement_noise_spread[batch_index, 0, 0],
            active_measure_total[batch_index, 0, 0],
            measured_point[batch_index, 0, 0],
        )
        return packet[None, None]

    neighbours = spread(packet_of(jnp.take(member_fields, measured_point[0, 0, 0], axis=1), 0))
    for batch_index in range(NB):
        if batch_index > 0:
            neighbours = spread(
                packet_of(
                    jnp.take(member_fields, measured_point[batch_index, 0, 0], axis=1), batch_index
                )
            )
        member_fields = strip_update(member_fields, unpack(neighbours))
    returned = member_fields.reshape(member_count, level_count, tile_rows, tile_cols).astype(
        jnp.bfloat16
    )
    return lax.all_to_all(returned, "mem", split_axis=0, concat_axis=2, tiled=True)


def solution(mesh):
    return jax.shard_map(
        on_device,
        mesh=mesh,
        in_specs=(
            P("mem", None, None, "tile"),
            P(None, "mem", "tile", None),
            P(None, "mem", "tile", None),
            P(None, "mem", "tile", None),
            P(None, "mem", "tile"),
        ),
        out_specs=P("mem", None, None, "tile"),
        check_vma=False,
    )
```

profile of v0, /device:TPU:71, one launch (start us, length us, event | category | flops | bytes accessed | tf_op | source)
XLA Modules:
  0.0 224.6 jit_solution(15237863216621765345)
XLA Ops:
  0.0 2.4 %copy.384 = bf16[1,2,256,512]{3,1,0,2:T(2,128)(2,1)} copy(bf16[1,2,256,512]{3,2,1,0:T(8,128)(2,1)} %param.71) | data formatting | bytes 1048576 | tf_op args[0]
  2.4 11.2 %all-to-all-start = ((bf16[1,2,256,512]{3,1,0,2:T(2,128)(2,1)}), bf16[1,2,256,512]{3,1,0,2:T(2,128)(2,1)S(1)}, u32[]{:S(2)}, u32[]{:S(2)}) async-start(bf16[1,2,256,512]{3,1,0,2:T(2,128)(2,1)} %copy.384), calls=%async_computation | async-start | bytes 1048576 | tf_op jit(solution)/shard_map/all_to_all | solution.py:150
  13.7 0.6 fusion.149
  14.8 16.1 %all-to-all-done = bf16[1,2,256,512]{3,1,0,2:T(2,128)(2,1)S(1)} async-done(((bf16[1,2,256,512]{3,1,0,2:T(2,128)(2,1)}), bf16[1,2,256,512]{3,1,0,2:T(2,128)(2,1)S(1)}, u32[]{:S(2)}, u32[]{:S(2)}) %all-to-all-start) | async-done | bytes 524320 | tf_op jit(solution)/shard_map/all_to_all | solution.py:150
  30.8 0.6 copy.385
  31.5 0.6 gather_fusion.24
  32.4 0.7 fusion.144
  33.5 4.0 %collective-permute-start = (f32[1,1,67,64]{2,3,1,0:T(8,128)S(1)}, f32[1,1,67,64]{2,3,1,0:T(8,128)S(1)}, u32[]{:S(2)}, u32[]{:S(2)}) collective-permute-start(f32[1,1,67,64]{2,3,1,0:T(8,128)S(1)} %maximum_bitcast_fusion), channel_id=1, source_target_pairs={{0,1},{1,2},{2,3},{3,4},{4,5},{5,6},{6,7},{8,9},{9,10},{10,11},{11... | collective-permute-start | bytes 51464 | tf_op jit(solution)/shard_map/ppermute | solution.py:17
  37.5 1.9 collective-permute-start.1
  39.7 3.1 %collective-permute-done.1 = f32[1,1,67,64]{2,3,1,0:T(8,128)S(1)} collective-permute-done((f32[1,1,67,64]{2,3,1,0:T(8,128)S(1)}, f32[1,1,67,64]{2,3,1,0:T(8,128)S(1)}, u32[]{:S(2)}, u32[]{:S(2)}) %collective-permute-start.1) | collective-permute-done | bytes 17184 | tf_op jit(solution)/shard_map/ppermute | solution.py:17
  42.8 3.6 %collective-permute-start.2 = (f32[1,3,67,64]{2,3,1,0:T(8,128)S(1)}, f32[1,3,67,64]{2,3,1,0:T(8,128)S(1)}, u32[]{:S(2)}, u32[]{:S(2)}) collective-permute-start(f32[1,3,67,64]{2,3,1,0:T(8,128)S(1)} %pad_maximum_fusion.4), channel_id=1, source_target_pairs={{0,8},{8,16},{16,24},{24,32},{32,40},{40,48},{48,56},{56,64},{64,7... | collective-permute-start | bytes 154376 | tf_op jit(solution)/shard_map/ppermute | solution.py:17
  46.4 1.9 collective-permute-start.3
  48.4 3.9 %collective-permute-done.3 = f32[1,3,67,64]{2,3,1,0:T(8,128)S(1)} collective-permute-done((f32[1,3,67,64]{2,3,1,0:T(8,128)S(1)}, f32[1,3,67,64]{2,3,1,0:T(8,128)S(1)}, u32[]{:S(2)}, u32[]{:S(2)}) %collective-permute-start.3) | collective-permute-done | bytes 51488 | tf_op jit(solution)/shard_map/ppermute | solution.py:17
  61.1 11.2 %while.124 = (s32[]{:T(128)}, f32[8,64,128]{2,1,0:T(8,128)S(1)}, f32[8,64,128]{2,1,0:T(8,128)S(1)}, f32[3,2,64]{2,1,0:T(2,128)}, s32[8,128]{1,0:T(8,128)S(1)}, /...) while((s32[]{:T(128)}, f32[8,64,128]{2,1,0:T(8,128)S(1)}, ...), condition=%wide.wide.region_4.6_spmd, body=%wide.wide.region_2.0_spmd.sunk | while | flops 78100864 | bytes 936617 | solution.py:126
  61.2 0.6 fusion.315
  62.6 0.6 fusion.315
  64.0 0.6 fusion.315
  65.4 0.6 fusion.315
  68.2 0.6 fusion.315
  69.6 0.6 fusion.315
  72.6 12.5 %while.120 = (s32[]{:T(128)}, f32[8,64,128]{2,1,0:T(8,128)S(1)}, f32[8,64,128]{2,1,0:T(8,128)S(1)}, f32[3,1,64]{2,1,0:T(1,128)S(1)}, s32[8,128]{1,0:T(8,128)S(1)...) while((s32[]{:T(128)}, f32[8,64,128]{2,1,0:T(8,128)S(1)}, ...), condition=%wide.region_7.9_spmd, body=%wide.region_5.8_spmd.sunk | while | flops 39074176 | bytes 586653 | solution.py:126
  85.2 12.5 %while.121 = (s32[]{:T(128)}, f32[8,64,128]{2,1,0:T(8,128)S(1)}, f32[8,64,128]{2,1,0:T(8,128)S(1)}, f32[3,1,64]{2,1,0:T(1,128)S(1)}, s32[8,128]{1,0:T(8,128)S(1)...) while((s32[]{:T(128)}, f32[8,64,128]{2,1,0:T(8,128)S(1)}, ...), condition=%wide.region_10.12_spmd, body=%wide.region_8.11_spmd.sunk | while | flops 39074176 | bytes 586653 | solution.py:126
  99.0 11.2 %while.125 = (s32[]{:T(128)}, f32[8,64,128]{2,1,0:T(8,128)S(1)}, f32[8,64,128]{2,1,0:T(8,128)S(1)}, f32[3,2,64]{2,1,0:T(2,128)}, s32[8,128]{1,0:T(8,128)S(1)}, /...) while((s32[]{:T(128)}, f32[8,64,128]{2,1,0:T(8,128)S(1)}, ...), condition=%wide.wide.region_13.15_spmd, body=%wide.wide.region_11.14_spmd.sunk | while | flops 78100864 | bytes 936617 | solution.py:126
  103.3 0.6 fusion.323
  110.3 2.0 copy.421
  112.3 2.2 gather_fusion.25
  114.8 0.6 fusion.145
  115.8 5.2 %collective-permute-start.4 = (f32[1,1,67,64]{2,3,1,0:T(8,128)S(1)}, f32[1,1,67,64]{2,3,1,0:T(8,128)S(1)}, u32[]{:S(2)}, u32[]{:S(2)}) collective-permute-start(f32[1,1,67,64]{2,3,1,0:T(8,128)S(1)} %maximum_bitcast_fusion.1), channel_id=1, source_target_pairs={{0,1},{1,2},{2,3},{3,4},{4,5},{5,6},{6,7},{8,9},{9,10},{10,11},{11... | collective-permute-start | bytes 51464 | tf_op jit(solution)/shard_map/ppermute | solution.py:17
  121.0 1.9 collective-permute-start.5
  122.9 4.2 %collective-permute-done.5 = f32[1,1,67,64]{2,3,1,0:T(8,128)S(1)} collective-permute-done((f32[1,1,67,64]{2,3,1,0:T(8,128)S(1)}, f32[1,1,67,64]{2,3,1,0:T(8,128)S(1)}, u32[]{:S(2)}, u32[]{:S(2)}) %collective-permute-start.5) | collective-permute-done | bytes 17184 | tf_op jit(solution)/shard_map/ppermute | solution.py:17
  127.1 3.0 %collective-permute-start.6 = (f32[1,3,67,64]{2,3,1,0:T(8,128)S(1)}, f32[1,3,67,64]{2,3,1,0:T(8,128)S(1)}, u32[]{:S(2)}, u32[]{:S(2)}) collective-permute-start(f32[1,3,67,64]{2,3,1,0:T(8,128)S(1)} %pad_maximum_fusion.5), channel_id=1, source_target_pairs={{0,8},{8,16},{16,24},{24,32},{32,40},{40,48},{48,56},{56,64},{64,7... | collective-permute-start | bytes 154376 | tf_op jit(solution)/shard_map/ppermute | solution.py:17
  130.1 3.5 %collective-permute-start.7 = (f32[1,3,67,64]{2,3,1,0:T(8,128)S(1)}, f32[1,3,67,64]{2,3,1,0:T(8,128)S(1)}, u32[]{:S(2)}, u32[]{:S(2)}) collective-permute-start(f32[1,3,67,64]{2,3,1,0:T(8,128)S(1)} %pad_maximum_fusion.5), channel_id=1, source_target_pairs={{8,0},{16,8},{24,16},{32,24},{40,32},{48,40},{56,48},{64,56},{72,6... | collective-permute-start | bytes 154376 | tf_op jit(solution)/shard_map/ppermute | solution.py:17
  133.8 2.6 %collective-permute-done.7 = f32[1,3,67,64]{2,3,1,0:T(8,128)S(1)} collective-permute-done((f32[1,3,67,64]{2,3,1,0:T(8,128)S(1)}, f32[1,3,67,64]{2,3,1,0:T(8,128)S(1)}, u32[]{:S(2)}, u32[]{:S(2)}) %collective-permute-start.7) | collective-permute-done | bytes 51488 | tf_op jit(solution)/shard_map/ppermute | solution.py:17
  145.2 11.3 %while.126 = (s32[]{:T(128)}, bf16[8,64,128]{2,1,0:T(8,128)(2,1)S(1)}, f32[8,64,128]{2,1,0:T(8,128)S(1)}, f32[3,2,64]{2,1,0:T(2,128)}, s32[8,128]{1,0:T(8,128)S(...) while((s32[]{:T(128)}, ...), condition=%wide.wide.region_18.20_spmd, body=%wide.wide.region_16.19_spmd.sunk | while | flops 78100864 | bytes 936617 | solution.py:126
  149.5 0.6 fusion.331
  150.9 0.6 fusion.331
  153.7 0.6 fusion.331
  155.1 0.6 fusion.331
  156.7 12.6 %while.122 = (s32[]{:T(128)}, bf16[8,64,128]{2,1,0:T(8,128)(2,1)S(1)}, f32[8,64,128]{2,1,0:T(8,128)S(1)}, f32[3,1,64]{2,1,0:T(1,128)S(1)}, s32[8,128]{1,0:T(8,12...) while((s32[]{:T(128)}, ...), condition=%wide.region_21.23_spmd, body=%wide.region_19.22_spmd.sunk | while | flops 39074176 | bytes 586653 | solution.py:126
  169.3 12.6 %while.123 = (s32[]{:T(128)}, bf16[8,64,128]{2,1,0:T(8,128)(2,1)S(1)}, f32[8,64,128]{2,1,0:T(8,128)S(1)}, f32[3,1,64]{2,1,0:T(1,128)S(1)}, s32[8,128]{1,0:T(8,12...) while((s32[]{:T(128)}, ...), condition=%wide.region_24.26_spmd, body=%wide.region_22.25_spmd.sunk | while | flops 39074176 | bytes 586653 | solution.py:126
  183.2 11.3 %while.127 = (s32[]{:T(128)}, bf16[8,64,128]{2,1,0:T(8,128)(2,1)S(1)}, f32[8,64,128]{2,1,0:T(8,128)S(1)}, f32[3,2,64]{2,1,0:T(2,128)}, s32[8,128]{1,0:T(8,128)S(...) while((s32[]{:T(128)}, ...), condition=%wide.wide.region_27.29_spmd, body=%wide.wide.region_25.28_spmd.sunk | while | flops 78100864 | bytes 936617 | solution.py:126
  184.7 0.6 fusion.339
  187.5 0.6 fusion.339
  188.9 0.6 fusion.339
  191.7 0.6 fusion.339
  193.1 0.6 fusion.339
  195.0 28.4 %all_to_all.27 = bf16[64,2,4,512]{3,2,1,0:T(4,128)(2,1)S(1)} all-to-all(bf16[64,2,4,512]{3,2,1,0:T(4,128)(2,1)S(1)} %copy.460), channel_id=1, replica_groups=mesh['mem'=64,'tile'=8] {'mem'}, dimensions={0} | all-to-all | bytes 1048576 | tf_op jit(solution)/shard_map/all_to_all | solution.py:180
  223.8 0.8 copy.458
  (971 shorter events, 107.0 us)
Async XLA Ops:
  0.0 13.7 %copy-start.23 = (s32[2,1,1,64]{3,2,1,0:T(1,128)S(1)}, s32[2,1,1,64]{3,2,1,0:T(1,128)}, u32[]{:S(2)}) copy-start(s32[2,1,1,64]{3,2,1,0:T(1,128)} %param.74) | copy-start | bytes 1540
  0.0 13.7 %copy-start.24 = (s32[2,1,1]{0,2,1:T(1,128)S(1)}, s32[2,1,1]{0,2,1:T(1,128)}, u32[]{:S(2)}) copy-start(s32[2,1,1]{0,2,1:T(1,128)} %param.75) | copy-start | bytes 28
  2.4 30.0 %copy-start.25 = (f32[2,1,1,64]{3,2,1,0:T(1,128)S(1)}, f32[2,1,1,64]{3,2,1,0:T(1,128)}, u32[]{:S(2)}) copy-start(f32[2,1,1,64]{3,2,1,0:T(1,128)} %param.72) | copy-start | bytes 1540
  2.4 30.0 %copy-start.26 = (f32[2,1,1,64]{3,2,1,0:T(1,128)S(1)}, f32[2,1,1,64]{3,2,1,0:T(1,128)}, u32[]{:S(2)}) copy-start(f32[2,1,1,64]{3,2,1,0:T(1,128)} %param.73) | copy-start | bytes 1540
  2.4 37.0 %copy-start.27 = (s32[2]{0:T(128)S(1)}, s32[2]{0:T(128)}, u32[]{:S(2)}) copy-start(s32[2]{0:T(128)} %constant.1928) | copy-start | bytes 28
  2.4 28.4 %all-to-all-start = ((bf16[1,2,256,512]{3,1,0,2:T(2,128)(2,1)}), bf16[1,2,256,512]{3,1,0,2:T(2,128)(2,1)S(1)}, u32[]{:S(2)}, u32[]{:S(2)}) async-start(bf16[1,2,256,512]{3,1,0,2:T(2,128)(2,1)} %copy.384), calls=%async_computation | async-start | bytes 1048576 | tf_op jit(solution)/shard_map/all_to_all | solution.py:150
  33.5 6.2 %collective-permute-start = (f32[1,1,67,64]{2,3,1,0:T(8,128)S(1)}, f32[1,1,67,64]{2,3,1,0:T(8,128)S(1)}, u32[]{:S(2)}, u32[]{:S(2)}) collective-permute-start(f32[1,1,67,64]{2,3,1,0:T(8,128)S(1)} %maximum_bitcast_fusion), channel_id=1, source_target_pairs={{0,1},{1,2},{2,3},{3,4},{4,5},{5,6},{6,7},{8,9},{9,10},{10,11},{11... | collective-permute-start | bytes 51464 | tf_op jit(solution)/shard_map/ppermute | solution.py:17
  37.5 5.3 %collective-permute-start.1 = (f32[1,1,67,64]{2,3,1,0:T(8,128)S(1)}, f32[1,1,67,64]{2,3,1,0:T(8,128)S(1)}, u32[]{:S(2)}, u32[]{:S(2)}) collective-permute-start(f32[1,1,67,64]{2,3,1,0:T(8,128)S(1)} %maximum_bitcast_fusion), channel_id=1, source_target_pairs={{1,0},{2,1},{3,2},{4,3},{5,4},{6,5},{7,6},{9,8},{10,9},{11,10},{12... | collective-permute-start | bytes 51464 | tf_op jit(solution)/shard_map/ppermute | solution.py:17
  42.8 5.6 %collective-permute-start.2 = (f32[1,3,67,64]{2,3,1,0:T(8,128)S(1)}, f32[1,3,67,64]{2,3,1,0:T(8,128)S(1)}, u32[]{:S(2)}, u32[]{:S(2)}) collective-permute-start(f32[1,3,67,64]{2,3,1,0:T(8,128)S(1)} %pad_maximum_fusion.4), channel_id=1, source_target_pairs={{0,8},{8,16},{16,24},{24,32},{32,40},{40,48},{48,56},{56,64},{64,7... | collective-permute-start | bytes 154376 | tf_op jit(solution)/shard_map/ppermute | solution.py:17
  46.4 5.9 %collective-permute-start.3 = (f32[1,3,67,64]{2,3,1,0:T(8,128)S(1)}, f32[1,3,67,64]{2,3,1,0:T(8,128)S(1)}, u32[]{:S(2)}, u32[]{:S(2)}) collective-permute-start(f32[1,3,67,64]{2,3,1,0:T(8,128)S(1)} %pad_maximum_fusion.4), channel_id=1, source_target_pairs={{8,0},{16,8},{24,16},{32,24},{40,32},{48,40},{56,48},{64,56},{72,6... | collective-permute-start | bytes 154376 | tf_op jit(solution)/shard_map/ppermute | solution.py:17
  60.2 0.6 copy-start.6
  60.3 0.6 copy-start.10
  60.4 0.6 copy-start.14
  60.5 0.6 copy-start.18
  60.6 0.6 copy-start.21
  98.1 0.6 copy-start.3
  98.2 0.6 copy-start.4
  98.2 0.6 copy-start.7
  98.3 0.6 copy-start.11
  98.4 0.6 copy-start.15
  115.8 7.1 %collective-permute-start.4 = (f32[1,1,67,64]{2,3,1,0:T(8,128)S(1)}, f32[1,1,67,64]{2,3,1,0:T(8,128)S(1)}, u32[]{:S(2)}, u32[]{:S(2)}) collective-permute-start(f32[1,1,67,64]{2,3,1,0:T(8,128)S(1)} %maximum_bitcast_fusion.1), channel_id=1, source_target_pairs={{0,1},{1,2},{2,3},{3,4},{4,5},{5,6},{6,7},{8,9},{9,10},{10,11},{11... | collective-permute-start | bytes 51464 | tf_op jit(solution)/shard_map/ppermute | solution.py:17
  121.0 6.1 %collective-permute-start.5 = (f32[1,1,67,64]{2,3,1,0:T(8,128)S(1)}, f32[1,1,67,64]{2,3,1,0:T(8,128)S(1)}, u32[]{:S(2)}, u32[]{:S(2)}) collective-permute-start(f32[1,1,67,64]{2,3,1,0:T(8,128)S(1)} %maximum_bitcast_fusion.1), channel_id=1, source_target_pairs={{1,0},{2,1},{3,2},{4,3},{5,4},{6,5},{7,6},{9,8},{10,9},{11,10},{12... | collective-permute-start | bytes 51464 | tf_op jit(solution)/shard_map/ppermute | solution.py:17
  127.1 6.6 %collective-permute-start.6 = (f32[1,3,67,64]{2,3,1,0:T(8,128)S(1)}, f32[1,3,67,64]{2,3,1,0:T(8,128)S(1)}, u32[]{:S(2)}, u32[]{:S(2)}) collective-permute-start(f32[1,3,67,64]{2,3,1,0:T(8,128)S(1)} %pad_maximum_fusion.5), channel_id=1, source_target_pairs={{0,8},{8,16},{16,24},{24,32},{32,40},{40,48},{48,56},{56,64},{64,7... | collective-permute-start | bytes 154376 | tf_op jit(solution)/shard_map/ppermute | solution.py:17
  130.1 6.2 %collective-permute-start.7 = (f32[1,3,67,64]{2,3,1,0:T(8,128)S(1)}, f32[1,3,67,64]{2,3,1,0:T(8,128)S(1)}, u32[]{:S(2)}, u32[]{:S(2)}) collective-permute-start(f32[1,3,67,64]{2,3,1,0:T(8,128)S(1)} %pad_maximum_fusion.5), channel_id=1, source_target_pairs={{8,0},{16,8},{24,16},{32,24},{40,32},{48,40},{56,48},{64,56},{72,6... | collective-permute-start | bytes 154376 | tf_op jit(solution)/shard_map/ppermute | solution.py:17
  133.7 11.5 %copy-start = (bf16[8,64,128]{2,1,0:T(8,128)(2,1)}, bf16[8,64,128]{2,1,0:T(8,128)(2,1)S(1)}, u32[]{:S(2)}) copy-start(bf16[8,64,128]{2,1,0:T(8,128)(2,1)S(1)} %fusion.148) | copy-start | bytes 393220
  144.2 0.6 copy-start.8
  144.3 0.6 copy-start.12
  144.4 0.6 copy-start.16
  144.5 0.6 copy-start.19
  144.6 0.6 copy-start.22
  156.7 12.6 %copy-start.2 = (bf16[8,64,128]{2,1,0:T(8,128)(2,1)S(1)}, bf16[8,64,128]{2,1,0:T(8,128)(2,1)}, u32[]{:S(2)}) copy-start(bf16[8,64,128]{2,1,0:T(8,128)(2,1)} %copy-done) | copy-start | bytes 393220
  169.3 13.9 %copy-start.1 = (bf16[8,64,128]{2,1,0:T(8,128)(2,1)S(1)}, bf16[8,64,128]{2,1,0:T(8,128)(2,1)}, u32[]{:S(2)}) copy-start(bf16[8,64,128]{2,1,0:T(8,128)(2,1)} %copy-done) | copy-start | bytes 393220
  182.2 0.6 copy-start.5
  182.3 0.6 copy-start.9
  182.4 0.6 copy-start.13
  182.5 0.6 copy-start.17
  182.6 0.6 copy-start.20
where the time goes:
time: 225 us
  matrix products  70.7 us (31%)
  local copies, waits for them, and re-layouts  44.4 us (20%)
  starting transfers between devices  36.4 us (16%)
  waiting for transfers between devices  29.9 us (13%)
  blocking collectives  28.4 us (13%)
  other arithmetic  11.7 us (5%)
  loops' own time  2.4 us (1%)
    dot_general x64, matrix products, update_block(): lax.dot_general(perturb, cell_pert, (((0,), (0,)), ((), ())), precision=l...  31.9 us
    all_to_all x1, blocking collectives, on_device(): lax.all_to_all(returned, 'mem', split_axis=0, concat_axis=2, tiled=True)  28.4 us
    dot_general x64, matrix products, update_block(): jnp.dot(perturb, gain_terms * pert_weight[:, None], precision=lax.Precisi...  25.4 us
    ppermute x8, starting transfers between devices, from_behind(): return lax.ppermute(block, axis, route)  25.1 us
    all_to_all x1, waiting for transfers between devices, on_device(): lax.all_to_all(background_members, 'mem', split_axis=2, concat_axis=0, ti...  16.1 us
    gather x38, local copies, waits for them, and re-layouts, select_columns(): return arranged[..., wanted, :].reshape(leading + (-1,))  14.3 us
    ppermute x8, waiting for transfers between devices, from_behind(): return lax.ppermute(block, axis, route)  13.8 us
    dot_general x64, matrix products, update_block(): jnp.dot(mean_weight[None, :], gain_terms, precision=lax.Precision.HIGHEST)  13.4 us
  transfers between devices with their start and end apart: 9, of which 5 were waited for; matrix products, arithmetic and copies ran while one was open for 1% of the time, Pallas kernels for 0%

commit v1 on v0

v1 whole, which is shorter than its diff:
```python
import functools

import jax
import jax.numpy as jnp
from jax import lax
from jax.experimental import pallas as pl
from jax.experimental.pallas import tpu as pltpu
from jax.sharding import PartitionSpec as P

MEMBERS = 64
LEVELS = 2
SPAN_NORTH = 4
SPAN_EAST = 512
SLOTS = 64
TILE_ROWS = 64
LINES = LEVELS * SPAN_NORTH
HALF = 256
PIECES = LINES * 2
STRIP = 128
STRIPS = SPAN_EAST // STRIP
REACH = 8
CHUNK = 64
SITE_CHUNK = 128
BATCH_LANES = 4 * SLOTS
F32 = jnp.float32
BF16 = jnp.bfloat16
VMEM_LIMIT = 48 * 1024 * 1024


def split(values):
    high = values.astype(BF16)
    return high, (values - high.astype(F32)).astype(BF16)


def relayout(wide, arranged, forward):
    for line in range(LINES):
        level, row = divmod(line, SPAN_NORTH)
        field_rows = pl.ds(level * TILE_ROWS * SPAN_NORTH + row, TILE_ROWS, stride=SPAN_NORTH)
        for strip in range(STRIPS):
            half, part = divmod(strip, 2)
            message_rows = pl.ds(2 * line + half, TILE_ROWS, stride=PIECES)
            if forward:
                arranged[part, message_rows, :] = wide[strip, field_rows, :]
            else:
                wide[strip, field_rows, :] = arranged[part, message_rows, :]


def pack_kernel(field_ref, message_ref, wide, arranged):
    for strip in range(STRIPS):
        wide[strip] = field_ref[:, strip * STRIP : (strip + 1) * STRIP].astype(F32)
    relayout(wide, arranged, True)
    for part in range(2):
        message_ref[:, part * STRIP : (part + 1) * STRIP] = arranged[part].astype(BF16)


def unpack_kernel(message_ref, field_ref, wide, arranged):
    for part in range(2):
        arranged[part] = message_ref[:, part * STRIP : (part + 1) * STRIP].astype(F32)
    relayout(wide, arranged, False)
    for strip in range(STRIPS):
        field_ref[:, strip * STRIP : (strip + 1) * STRIP] = wide[strip].astype(BF16)


def pick_kernel(field_ref, point_ref, raw_ref, scratch):
    point = point_ref[...]
    offset = point & (HALF - 1)
    piece = point >> 8
    place = lax.broadcasted_iota(jnp.int32, (HALF, 2 * SLOTS), 0)
    chooser = jnp.where(place == offset, 1.0, 0.0).astype(BF16)
    scratch[...] = jnp.dot(field_ref[...], chooser, preferred_element_type=F32)
    total = jnp.zeros((MEMBERS, 2 * SLOTS), F32)
    for index in range(PIECES):
        block = scratch[pl.ds(index, MEMBERS, stride=PIECES), :]
        total = total + jnp.where(piece == index, block, 0.0)
    raw_ref[...] = total.astype(BF16)


def weights_of(columns, datum, noise, live):
    mean = jnp.sum(columns, axis=0, keepdims=True) * (1.0 / MEMBERS)
    pert = columns - mean
    variance = jnp.sum(pert * pert, axis=0, keepdims=True) / (MEMBERS - 1)
    denominator = jnp.where(live > 0.0, variance + noise, 1.0)
    factor = 1.0 / (1.0 + jnp.sqrt(noise / denominator))
    return pert, live * (datum - mean) / denominator, live * factor / denominator


def positions(masks):
    rows, lanes = masks.shape
    before = lax.broadcasted_iota(jnp.int32, (128, 128), 0)
    after = lax.broadcasted_iota(jnp.int32, (128, 128), 1)
    triangle = jnp.where(before < after, 1.0, 0.0).astype(BF16)
    total = jnp.zeros((rows, 1), F32)
    parts = []
    for start in range(0, lanes, 128):
        block = masks[:, start : start + 128]
        rank = jnp.dot(block.astype(BF16), triangle, preferred_element_type=F32) + total
        parts.append(jnp.where(block > 0.0, rank, -1.0))
        total = total + jnp.sum(block, axis=1, keepdims=True)
    return jnp.concatenate(parts, axis=1), total


def taper(square):
    inverse = lax.rsqrt(jnp.maximum(square, 1.0))
    s = square * inverse * 0.25
    inside = (((-0.25 * s + 0.5) * s + 0.625) * s - 5.0 / 3.0) * s * s + 1.0
    outside = (
        ((((s * (1.0 / 12.0) - 0.5) * s + 0.625) * s + 5.0 / 3.0) * s - 5.0) * s
        + 4.0
        - (8.0 / 3.0) * inverse
    )
    return jnp.where(square <= 16.0, inside, jnp.where(square < 64.0, outside, 0.0))


def table_of(pert, mean_weight, pert_weight, row, col, level):
    high, low = split(pert)
    mean_high, mean_low = split(mean_weight)
    pert_high, pert_low = split(pert_weight)
    tail = [
        row.astype(F32).astype(BF16),
        (col & ~127).astype(F32).astype(BF16),
        (col & 127).astype(F32).astype(BF16),
        level.astype(F32).astype(BF16),
        mean_high,
        mean_low,
        pert_high,
        pert_low,
    ]
    lanes = pert.shape[1]
    rows = lax.broadcasted_iota(jnp.int32, (16, lanes), 0)
    block = jnp.zeros((16, lanes), F32)
    for index, line in enumerate(tail):
        block = jnp.where(rows == index, line.astype(F32), block)
    return high, low, block.astype(BF16)


def chosen_records(ranks, base, count, table):
    place = lax.broadcasted_iota(jnp.int32, (count, 1), 0).astype(F32) + base
    chooser = jnp.where(ranks == place, 1.0, 0.0).astype(BF16)
    return lax.dot_general(chooser, table, (((1,), (1,)), ((), ())), preferred_element_type=F32)


def open_records(records):
    pert = records[:, : 2 * MEMBERS].astype(BF16)
    tail = records[:, 2 * MEMBERS :]
    row = tail[:, 0:1]
    col = tail[:, 1:2] + tail[:, 2:3]
    level = tail[:, 3:4]
    mean_weight = tail[:, 4:5] + tail[:, 5:6]
    pert_weight = tail[:, 6:7] + tail[:, 7:8]
    step = mean_weight - pert_weight * (records[:, :MEMBERS] + records[:, MEMBERS : 2 * MEMBERS])
    high, low = split(step)
    return pert, row, col, level, jnp.concatenate([high, low, high], axis=0)


def advance(step, gain):
    high, low = split(gain)
    return lax.dot_general(
        step,
        jnp.concatenate([high, high, low], axis=0),
        (((0,), (0,)), ((), ())),
        preferred_element_type=F32,
    )


def level_factor(level, target):
    return (1.0 / (MEMBERS - 1)) / (1.0 + jnp.abs(level - float(target)))


def update_tile(ranks, total, table, source, state, wide_state):
    chunks = (jnp.max(total).astype(jnp.int32) + (CHUNK - 1)) // CHUNK

    def one(index, carry):
        base = (index * CHUNK).astype(F32)
        for strip in range(STRIPS):
            records = chosen_records(ranks[strip : strip + 1], base, CHUNK, table)
            pert, row, col, level, step = open_records(records)
            lane = lax.broadcasted_iota(jnp.int32, (1, STRIP), 1).astype(F32) + strip * STRIP
            across = col - lane
            across = across * across
            tapers = []
            for line in range(SPAN_NORTH):
                down = row - float(line)
                tapers.append(taper(across + down * down))
            weight = jnp.concatenate(
                [t * level_factor(level, target) for target in range(LEVELS) for t in tapers], axis=1
            )
            if wide_state:
                pert = jnp.concatenate([pert, pert[:, :MEMBERS]], axis=1)
            covariance = jnp.dot(pert, source[strip], preferred_element_type=F32)
            state[strip] = state[strip] + advance(step, weight * covariance)
        return carry

    lax.fori_loop(0, chunks, one, 0)


def analysis_kernel(
    field_ref, cat_n2, cat_n1, cat_0, cat_s1, cat_s2, meta_n2, meta_n1, meta_0, meta_s1, meta_s2,
    message_ref, wide, state, narrow, source, site_state,
):
    for part in range(2):
        wide[part] = field_ref[:, part * STRIP : (part + 1) * STRIP].astype(F32)
    for strip in range(STRIPS):
        half, part = divmod(strip, 2)
        for line in range(LINES):
            piece = wide[part, pl.ds(2 * line + half, MEMBERS, stride=PIECES), :]
            lanes = pl.ds(line * STRIP, STRIP)
            state[strip, :, lanes] = piece
            low = piece.astype(BF16)
            narrow[strip, :MEMBERS, lanes] = low
            narrow[strip, MEMBERS:, lanes] = low

    def facts(metas, rows, batch):
        lanes = pl.ds(batch * BATCH_LANES, BATCH_LANES)
        meta = jnp.concatenate([m[:, lanes] for m in metas], axis=1)
        point = meta[2:3].astype(jnp.int32)
        lane = lax.broadcasted_iota(jnp.int32, point.shape, 1)
        tile_row = (lane >> 8) - rows
        tile_col = ((lane >> 6) & 3) - 1
        row = tile_row * SPAN_NORTH + ((point >> 9) & 3)
        col = tile_col * SPAN_EAST + (point & (SPAN_EAST - 1))
        return meta[0:1], meta[1:2], meta[3:4], row, col, point >> 11

    def strip_masks(col, live):
        rows = lax.broadcasted_iota(jnp.int32, (8, col.shape[1]), 0)
        west = rows * STRIP - REACH
        inside = (col > west) & (col < west + STRIP + 2 * REACH - 1) & (rows < STRIPS)
        return jnp.where(inside, live, 0.0)

    first = jnp.concatenate(
        [c[:, pl.ds(0, BATCH_LANES)] for c in (cat_n2, cat_n1, cat_0, cat_s1, cat_s2)], axis=1
    ).astype(F32)
    datum, noise, live, row, col, level = facts((meta_n2, meta_n1, meta_0, meta_s1, meta_s2), 2, 0)
    pert, mean_weight, pert_weight = weights_of(first, datum, noise, live)
    table = jnp.concatenate(
        table_of(pert, mean_weight, pert_weight, row, col, level), axis=0
    )
    near = slice(BATCH_LANES, 4 * BATCH_LANES)
    ranks, total = positions(strip_masks(col[:, near], live[:, near]))
    update_tile(ranks, total, table[:, near], narrow, state, False)

    sites = jnp.concatenate(
        [c[:, pl.ds(BATCH_LANES, BATCH_LANES)] for c in (cat_n1, cat_0, cat_s1)], axis=1
    )
    site_state[...] = sites.astype(F32)
    datum_1, noise_1, live_1, row_1, col_1, level_1 = facts((meta_n1, meta_0, meta_s1), 1, 1)
    reached = (col > -2 * REACH) & (col < SPAN_EAST + 2 * REACH - 1)
    wanted = jnp.broadcast_to(jnp.where(reached, live, 0.0), (8, col.shape[1]))
    site_ranks, site_total = positions(wanted)
    site_row = row_1.astype(F32)
    site_col = col_1.astype(F32)
    site_level = level_1.astype(F32)
    site_tile = (row_1 >> 2).astype(F32)
    doubled = jnp.concatenate([sites, sites], axis=0)

    def one(index, carry):
        base = (index * SITE_CHUNK).astype(F32)
        records = chosen_records(site_ranks[0:1], base, SITE_CHUNK, table)
        obs, obs_row, obs_col, obs_level, step = open_records(records)
        down = obs_row - site_row
        across = obs_col - site_col
        weight = taper(down * down + across * across)
        weight = weight * ((1.0 / (MEMBERS - 1)) / (1.0 + jnp.abs(obs_level - site_level)))
        obs_tile = jnp.floor(obs_row * (1.0 / SPAN_NORTH))
        weight = jnp.where(jnp.abs(obs_tile - site_tile) <= 1.0, weight, 0.0)
        covariance = jnp.dot(obs, doubled, preferred_element_type=F32)
        site_state[...] = site_state[...] + advance(step, weight * covariance)
        return carry

    chunks = (jnp.max(site_total).astype(jnp.int32) + (SITE_CHUNK - 1)) // SITE_CHUNK
    lax.fori_loop(0, chunks, one, 0)

    pert, mean_weight, pert_weight = weights_of(site_state[...], datum_1, noise_1, live_1)
    table_1 = jnp.concatenate(
        table_of(pert, mean_weight, pert_weight, row_1, col_1, level_1), axis=0
    )
    ranks_1, total_1 = positions(strip_masks(col_1, live_1))
    for strip in range(STRIPS):
        high, low = split(state[strip])
        source[strip, :MEMBERS, :] = high
        source[strip, MEMBERS : 2 * MEMBERS, :] = high
        source[strip, 2 * MEMBERS :, :] = low
    update_tile(ranks_1, total_1, table_1, source, state, True)

    for strip in range(STRIPS):
        half, part = divmod(strip, 2)
        for line in range(LINES):
            wide[part, pl.ds(2 * line + half, MEMBERS, stride=PIECES), :] = state[
                strip, :, pl.ds(line * STRIP, STRIP)
            ]
    for part in range(2):
        message_ref[:, part * STRIP : (part + 1) * STRIP] = wide[part].astype(BF16)


def pack(field):
    return pl.pallas_call(
        pack_kernel,
        out_shape=jax.ShapeDtypeStruct((TILE_ROWS * PIECES, HALF), BF16),
        scratch_shapes=[
            pltpu.VMEM((STRIPS, LEVELS * TILE_ROWS * SPAN_NORTH, STRIP), F32),
            pltpu.VMEM((2, TILE_ROWS * PIECES, STRIP), F32),
        ],
        compiler_params=pltpu.CompilerParams(vmem_limit_bytes=VMEM_LIMIT),
        cost_estimate=pl.CostEstimate(flops=0, bytes_accessed=1 << 20, transcendentals=0),
    )(field)


def unpack(message):
    return pl.pallas_call(
        unpack_kernel,
        out_shape=jax.ShapeDtypeStruct((LEVELS * TILE_ROWS * SPAN_NORTH, SPAN_EAST), BF16),
        scratch_shapes=[
            pltpu.VMEM((STRIPS, LEVELS * TILE_ROWS * SPAN_NORTH, STRIP), F32),
            pltpu.VMEM((2, TILE_ROWS * PIECES, STRIP), F32),
        ],
        compiler_params=pltpu.CompilerParams(vmem_limit_bytes=VMEM_LIMIT),
        cost_estimate=pl.CostEstimate(flops=0, bytes_accessed=1 << 20, transcendentals=0),
    )(message)


def pick(field, points):
    return pl.pallas_call(
        pick_kernel,
        out_shape=jax.ShapeDtypeStruct((MEMBERS, 2 * SLOTS), BF16),
        scratch_shapes=[pltpu.VMEM((MEMBERS * PIECES, 2 * SLOTS), F32)],
        compiler_params=pltpu.CompilerParams(vmem_limit_bytes=VMEM_LIMIT),
        cost_estimate=pl.CostEstimate(flops=1 << 26, bytes_accessed=1 << 19, transcendentals=0),
    )(field, points)


def analyse(field, cats, metas):
    return pl.pallas_call(
        analysis_kernel,
        out_shape=jax.ShapeDtypeStruct((MEMBERS * PIECES, HALF), BF16),
        scratch_shapes=[
            pltpu.VMEM((2, MEMBERS * PIECES, STRIP), F32),
            pltpu.VMEM((STRIPS, MEMBERS, LINES * STRIP), F32),
            pltpu.VMEM((STRIPS, 2 * MEMBERS, LINES * STRIP), BF16),
            pltpu.VMEM((STRIPS, 3 * MEMBERS, LINES * STRIP), BF16),
            pltpu.VMEM((MEMBERS, 3 * BATCH_LANES), F32),
        ],
        compiler_params=pltpu.CompilerParams(vmem_limit_bytes=VMEM_LIMIT),
        cost_estimate=pl.CostEstimate(flops=1 << 30, bytes_accessed=1 << 20, transcendentals=0),
    )(field, *cats, *metas)


def from_behind(block, axis, distance):
    size = lax.axis_size(axis)
    route = [(i - distance, i) for i in range(size) if 0 <= i - distance < size]
    return lax.ppermute(block, axis, route)


def gather_row(own):
    west = from_behind(own, "tile", 1)
    east = from_behind(own, "tile", -1)
    none = jnp.zeros((own.shape[0], SLOTS), own.dtype)
    parts = []
    for batch in range(2):
        lanes = slice(batch * SLOTS, (batch + 1) * SLOTS)
        parts += [west[:, lanes], own[:, lanes], east[:, lanes], none]
    return jnp.concatenate(parts, axis=1)


def gather_column(row):
    first = row[:, :BATCH_LANES]
    return (
        from_behind(first, "mem", 2),
        from_behind(row, "mem", 1),
        row,
        from_behind(row, "mem", -1),
        from_behind(first, "mem", -2),
    )


def on_device(members, datum, noise, point, count):
    message = pack(members.reshape(LEVELS * TILE_ROWS * SPAN_NORTH, SPAN_EAST))
    field = lax.all_to_all(message, "mem", split_axis=0, concat_axis=0, tiled=True)

    point = point.reshape(1, 2 * SLOTS)
    slot = lax.broadcasted_iota(jnp.int32, (2, SLOTS), 1)
    live = (slot < count.reshape(2, 1)).astype(F32).reshape(1, 2 * SLOTS)
    meta = jnp.concatenate(
        [
            datum.reshape(1, 2 * SLOTS),
            noise.reshape(1, 2 * SLOTS),
            point.astype(F32),
            live,
            jnp.zeros((4, 2 * SLOTS), F32),
        ],
        axis=0,
    )
    metas = gather_column(gather_row(meta))
    cats = gather_column(gather_row(pick(field, point)))
    returned = analyse(field, cats, metas)
    message = lax.all_to_all(returned, "mem", split_axis=0, concat_axis=0, tiled=True)
    return unpack(message).reshape(1, LEVELS, TILE_ROWS * SPAN_NORTH, SPAN_EAST)


def solution(mesh):
    return jax.shard_map(
        on_device,
        mesh=mesh,
        in_specs=(
            P("mem", None, None, "tile"),
            P(None, "mem", "tile", None),
            P(None, "mem", "tile", None),
            P(None, "mem", "tile", None),
            P(None, "mem", "tile"),
        ),
        out_specs=P("mem", None, None, "tile"),
        check_vma=False,
    )
```

time: 225 us -> 101 us (0.45)
  the two profiles are of different devices: /device:TPU:71 before, /device:TPU:199 now
where the time goes in v1:
time: 101 us
  starting transfers between devices  52.4 us (52%)
  blocking collectives  25.6 us (25%)
  Pallas kernels  11.4 us (11%)
  local copies, waits for them, and re-layouts  4.64 us (5%)
  waiting for transfers between devices  4.2 us (4%)
  other arithmetic  2.2 us (2%)
    ppermute x12, starting transfers between devices, from_behind(): return lax.ppermute(block, axis, route)  41.3 us
    all_to_all x1, blocking collectives, on_device(): lax.all_to_all(returned, 'mem', split_axis=0, concat_axis=0, tiled=True)  25.6 us
    all_to_all x1, starting transfers between devices, on_device(): lax.all_to_all(message, 'mem', split_axis=0, concat_axis=0, tiled=True)  11.1 us
    pallas_call x1, Pallas kernels, analyse(): pl.pallas_call(analysis_kernel, out_shape=jax.ShapeDtypeStruct((MEMBERS *...  8.3 us
    ppermute x12, waiting for transfers between devices, from_behind(): return lax.ppermute(block, axis, route)  4.19 us
    unnamed x12, local copies, waits for them, and re-layouts  3.64 us
  transfers between devices with their start and end apart: 13, of which 4 were waited for; matrix products, arithmetic and copies ran while one was open for 4% of the time, Pallas kernels for 0%

profile of v1, /device:TPU:199, one launch (start us, length us, event | category | flops | bytes accessed | tf_op | source)
XLA Modules:
  0.0 100.7 jit_solution(16826126673486210494)
XLA Ops:
  0.0 1.0 %copy-done = bf16[1,2,256,512]{3,2,1,0:T(8,128)(2,1)S(1)} copy-done((bf16[1,2,256,512]{3,2,1,0:T(8,128)(2,1)S(1)}, bf16[1,2,256,512]{3,2,1,0:T(8,128)(2,1)}, u32[]{:S(2)}) %copy-start) | copy-done | bytes 524312
  1.0 1.5 %shard_map.55 = bf16[1024,256]{1,0:T(8,128)(2,1)} custom-call(bf16[512,512]{1,0:T(8,128)(2,1)S(1)} %bitcast.10), custom_call_target="tpu_custom_call" | custom-call | bytes 1048576 | tf_op jit(solution)/shard_map/pallas_call | solution.py:295
  2.5 11.1 %all-to-all-start = ((bf16[64,16,256]{2,1,0:T(8,128)(2,1)}), bf16[64,16,256]{2,1,0:T(8,128)(2,1)S(1)}, u32[]{:S(2)}, u32[]{:S(2)}) async-start(bf16[64,16,256]{2,1,0:T(8,128)(2,1)} %bitcast.1), calls=%async_computation | async-start | bytes 1048576 | tf_op jit(solution)/shard_map/all_to_all | solution.py:376
  13.6 0.0 copy-start.1
  13.7 0.5 broadcast.14
  14.2 0.1 copy-done.1
  14.3 0.7 reduce.9
  15.0 0.1 reshape.62.point_ref
  15.1 0.5 broadcast.15
  15.6 0.1 copy-done.2
  15.8 0.7 reduce.10
  16.4 0.1 reshape.63
  16.5 0.6 copy-done.3
  17.1 0.7 reduce.11
  17.7 0.1 reshape.64
  17.8 0.7 copy-done.4
  18.5 0.1 compare_convert_fusion
  18.5 0.1 reshape.66
  18.7 1.9 %collective-permute-start.7 = (f32[8,128]{1,0:T(8,128)S(1)}, f32[8,128]{1,0:T(8,128)S(1)}, u32[]{:S(2)}, u32[]{:S(2)}) collective-permute-start(f32[8,128]{1,0:T(8,128)S(1)} %concatenate.17), channel_id=1, source_target_pairs={{1,0},{2,1},{3,2},{4,3},{5,4},{6,5},{7,6},{9,8},{10,9},{11,10},{12... | collective-permute-start | bytes 12296 | tf_op jit(solution)/shard_map/ppermute | solution.py:349
  20.6 5.2 %collective-permute-start.6 = (f32[8,128]{1,0:T(8,128)S(1)}, f32[8,128]{1,0:T(8,128)S(1)}, u32[]{:S(2)}, u32[]{:S(2)}) collective-permute-start(f32[8,128]{1,0:T(8,128)S(1)} %concatenate.17), channel_id=1, source_target_pairs={{0,1},{1,2},{2,3},{3,4},{4,5},{5,6},{6,7},{8,9},{9,10},{10,11},{11... | collective-permute-start | bytes 12296 | tf_op jit(solution)/shard_map/ppermute | solution.py:349
  25.8 0.1 fusion.4
  25.9 0.1 fusion.3
  25.9 0.6 collective-permute-done.6
  26.5 0.1 fusion.5
  26.6 0.1 pad_maximum_fusion.1
  26.7 4.6 %collective-permute-start.11 = (f32[8,256]{1,0:T(8,128)S(1)}, f32[8,256]{1,0:T(8,128)S(1)}, u32[]{:S(2)}, u32[]{:S(2)}) collective-permute-start(f32[8,256]{1,0:T(8,128)S(1)} %pad_maximum_fusion.1), channel_id=1, source_target_pairs={{16,0},{24,8},{32,16},{40,24},{48,32},{56,40},{64,48},{72,56},{80,... | collective-permute-start | bytes 24584 | tf_op jit(solution)/shard_map/ppermute | solution.py:349
  31.3 1.9 %collective-permute-start.8 = (f32[8,256]{1,0:T(8,128)S(1)}, f32[8,256]{1,0:T(8,128)S(1)}, u32[]{:S(2)}, u32[]{:S(2)}) collective-permute-start(f32[8,256]{1,0:T(8,128)S(1)} %pad_maximum_fusion.1), channel_id=1, source_target_pairs={{0,16},{8,24},{16,32},{24,40},{32,48},{40,56},{48,64},{56,72},{64,... | collective-permute-start | bytes 24584 | tf_op jit(solution)/shard_map/ppermute | solution.py:349
  33.2 0.1 concatenate.19.meta_0
  33.3 3.4 %collective-permute-start.10 = (f32[8,512]{1,0:T(8,128)S(1)}, f32[8,512]{1,0:T(8,128)S(1)}, u32[]{:S(2)}, u32[]{:S(2)}) collective-permute-start(f32[8,512]{1,0:T(8,128)S(1)} %concatenate.19.meta_0), channel_id=1, source_target_pairs={{8,0},{16,8},{24,16},{32,24},{40,32},{48,40},{56,48},{64,56},{72,6... | collective-permute-start | bytes 49160 | tf_op jit(solution)/shard_map/ppermute | solution.py:349
  36.7 0.4 shard_map.56
  37.1 1.9 %collective-permute-start.1 = (bf16[64,128]{1,0:T(8,128)(2,1)S(1)}, bf16[64,128]{1,0:T(8,128)(2,1)S(1)}, u32[]{:S(2)}, u32[]{:S(2)}) collective-permute-start(bf16[64,128]{1,0:T(8,128)(2,1)S(1)} %shard_map.56), channel_id=1, source_target_pairs={{1,0},{2,1},{3,2},{4,3},{5,4},{6,5},{7,6},{9,8},{10,9},{11,10},{12... | collective-permute-start | bytes 49160 | tf_op jit(solution)/shard_map/ppermute | solution.py:349
  39.0 5.1 %collective-permute-start = (bf16[64,128]{1,0:T(8,128)(2,1)S(1)}, bf16[64,128]{1,0:T(8,128)(2,1)S(1)}, u32[]{:S(2)}, u32[]{:S(2)}) collective-permute-start(bf16[64,128]{1,0:T(8,128)(2,1)S(1)} %shard_map.56), channel_id=1, source_target_pairs={{0,1},{1,2},{2,3},{3,4},{4,5},{5,6},{6,7},{8,9},{9,10},{10,11},{11... | collective-permute-start | bytes 49160 | tf_op jit(solution)/shard_map/ppermute | solution.py:349
  44.1 0.1 fusion.1
  44.2 0.1 fusion
  44.3 0.7 collective-permute-done
  45.0 0.1 fusion.2
  45.1 0.1 concatenate.16.cat_0
  45.2 5.2 %collective-permute-start.4 = (bf16[64,512]{1,0:T(8,128)(2,1)S(1)}, bf16[64,512]{1,0:T(8,128)(2,1)S(1)}, u32[]{:S(2)}, u32[]{:S(2)}) collective-permute-start(bf16[64,512]{1,0:T(8,128)(2,1)S(1)} %concatenate.16.cat_0), channel_id=1, source_target_pairs={{8,0},{16,8},{24,16},{32,24},{40,32},{48,40},{56,48},{64,56},{72,6... | collective-permute-start | bytes 196616 | tf_op jit(solution)/shard_map/ppermute | solution.py:349
  50.4 1.9 %collective-permute-start.3 = (bf16[64,512]{1,0:T(8,128)(2,1)S(1)}, bf16[64,512]{1,0:T(8,128)(2,1)S(1)}, u32[]{:S(2)}, u32[]{:S(2)}) collective-permute-start(bf16[64,512]{1,0:T(8,128)(2,1)S(1)} %concatenate.16.cat_0), channel_id=1, source_target_pairs={{0,8},{8,16},{16,24},{24,32},{32,40},{40,48},{48,56},{56,64},{64,7... | collective-permute-start | bytes 196616 | tf_op jit(solution)/shard_map/ppermute | solution.py:349
  52.3 0.1 pad_maximum_fusion
  52.4 6.3 %collective-permute-start.5 = (bf16[64,256]{1,0:T(8,128)(2,1)S(1)}, bf16[64,256]{1,0:T(8,128)(2,1)S(1)}, u32[]{:S(2)}, u32[]{:S(2)}) collective-permute-start(bf16[64,256]{1,0:T(8,128)(2,1)S(1)} %pad_maximum_fusion), channel_id=1, source_target_pairs={{16,0},{24,8},{32,16},{40,24},{48,32},{56,40},{64,48},{72,56},{80,... | collective-permute-start | bytes 98312 | tf_op jit(solution)/shard_map/ppermute | solution.py:349
  58.7 1.9 %collective-permute-start.2 = (bf16[64,256]{1,0:T(8,128)(2,1)S(1)}, bf16[64,256]{1,0:T(8,128)(2,1)S(1)}, u32[]{:S(2)}, u32[]{:S(2)}) collective-permute-start(bf16[64,256]{1,0:T(8,128)(2,1)S(1)} %pad_maximum_fusion), channel_id=1, source_target_pairs={{0,16},{8,24},{16,32},{24,40},{32,48},{40,56},{48,64},{56,72},{64,... | collective-permute-start | bytes 98312 | tf_op jit(solution)/shard_map/ppermute | solution.py:349
  60.7 1.9 %collective-permute-start.9 = (f32[8,512]{1,0:T(8,128)S(1)}, f32[8,512]{1,0:T(8,128)S(1)}, u32[]{:S(2)}, u32[]{:S(2)}) collective-permute-start(f32[8,512]{1,0:T(8,128)S(1)} %concatenate.19.meta_0), channel_id=1, source_target_pairs={{0,8},{8,16},{16,24},{24,32},{32,40},{40,48},{48,56},{56,64},{64,7... | collective-permute-start | bytes 49160 | tf_op jit(solution)/shard_map/ppermute | solution.py:349
  62.6 1.1 %collective-permute-done.9.meta_n1 = f32[8,512]{1,0:T(8,128)S(1)} collective-permute-done((f32[8,512]{1,0:T(8,128)S(1)}, f32[8,512]{1,0:T(8,128)S(1)}, u32[]{:S(2)}, u32[]{:S(2)}) %collective-permute-start.9) | collective-permute-done | bytes 16416 | tf_op jit(solution)/shard_map/ppermute | solution.py:349
  63.8 1.7 %collective-permute-done.2.cat_n2 = bf16[64,256]{1,0:T(8,128)(2,1)S(1)} collective-permute-done((bf16[64,256]{1,0:T(8,128)(2,1)S(1)}, bf16[64,256]{1,0:T(8,128)(2,1)S(1)}, u32[]{:S(2)}, u32[]{:S(2)}) %collective-permute-start.2) | collective-permute-done | bytes 32800 | tf_op jit(solution)/shard_map/ppermute | solution.py:349
  65.5 8.3 %shard_map.57 = bf16[1024,256]{1,0:T(8,128)(2,1)S(1)} custom-call(bf16[1024,256]{1,0:T(8,128)(2,1)S(1)} %bitcast.8, bf16[64,256]{1,0:T(8,128)(2,1)S(1)} %collective-permute-done.2.cat_n2, bf16[64,512]{1,0:T(8,128)(2,1)S(1)} %collective-permute-done.3.cat_n1, bf16[64,512]{1,0:T(8,128)(2,1)S(1)} %concatenate.16.cat_0, ...), custom_call_target="tpu_custom_call" | custom-call | flops 1073741824 | bytes 1048576 | tf_op jit(solution)/shard_map/pallas_call | solution.py:331
  73.8 25.6 %all_to_all.22 = bf16[64,16,256]{2,1,0:T(8,128)(2,1)S(1)} all-to-all(bf16[64,16,256]{2,1,0:T(8,128)(2,1)S(1)} %bitcast.11), channel_id=1, replica_groups=mesh['mem'=64,'tile'=8] {'mem'}, dimensions={0} | all-to-all | bytes 1048576 | tf_op jit(solution)/shard_map/all_to_all | solution.py:394
  99.4 1.3 %shard_map.58 = bf16[512,512]{1,0:T(8,128)(2,1)} custom-call(bf16[1024,256]{1,0:T(8,128)(2,1)S(1)} %bitcast.9), custom_call_target="tpu_custom_call" | custom-call | bytes 1048576 | tf_op jit(solution)/shard_map/pallas_call | solution.py:308
  (18 shorter events, 0.1 us)
Async XLA Ops:
  0.0 1.0 %copy-start = (bf16[1,2,256,512]{3,2,1,0:T(8,128)(2,1)S(1)}, bf16[1,2,256,512]{3,2,1,0:T(8,128)(2,1)}, u32[]{:S(2)}) copy-start(bf16[1,2,256,512]{3,2,1,0:T(8,128)(2,1)} %param.5) | copy-start | bytes 1572868
  2.5 34.2 %all-to-all-start = ((bf16[64,16,256]{2,1,0:T(8,128)(2,1)}), bf16[64,16,256]{2,1,0:T(8,128)(2,1)S(1)}, u32[]{:S(2)}, u32[]{:S(2)}) async-start(bf16[64,16,256]{2,1,0:T(8,128)(2,1)} %bitcast.1), calls=%async_computation | async-start | bytes 1048576 | tf_op jit(solution)/shard_map/all_to_all | solution.py:376
  13.6 0.7 copy-start.1
  15.1 0.7 copy-start.2
  16.4 0.7 copy-start.3
  17.8 0.7 copy-start.4
  18.7 7.2 %collective-permute-start.7 = (f32[8,128]{1,0:T(8,128)S(1)}, f32[8,128]{1,0:T(8,128)S(1)}, u32[]{:S(2)}, u32[]{:S(2)}) collective-permute-start(f32[8,128]{1,0:T(8,128)S(1)} %concatenate.17), channel_id=1, source_target_pairs={{1,0},{2,1},{3,2},{4,3},{5,4},{6,5},{7,6},{9,8},{10,9},{11,10},{12... | collective-permute-start | bytes 12296 | tf_op jit(solution)/shard_map/ppermute | solution.py:349
  20.6 6.0 %collective-permute-start.6 = (f32[8,128]{1,0:T(8,128)S(1)}, f32[8,128]{1,0:T(8,128)S(1)}, u32[]{:S(2)}, u32[]{:S(2)}) collective-permute-start(f32[8,128]{1,0:T(8,128)S(1)} %concatenate.17), channel_id=1, source_target_pairs={{0,1},{1,2},{2,3},{3,4},{4,5},{5,6},{6,7},{8,9},{9,10},{10,11},{11... | collective-permute-start | bytes 12296 | tf_op jit(solution)/shard_map/ppermute | solution.py:349
  26.7 25.7 %collective-permute-start.11 = (f32[8,256]{1,0:T(8,128)S(1)}, f32[8,256]{1,0:T(8,128)S(1)}, u32[]{:S(2)}, u32[]{:S(2)}) collective-permute-start(f32[8,256]{1,0:T(8,128)S(1)} %pad_maximum_fusion.1), channel_id=1, source_target_pairs={{16,0},{24,8},{32,16},{40,24},{48,32},{56,40},{64,48},{72,56},{80,... | collective-permute-start | bytes 24584 | tf_op jit(solution)/shard_map/ppermute | solution.py:349
  31.3 27.5 %collective-permute-start.8 = (f32[8,256]{1,0:T(8,128)S(1)}, f32[8,256]{1,0:T(8,128)S(1)}, u32[]{:S(2)}, u32[]{:S(2)}) collective-permute-start(f32[8,256]{1,0:T(8,128)S(1)} %pad_maximum_fusion.1), channel_id=1, source_target_pairs={{0,16},{8,24},{16,32},{24,40},{32,48},{40,56},{48,64},{56,72},{64,... | collective-permute-start | bytes 24584 | tf_op jit(solution)/shard_map/ppermute | solution.py:349
  33.3 27.4 %collective-permute-start.10 = (f32[8,512]{1,0:T(8,128)S(1)}, f32[8,512]{1,0:T(8,128)S(1)}, u32[]{:S(2)}, u32[]{:S(2)}) collective-permute-start(f32[8,512]{1,0:T(8,128)S(1)} %concatenate.19.meta_0), channel_id=1, source_target_pairs={{8,0},{16,8},{24,16},{32,24},{40,32},{48,40},{56,48},{64,56},{72,6... | collective-permute-start | bytes 49160 | tf_op jit(solution)/shard_map/ppermute | solution.py:349
  37.1 7.1 %collective-permute-start.1 = (bf16[64,128]{1,0:T(8,128)(2,1)S(1)}, bf16[64,128]{1,0:T(8,128)(2,1)S(1)}, u32[]{:S(2)}, u32[]{:S(2)}) collective-permute-start(bf16[64,128]{1,0:T(8,128)(2,1)S(1)} %shard_map.56), channel_id=1, source_target_pairs={{1,0},{2,1},{3,2},{4,3},{5,4},{6,5},{7,6},{9,8},{10,9},{11,10},{12... | collective-permute-start | bytes 49160 | tf_op jit(solution)/shard_map/ppermute | solution.py:349
  39.0 6.0 %collective-permute-start = (bf16[64,128]{1,0:T(8,128)(2,1)S(1)}, bf16[64,128]{1,0:T(8,128)(2,1)S(1)}, u32[]{:S(2)}, u32[]{:S(2)}) collective-permute-start(bf16[64,128]{1,0:T(8,128)(2,1)S(1)} %shard_map.56), channel_id=1, source_target_pairs={{0,1},{1,2},{2,3},{3,4},{4,5},{5,6},{6,7},{8,9},{9,10},{10,11},{11... | collective-permute-start | bytes 49160 | tf_op jit(solution)/shard_map/ppermute | solution.py:349
  45.2 20.3 %collective-permute-start.4 = (bf16[64,512]{1,0:T(8,128)(2,1)S(1)}, bf16[64,512]{1,0:T(8,128)(2,1)S(1)}, u32[]{:S(2)}, u32[]{:S(2)}) collective-permute-start(bf16[64,512]{1,0:T(8,128)(2,1)S(1)} %concatenate.16.cat_0), channel_id=1, source_target_pairs={{8,0},{16,8},{24,16},{32,24},{40,32},{48,40},{56,48},{64,56},{72,6... | collective-permute-start | bytes 196616 | tf_op jit(solution)/shard_map/ppermute | solution.py:349
  50.4 15.1 %collective-permute-start.3 = (bf16[64,512]{1,0:T(8,128)(2,1)S(1)}, bf16[64,512]{1,0:T(8,128)(2,1)S(1)}, u32[]{:S(2)}, u32[]{:S(2)}) collective-permute-start(bf16[64,512]{1,0:T(8,128)(2,1)S(1)} %concatenate.16.cat_0), channel_id=1, source_target_pairs={{0,8},{8,16},{16,24},{24,32},{32,40},{40,48},{48,56},{56,64},{64,7... | collective-permute-start | bytes 196616 | tf_op jit(solution)/shard_map/ppermute | solution.py:349
  52.4 11.3 %collective-permute-start.5 = (bf16[64,256]{1,0:T(8,128)(2,1)S(1)}, bf16[64,256]{1,0:T(8,128)(2,1)S(1)}, u32[]{:S(2)}, u32[]{:S(2)}) collective-permute-start(bf16[64,256]{1,0:T(8,128)(2,1)S(1)} %pad_maximum_fusion), channel_id=1, source_target_pairs={{16,0},{24,8},{32,16},{40,24},{48,32},{56,40},{64,48},{72,56},{80,... | collective-permute-start | bytes 98312 | tf_op jit(solution)/shard_map/ppermute | solution.py:349
  58.7 6.8 %collective-permute-start.2 = (bf16[64,256]{1,0:T(8,128)(2,1)S(1)}, bf16[64,256]{1,0:T(8,128)(2,1)S(1)}, u32[]{:S(2)}, u32[]{:S(2)}) collective-permute-start(bf16[64,256]{1,0:T(8,128)(2,1)S(1)} %pad_maximum_fusion), channel_id=1, source_target_pairs={{0,16},{8,24},{16,32},{24,40},{32,48},{40,56},{48,64},{56,72},{64,... | collective-permute-start | bytes 98312 | tf_op jit(solution)/shard_map/ppermute | solution.py:349
  60.7 3.1 %collective-permute-start.9 = (f32[8,512]{1,0:T(8,128)S(1)}, f32[8,512]{1,0:T(8,128)S(1)}, u32[]{:S(2)}, u32[]{:S(2)}) collective-permute-start(f32[8,512]{1,0:T(8,128)S(1)} %concatenate.19.meta_0), channel_id=1, source_target_pairs={{0,8},{8,16},{16,24},{24,32},{32,40},{40,48},{48,56},{56,64},{64,7... | collective-permute-start | bytes 49160 | tf_op jit(solution)/shard_map/ppermute | solution.py:349

commit v2 on v1

v2 whole, which is shorter than its diff:
```python
import jax
import jax.numpy as jnp
from jax import lax
from jax.experimental import pallas as pl
from jax.experimental.pallas import tpu as pltpu
from jax.sharding import PartitionSpec as P

MEMBERS = 64
LEVELS = 2
SPAN_NORTH = 4
SPAN_EAST = 512
SLOTS = 64
CHIPS = 32
ROWS = 2 * SPAN_NORTH
LINES = LEVELS * ROWS
HALF = SPAN_EAST // 2
STRIP = 128
STRIPS = HALF // STRIP
REACH = 8
CHUNK = 64
SITE_CHUNK = 128
FACTS = 16
PACKET = MEMBERS + FACTS
BATCH_LANES = 4 * SLOTS
F32 = jnp.float32
BF16 = jnp.bfloat16
VMEM_LIMIT = 48 * 1024 * 1024


def split(values):
    high = values.astype(BF16)
    return high, (values - high.astype(F32)).astype(BF16)


def pack_kernel(field_ref, message_ref):
    for group in range(CHIPS // 2):
        upper, lower = (
            field_ref[level, pl.ds(2 * ROWS * group, 2 * ROWS), :].astype(F32) for level in range(LEVELS)
        )
        for chip in range(2):
            rows = slice(chip * ROWS, (chip + 1) * ROWS)
            for half in range(2):
                lanes = slice(half * HALF, (half + 1) * HALF)
                place = (2 * (2 * group + chip) + half) * LINES
                message_ref[pl.ds(place, LINES), :] = jnp.concatenate(
                    [upper[rows, lanes], lower[rows, lanes]], axis=0
                ).astype(BF16)


def unpack_kernel(message_ref, field_ref):
    for group in range(CHIPS // 2):
        for half in range(2):
            lanes = pl.ds(half * HALF, HALF)
            first, second = (
                message_ref[pl.ds((2 * (2 * group + chip) + half) * LINES, LINES), :].astype(F32)
                for chip in range(2)
            )
            for level in range(LEVELS):
                rows = slice(level * ROWS, (level + 1) * ROWS)
                field_ref[level, pl.ds(2 * ROWS * group, 2 * ROWS), lanes] = jnp.concatenate(
                    [first[rows], second[rows]], axis=0
                ).astype(BF16)


def parts_of(values):
    high = values.astype(BF16).astype(F32)
    rest = values - high
    middle = rest.astype(BF16).astype(F32)
    return [high, middle, rest - middle]


def stack_rows(lines, count):
    shape = (count, lines[0].shape[1])
    rows = lax.broadcasted_iota(jnp.int32, shape, 0)
    block = jnp.zeros(shape, F32)
    for index, line in enumerate(lines):
        block = jnp.where(rows == index, line, block)
    return block


def facts_kernel(place_ref, datum_ref, noise_ref, point_ref, count_ref, facts_ref):
    lane = lax.broadcasted_iota(jnp.int32, (1, 2 * SLOTS), 1)

    def both(ref):
        first = jnp.concatenate([ref[0, 0], ref[0, 0]], axis=1)
        second = jnp.concatenate([ref[1, 0], ref[1, 0]], axis=1)
        return jnp.where(lane < SLOTS, first, second)

    point = both(point_ref)
    count = jnp.where(lane < SLOTS, count_ref[0], count_ref[1])
    col = place_ref[1] + (point & (SPAN_EAST - 1))
    row = place_ref[0] + ((point >> 9) & (SPAN_NORTH - 1))
    live = jnp.where((lane & (SLOTS - 1)) < count, 1.0, 0.0)
    lines = parts_of(both(datum_ref)) + parts_of(both(noise_ref))
    lines += [(col >> 7).astype(F32), (col & 127).astype(F32), row.astype(F32), (point >> 11).astype(F32), live]
    facts_ref[...] = stack_rows(lines, FACTS).astype(BF16)


def pick_kernel(place_ref, field_ref, own_ref, other_ref, packet_ref, scratch):
    own = own_ref[...].astype(F32)
    other = other_ref[...].astype(F32)
    half = place_ref[2]
    first = jnp.where(half == 0, own, other)
    second = jnp.where(half == 0, other, own)
    lane = lax.broadcasted_iota(jnp.int32, first.shape, 1)
    batches = (
        jnp.where(lane < SLOTS, first, pltpu.roll(second, SLOTS, 1)),
        jnp.where(lane < SLOTS, pltpu.roll(first, SLOTS, 1), second),
    )
    place = lax.broadcasted_iota(jnp.int32, (HALF, 2 * SLOTS), 0)
    for batch in range(2):
        facts = batches[batch]
        col = (facts[6:7] * 128.0 + facts[7:8]).astype(jnp.int32) - place_ref[4]
        line = (facts[9:10] * ROWS + facts[8:9]).astype(jnp.int32) - place_ref[3]
        chooser = jnp.where(place == col, 1.0, 0.0).astype(BF16)
        scratch[...] = jnp.dot(field_ref[...], chooser, preferred_element_type=F32)
        total = jnp.zeros((MEMBERS, 2 * SLOTS), F32)
        for index in range(LINES):
            block = scratch[pl.ds(index, MEMBERS, stride=LINES), :]
            total = total + jnp.where(line == index, block, 0.0)
        lanes = pl.ds(batch * 2 * SLOTS, 2 * SLOTS)
        packet_ref[pl.ds(0, MEMBERS), lanes] = total.astype(BF16)
        packet_ref[pl.ds(MEMBERS, FACTS), lanes] = facts.astype(BF16)


def merge_kernel(own_ref, other_ref, beyond_ref, cat_ref):
    for batch in range(2):
        lanes = pl.ds(batch * 2 * SLOTS, 2 * SLOTS)
        here = pl.ds(batch * BATCH_LANES, 2 * SLOTS)
        members = pl.ds(0, MEMBERS)
        facts = pl.ds(MEMBERS, FACTS)
        cat_ref[members, here] = own_ref[members, lanes] + other_ref[members, lanes]
        cat_ref[facts, here] = own_ref[facts, lanes]
        cat_ref[:, pl.ds(batch * BATCH_LANES + 2 * SLOTS, 2 * SLOTS)] = beyond_ref[:, lanes]


def weights_of(columns, datum, noise, live):
    mean = jnp.sum(columns, axis=0, keepdims=True) * (1.0 / MEMBERS)
    pert = columns - mean
    variance = jnp.sum(pert * pert, axis=0, keepdims=True) / (MEMBERS - 1)
    denominator = jnp.where(live > 0.0, variance + noise, 1.0)
    factor = 1.0 / (1.0 + jnp.sqrt(noise / denominator))
    return pert, live * (datum - mean) / denominator, live * factor / denominator


def positions(masks):
    rows, lanes = masks.shape
    before = lax.broadcasted_iota(jnp.int32, (128, 128), 0)
    after = lax.broadcasted_iota(jnp.int32, (128, 128), 1)
    triangle = jnp.where(before < after, 1.0, 0.0).astype(BF16)
    total = jnp.zeros((rows, 1), F32)
    parts = []
    for start in range(0, lanes, 128):
        block = masks[:, start : start + 128]
        rank = jnp.dot(block.astype(BF16), triangle, preferred_element_type=F32) + total
        parts.append(jnp.where(block > 0.0, rank, -1.0))
        total = total + jnp.sum(block, axis=1, keepdims=True)
    return jnp.concatenate(parts, axis=1), total


def taper(square):
    inverse = lax.rsqrt(jnp.maximum(square, 1.0))
    s = square * inverse * 0.25
    inside = (((-0.25 * s + 0.5) * s + 0.625) * s - 5.0 / 3.0) * s * s + 1.0
    outside = (
        ((((s * (1.0 / 12.0) - 0.5) * s + 0.625) * s + 5.0 / 3.0) * s - 5.0) * s
        + 4.0
        - (8.0 / 3.0) * inverse
    )
    return jnp.where(square <= 16.0, inside, jnp.where(square < 64.0, outside, 0.0))


def table_of(pert, mean_weight, pert_weight, row, col, level):
    high, low = split(pert)
    tail = [row.astype(F32), (col & ~127).astype(F32), (col & 127).astype(F32), level]
    for weight in (mean_weight, pert_weight):
        weight_high, weight_low = split(weight)
        tail += [weight_high.astype(F32), weight_low.astype(F32)]
    return jnp.concatenate([high, low, stack_rows(tail, 16).astype(BF16)], axis=0)


def chosen_records(ranks, base, count, table):
    place = lax.broadcasted_iota(jnp.int32, (count, 1), 0).astype(F32) + base
    chooser = jnp.where(ranks == place, 1.0, 0.0).astype(BF16)
    return lax.dot_general(chooser, table, (((1,), (1,)), ((), ())), preferred_element_type=F32)


def open_records(records):
    pert = records[:, : 2 * MEMBERS].astype(BF16)
    tail = records[:, 2 * MEMBERS :]
    row = tail[:, 0:1]
    col = tail[:, 1:2] + tail[:, 2:3]
    level = tail[:, 3:4]
    mean_weight = tail[:, 4:5] + tail[:, 5:6]
    pert_weight = tail[:, 6:7] + tail[:, 7:8]
    step = mean_weight - pert_weight * (records[:, :MEMBERS] + records[:, MEMBERS : 2 * MEMBERS])
    high, low = split(step)
    return pert, row, col, level, jnp.concatenate([high, low, high], axis=0)


def advance(step, gain):
    high, low = split(gain)
    return lax.dot_general(
        step,
        jnp.concatenate([high, high, low], axis=0),
        (((0,), (0,)), ((), ())),
        preferred_element_type=F32,
    )


def level_factor(level, target):
    return (1.0 / (MEMBERS - 1)) / (1.0 + jnp.abs(level - target))


def update_region(ranks, total, table, source, state, wide_state):
    chunks = (jnp.max(total).astype(jnp.int32) + (CHUNK - 1)) // CHUNK

    def one(index, carry):
        base = (index * CHUNK).astype(F32)
        for strip in range(STRIPS):
            records = chosen_records(ranks[strip : strip + 1], base, CHUNK, table)
            pert, row, col, level, step = open_records(records)
            lane = lax.broadcasted_iota(jnp.int32, (1, STRIP), 1).astype(F32) + strip * STRIP
            across = col - lane
            across = across * across
            tile = jnp.floor(row * (1.0 / SPAN_NORTH))
            beside = [
                jnp.where(jnp.abs(tile - target) <= 1.0, 1.0, 0.0) for target in range(ROWS // SPAN_NORTH)
            ]
            tapers = []
            for line in range(ROWS):
                down = row - float(line)
                tapers.append(taper(across + down * down) * beside[line // SPAN_NORTH])
            if wide_state:
                pert = jnp.concatenate([pert, pert[:, :MEMBERS]], axis=1)
            for target in range(LEVELS):
                lanes = pl.ds(target * ROWS * STRIP, ROWS * STRIP)
                factor = level_factor(level, float(target))
                weight = jnp.concatenate([t * factor for t in tapers], axis=1)
                covariance = jnp.dot(pert, source[strip, :, lanes], preferred_element_type=F32)
                state[strip, :, lanes] = state[strip, :, lanes] + advance(step, weight * covariance)
        return carry

    lax.fori_loop(0, chunks, one, 0)


def facts_of(cats, batch, place_ref):
    lanes = pl.ds(batch * BATCH_LANES, BATCH_LANES)
    facts = jnp.concatenate([c[pl.ds(MEMBERS, FACTS), lanes] for c in cats], axis=1).astype(F32)
    datum = facts[0:1] + facts[1:2] + facts[2:3]
    noise = facts[3:4] + facts[4:5] + facts[5:6]
    col = (facts[6:7] * 128.0 + facts[7:8]).astype(jnp.int32) - place_ref[4]
    row = facts[8:9].astype(jnp.int32) - place_ref[3]
    return datum, noise, col, row, facts[9:10], facts[10:11]


def masks_of(col, row, live):
    masks = []
    for strip in range(STRIPS):
        west = strip * STRIP - REACH
        inside = (col > west) & (col < west + STRIP + 2 * REACH - 1)
        inside = inside & (row >= -SPAN_NORTH) & (row < ROWS + SPAN_NORTH)
        masks.append(jnp.where(inside, live, 0.0))
    inside = (col > -2 * REACH) & (col < HALF + 2 * REACH - 1)
    masks.append(jnp.where(inside, live, 0.0))
    return stack_rows(masks, 8)


def analysis_kernel(
    place_ref, field_ref, north_ref, here_ref, south_ref, message_ref, wide, state, narrow, source, site_state
):
    cats = (north_ref, here_ref, south_ref)
    for part in range(STRIPS):
        wide[part] = field_ref[:, part * STRIP : (part + 1) * STRIP].astype(F32)
    for strip in range(STRIPS):
        for line in range(LINES):
            piece = wide[strip, pl.ds(line, MEMBERS, stride=LINES), :]
            lanes = pl.ds(line * STRIP, STRIP)
            state[strip, :, lanes] = piece
            low = piece.astype(BF16)
            narrow[strip, :MEMBERS, lanes] = low
            narrow[strip, MEMBERS:, lanes] = low

    first, sites = (
        jnp.concatenate([c[pl.ds(0, MEMBERS), pl.ds(b * BATCH_LANES, BATCH_LANES)] for c in cats], axis=1)
        for b in range(2)
    )
    datum, noise, col, row, level, live = facts_of(cats, 0, place_ref)
    pert, mean_weight, pert_weight = weights_of(first.astype(F32), datum, noise, live)
    table = table_of(pert, mean_weight, pert_weight, row, col, level)
    ranks, total = positions(masks_of(col, row, live))
    update_region(ranks, total[:STRIPS], table, narrow, state, False)

    site_state[...] = sites.astype(F32)
    datum_1, noise_1, col_1, row_1, level_1, live_1 = facts_of(cats, 1, place_ref)
    site_row = row_1.astype(F32)
    site_col = col_1.astype(F32)
    site_tile = (row_1 >> 2).astype(F32)
    doubled = jnp.concatenate([sites, sites], axis=0)

    def one(index, carry):
        base = (index * SITE_CHUNK).astype(F32)
        records = chosen_records(ranks[STRIPS : STRIPS + 1], base, SITE_CHUNK, table)
        obs, obs_row, obs_col, obs_level, step = open_records(records)
        down = obs_row - site_row
        across = obs_col - site_col
        weight = taper(down * down + across * across) * level_factor(obs_level, level_1)
        obs_tile = jnp.floor(obs_row * (1.0 / SPAN_NORTH))
        weight = jnp.where(jnp.abs(obs_tile - site_tile) <= 1.0, weight, 0.0)
        covariance = jnp.dot(obs, doubled, preferred_element_type=F32)
        site_state[...] = site_state[...] + advance(step, weight * covariance)
        return carry

    chunks = (jnp.max(total[STRIPS : STRIPS + 1]).astype(jnp.int32) + (SITE_CHUNK - 1)) // SITE_CHUNK
    lax.fori_loop(0, chunks, one, 0)

    pert, mean_weight, pert_weight = weights_of(site_state[...], datum_1, noise_1, live_1)
    table_1 = table_of(pert, mean_weight, pert_weight, row_1, col_1, level_1)
    ranks_1, total_1 = positions(masks_of(col_1, row_1, live_1))
    for strip in range(STRIPS):
        high, low = split(state[strip])
        source[strip, :MEMBERS, :] = high
        source[strip, MEMBERS : 2 * MEMBERS, :] = high
        source[strip, 2 * MEMBERS :, :] = low
    update_region(ranks_1, total_1[:STRIPS], table_1, source, state, True)

    for strip in range(STRIPS):
        for line in range(LINES):
            wide[strip, pl.ds(line, MEMBERS, stride=LINES), :] = state[strip, :, pl.ds(line * STRIP, STRIP)]
    for part in range(STRIPS):
        message_ref[:, part * STRIP : (part + 1) * STRIP] = wide[part].astype(BF16)


def call(kernel, shape, operands, scratch=(), scalars=0, flops=0, moved=1 << 18):
    smem = pl.BlockSpec(memory_space=pltpu.SMEM)
    vmem = pl.BlockSpec(memory_space=pltpu.VMEM)
    return pl.pallas_call(
        kernel,
        out_shape=jax.ShapeDtypeStruct(shape, BF16),
        in_specs=[smem if index < scalars else vmem for index in range(len(operands))],
        out_specs=vmem,
        scratch_shapes=list(scratch),
        compiler_params=pltpu.CompilerParams(vmem_limit_bytes=VMEM_LIMIT),
        cost_estimate=pl.CostEstimate(flops=flops, bytes_accessed=moved, transcendentals=0),
    )(*operands)


MESSAGE = (MEMBERS * LINES, HALF)


def pack(field):
    return call(pack_kernel, MESSAGE, (field,), moved=1 << 20)


def unpack(message):
    return call(unpack_kernel, (LEVELS, CHIPS * ROWS, SPAN_EAST), (message,), moved=1 << 20)


def state_facts(place, datum, noise, point, count):
    smem = pl.BlockSpec(memory_space=pltpu.SMEM)
    vmem = pl.BlockSpec(memory_space=pltpu.VMEM)
    return pl.pallas_call(
        facts_kernel,
        out_shape=jax.ShapeDtypeStruct((FACTS, 2 * SLOTS), BF16),
        in_specs=[smem, vmem, vmem, vmem, smem],
        out_specs=vmem,
        compiler_params=pltpu.CompilerParams(vmem_limit_bytes=VMEM_LIMIT),
    )(place, datum, noise, point, count)


def pick(place, field, own, other):
    scratch = [pltpu.VMEM((MEMBERS * LINES, 2 * SLOTS), F32)]
    return call(
        pick_kernel, (PACKET, 4 * SLOTS), (place, field, own, other), scratch, 1, 1 << 27, 1 << 19
    )


def merge(own, other, beyond):
    return call(merge_kernel, (PACKET, 2 * BATCH_LANES), (own, other, beyond))


def analyse(place, field, north, here, south):
    scratch = [
        pltpu.VMEM((STRIPS, MEMBERS * LINES, STRIP), F32),
        pltpu.VMEM((STRIPS, MEMBERS, LINES * STRIP), F32),
        pltpu.VMEM((STRIPS, 2 * MEMBERS, LINES * STRIP), BF16),
        pltpu.VMEM((STRIPS, 3 * MEMBERS, LINES * STRIP), BF16),
        pltpu.VMEM((MEMBERS, 3 * BATCH_LANES), F32),
    ]
    return call(
        analysis_kernel, MESSAGE, (place, field, north, here, south), scratch, 1, 1 << 30, 1 << 20
    )


def swap_cores(block):
    return lax.ppermute(block, "mem", [(i, i ^ 1) for i in range(lax.axis_size("mem"))])


def swap_beyond(block):
    rows, columns = lax.axis_size("mem"), lax.axis_size("tile")
    route = []
    for row in range(0, rows, 2):
        for column in range(columns - 1):
            west, east = (row + 1) * columns + column, row * columns + column + 1
            route += [(west, east), (east, west)]
    return lax.ppermute(block, ("mem", "tile"), route)


def from_behind(block, distance):
    size = lax.axis_size("mem")
    route = [(i - distance, i) for i in range(size) if 0 <= i - distance < size]
    return lax.ppermute(block, "mem", route)


def on_device(members, datum, noise, point, count):
    row = lax.axis_index("mem")
    column = lax.axis_index("tile")
    half = row % 2
    place = jnp.stack(
        [row * SPAN_NORTH, column * SPAN_EAST, half, (row // 2) * ROWS, column * SPAN_EAST + half * HALF]
    ).astype(jnp.int32)
    message = pack(members[0])
    field = lax.all_to_all(message, "mem", split_axis=0, concat_axis=0, tiled=True)
    facts = state_facts(place, datum, noise, point, count.reshape(2))
    packet = pick(place, field, facts, swap_cores(facts))
    here = merge(packet, swap_cores(packet), swap_beyond(packet))
    north, south = from_behind(here, 2), from_behind(here, -2)
    message = analyse(place, field, north, here, south)
    message = lax.all_to_all(message, "mem", split_axis=0, concat_axis=0, tiled=True)
    return unpack(message)[None]


def solution(mesh):
    return jax.shard_map(
        on_device,
        mesh=mesh,
        in_specs=(
            P("mem", None, None, "tile"),
            P(None, "mem", "tile", None),
            P(None, "mem", "tile", None),
            P(None, "mem", "tile", None),
            P(None, "mem", "tile"),
        ),
        out_specs=P("mem", None, None, "tile"),
        check_vma=False,
    )
```

time: 101 us -> 84.4 us (0.84)
  starting transfers between devices: 52.4 us -> 25.6 us
  waiting for transfers between devices: 4.2 us -> 19.5 us
  local copies, waits for them, and re-layouts: 4.64 us -> 1.81 us
  other arithmetic: 2.2 us -> 0 us
    ppermute x12 -> x5, starting transfers between devices: 41.3 us -> 14.5 us  [the longest x2 5.28 us: from_behind(): return lax.ppermute(block, 'mem', route)]
    all_to_all x1, waiting for transfers between devices: 0.01 us -> 12.6 us  [on_device(): lax.all_to_all(message, 'mem', split_axis=0, concat_axis=0, tiled=True)]
    ppermute x12 -> x5, waiting for transfers between devices: 4.19 us -> 6.85 us  [the longest x2 4.87 us: from_behind(): return lax.ppermute(block, 'mem', route)]
    unnamed x3 -> x0, other arithmetic: 1.96 us -> none
    unnamed x12 -> x10, local copies, waits for them, and re-layouts: 3.64 us -> 1.73 us
    pallas_call x4 -> x6, Pallas kernels: 11.4 us -> 11.4 us  [the longest x5 10.8 us: call(): pl.pallas_call(kernel, out_shape=jax.ShapeDtypeStruct(shape, BF16), in_sp...]
  transfers between devices with their start and end apart: 13 -> 6, of which waited for: 4 -> 5; matrix products, arithmetic and copies ran while one was open for 4% -> 0% of each run, Pallas kernels for 0% -> 1%
where the time goes in v2:
time: 84.4 us; the launch traced here: 84 us
  starting transfers between devices  25.6 us (30%)
  blocking collectives  25.6 us (30%)
  waiting for transfers between devices  19.5 us (23%)
  Pallas kernels  11.4 us (14%)
  local copies, waits for them, and re-layouts  1.81 us (2%)
    all_to_all x1, blocking collectives, on_device(): lax.all_to_all(message, 'mem', split_axis=0, concat_axis=0, tiled=True)  25.6 us
    all_to_all x1, waiting for transfers between devices, on_device(): lax.all_to_all(message, 'mem', split_axis=0, concat_axis=0, tiled=True)  12.6 us
    all_to_all x1, starting transfers between devices, on_device(): lax.all_to_all(message, 'mem', split_axis=0, concat_axis=0, tiled=True)  11.1 us
    pallas_call x5, Pallas kernels, call(): pl.pallas_call(kernel, out_shape=jax.ShapeDtypeStruct(shape, BF16), in_sp...  10.8 us
    ppermute x2, starting transfers between devices, from_behind(): return lax.ppermute(block, 'mem', route)  5.28 us
    ppermute x1, starting transfers between devices, swap_beyond(): return lax.ppermute(block, ('mem', 'tile'), route)  4.99 us
    ppermute x2, waiting for transfers between devices, from_behind(): return lax.ppermute(block, 'mem', route)  4.87 us
    ppermute x2, starting transfers between devices, swap_cores(): lax.ppermute(block, 'mem', [(i, i ^ 1) for i in range(lax.axis_size('mem'...  4.19 us
  transfers between devices with their start and end apart: 6, of which 5 were waited for; matrix products, arithmetic and copies ran while one was open for 0% of the time, Pallas kernels for 1%

profile of v2, /device:TPU:199, one launch (start us, length us, event | category | flops | bytes accessed | tf_op | source)
XLA Modules:
  0.0 84.0 jit_solution(17027782282450132177)
XLA Ops:
  0.0 0.0 copy-start
  0.0 1.0 %copy-done = bf16[1,2,256,512]{3,2,1,0:T(8,128)(2,1)S(1)} copy-done((bf16[1,2,256,512]{3,2,1,0:T(8,128)(2,1)S(1)}, bf16[1,2,256,512]{3,2,1,0:T(8,128)(2,1)}, u32[]{:S(2)}) %copy-start) | copy-done | bytes 524312
  1.0 0.8 shard_map.55
  1.9 11.1 %all-to-all-start = ((bf16[64,16,256]{2,1,0:T(8,128)(2,1)}), bf16[64,16,256]{2,1,0:T(8,128)(2,1)S(1)}, u32[]{:S(2)}, u32[]{:S(2)}) async-start(bf16[64,16,256]{2,1,0:T(8,128)(2,1)} %bitcast.6), calls=%async_computation | async-start | bytes 1048576 | tf_op jit(solution)/shard_map/all_to_all | solution.py:423
  13.0 0.0 copy-start.2
  13.0 0.0 copy-start.3
  13.0 0.1 stack.23.place_ref
  13.1 0.0 copy-start.1
  13.1 0.0 copy-start.4
  13.1 0.6 copy-done.2
  13.7 0.0 copy-done.3
  13.7 0.1 copy-done.1
  13.8 0.0 copy-done.4
  13.8 0.6 shard_map.56.own_ref
  14.4 2.3 %collective-permute-start = (bf16[16,128]{1,0:T(8,128)(2,1)S(1)}, bf16[16,128]{1,0:T(8,128)(2,1)S(1)}, u32[]{:S(2)}, u32[]{:S(2)}) collective-permute-start(bf16[16,128]{1,0:T(8,128)(2,1)S(1)} %shard_map.56.own_ref), channel_id=1, source_target_pairs={{0,8},{8,0},{16,24},{24,16},{32,40},{40,32},{48,56},{56,48},{64,72... | collective-permute-start | bytes 12296 | tf_op jit(solution)/shard_map/ppermute | solution.py:396
  16.7 0.8 collective-permute-done.other_ref
  17.5 12.6 %all-to-all-done = bf16[64,16,256]{2,1,0:T(8,128)(2,1)S(1)} async-done(((bf16[64,16,256]{2,1,0:T(8,128)(2,1)}), bf16[64,16,256]{2,1,0:T(8,128)(2,1)S(1)}, u32[]{:S(2)}, u32[]{:S(2)}) %all-to-all-start) | async-done | bytes 524320 | tf_op jit(solution)/shard_map/all_to_all | solution.py:423
  30.2 1.3 %shard_map.57.own_ref = bf16[80,256]{1,0:T(8,128)(2,1)S(1)} custom-call(s32[5]{0:T(128)S(1)} %stack.23.place_ref, bf16[1024,256]{1,0:T(8,128)(2,1)S(1)} %bitcast.12, bf16[16,128]{1,0:T(8,128)(2,1)S(1)} %shard_map.56.own_ref, bf16[16,128]{1,0:T(8,128)(2,1)S(1)} %collective-permute-done.other_ref), custom_call_target="tpu_custom_call" | custom-call | flops 134217728 | bytes 524288 | tf_op jit(solution)/shard_map/pallas_call | solution.py:337
  31.4 5.0 %collective-permute-start.2 = (bf16[80,256]{1,0:T(8,128)(2,1)S(1)}, bf16[80,256]{1,0:T(8,128)(2,1)S(1)}, u32[]{:S(2)}, u32[]{:S(2)}) collective-permute-start(bf16[80,256]{1,0:T(8,128)(2,1)S(1)} %shard_map.57.own_ref), channel_id=1, source_target_pairs={{8,1},{1,8},{9,2},{2,9},{10,3},{3,10},{11,4},{4,11},{12,5},{5,12},... | collective-permute-start | bytes 122888 | tf_op jit(solution)/shard_map/ppermute | solution.py:406
  36.4 1.9 %collective-permute-start.1 = (bf16[80,256]{1,0:T(8,128)(2,1)S(1)}, bf16[80,256]{1,0:T(8,128)(2,1)S(1)}, u32[]{:S(2)}, u32[]{:S(2)}) collective-permute-start(bf16[80,256]{1,0:T(8,128)(2,1)S(1)} %shard_map.57.own_ref), channel_id=1, source_target_pairs={{0,8},{8,0},{16,24},{24,16},{32,40},{40,32},{48,56},{56,48},{64,72... | collective-permute-start | bytes 122888 | tf_op jit(solution)/shard_map/ppermute | solution.py:396
  38.4 0.0 collective-permute-done.2.beyond_ref
  38.4 1.2 %collective-permute-done.1.other_ref = bf16[80,256]{1,0:T(8,128)(2,1)S(1)} collective-permute-done((bf16[80,256]{1,0:T(8,128)(2,1)S(1)}, bf16[80,256]{1,0:T(8,128)(2,1)S(1)}, u32[]{:S(2)}, u32[]{:S(2)}) %collective-permute-start.1) | collective-permute-done | bytes 40992 | tf_op jit(solution)/shard_map/ppermute | solution.py:396
  39.6 2.9 %collective-permute-start.4 = (bf16[80,512]{1,0:T(8,128)(2,1)S(1)}, bf16[80,512]{1,0:T(8,128)(2,1)S(1)}, u32[]{:S(2)}, u32[]{:S(2)}) collective-permute-start(bf16[80,512]{1,0:T(8,128)(2,1)S(1)} %shard_map.58.here_ref), channel_id=1, source_target_pairs={{16,0},{24,8},{32,16},{40,24},{48,32},{56,40},{64,48},{72,56},{80,... | collective-permute-start | bytes 245768 | tf_op jit(solution)/shard_map/ppermute | solution.py:412
  42.5 2.4 %collective-permute-start.3 = (bf16[80,512]{1,0:T(8,128)(2,1)S(1)}, bf16[80,512]{1,0:T(8,128)(2,1)S(1)}, u32[]{:S(2)}, u32[]{:S(2)}) collective-permute-start(bf16[80,512]{1,0:T(8,128)(2,1)S(1)} %shard_map.58.here_ref), channel_id=1, source_target_pairs={{0,16},{8,24},{16,32},{24,40},{32,48},{40,56},{48,64},{56,72},{64,... | collective-permute-start | bytes 245768 | tf_op jit(solution)/shard_map/ppermute | solution.py:412
  44.9 0.5 collective-permute-done.4.south_ref
  45.4 4.4 %collective-permute-done.3.north_ref = bf16[80,512]{1,0:T(8,128)(2,1)S(1)} collective-permute-done((bf16[80,512]{1,0:T(8,128)(2,1)S(1)}, bf16[80,512]{1,0:T(8,128)(2,1)S(1)}, u32[]{:S(2)}, u32[]{:S(2)}) %collective-permute-start.3) | collective-permute-done | bytes 81952 | tf_op jit(solution)/shard_map/ppermute | solution.py:412
  49.8 7.8 %shard_map.59 = bf16[1024,256]{1,0:T(8,128)(2,1)S(1)} custom-call(s32[5]{0:T(128)S(1)} %stack.23.place_ref, bf16[1024,256]{1,0:T(8,128)(2,1)S(1)} %bitcast.13, bf16[80,512]{1,0:T(8,128)(2,1)S(1)} %collective-permute-done.3.north_ref, bf16[80,512]{1,0:T(8,128)(2,1)S(1)} %shard_map.58.here_ref, bf16[80,512]{1,0:T(8,128)(2,1)S(1)} %collective-permute-done.4.south_ref), custom_call_target="tpu_custom_call" | custom-call | flops 1073741824 | bytes 1048576 | tf_op jit(solution)/shard_map/pallas_call | solution.py:337
  57.6 25.6 %all_to_all.22 = bf16[64,16,256]{2,1,0:T(8,128)(2,1)S(1)} all-to-all(bf16[64,16,256]{2,1,0:T(8,128)(2,1)S(1)} %bitcast.16), channel_id=1, replica_groups=mesh['mem'=64,'tile'=8] {'mem'}, dimensions={0} | all-to-all | bytes 1048576 | tf_op jit(solution)/shard_map/all_to_all | solution.py:429
  83.2 0.8 shard_map.60
  (1 shorter events, 0.0 us)
Async XLA Ops:
  0.0 1.0 %copy-start = (bf16[1,2,256,512]{3,2,1,0:T(8,128)(2,1)S(1)}, bf16[1,2,256,512]{3,2,1,0:T(8,128)(2,1)}, u32[]{:S(2)}) copy-start(bf16[1,2,256,512]{3,2,1,0:T(8,128)(2,1)} %param.5) | copy-start | bytes 1572868
  1.9 28.3 %all-to-all-start = ((bf16[64,16,256]{2,1,0:T(8,128)(2,1)}), bf16[64,16,256]{2,1,0:T(8,128)(2,1)S(1)}, u32[]{:S(2)}, u32[]{:S(2)}) async-start(bf16[64,16,256]{2,1,0:T(8,128)(2,1)} %bitcast.6), calls=%async_computation | async-start | bytes 1048576 | tf_op jit(solution)/shard_map/all_to_all | solution.py:423
  13.0 0.7 copy-start.2
  13.0 0.7 copy-start.3
  13.1 0.7 copy-start.1
  13.1 0.7 copy-start.4
  14.4 3.1 %collective-permute-start = (bf16[16,128]{1,0:T(8,128)(2,1)S(1)}, bf16[16,128]{1,0:T(8,128)(2,1)S(1)}, u32[]{:S(2)}, u32[]{:S(2)}) collective-permute-start(bf16[16,128]{1,0:T(8,128)(2,1)S(1)} %shard_map.56.own_ref), channel_id=1, source_target_pairs={{0,8},{8,0},{16,24},{24,16},{32,40},{40,32},{48,56},{56,48},{64,72... | collective-permute-start | bytes 12296 | tf_op jit(solution)/shard_map/ppermute | solution.py:396
  31.4 6.9 %collective-permute-start.2 = (bf16[80,256]{1,0:T(8,128)(2,1)S(1)}, bf16[80,256]{1,0:T(8,128)(2,1)S(1)}, u32[]{:S(2)}, u32[]{:S(2)}) collective-permute-start(bf16[80,256]{1,0:T(8,128)(2,1)S(1)} %shard_map.57.own_ref), channel_id=1, source_target_pairs={{8,1},{1,8},{9,2},{2,9},{10,3},{3,10},{11,4},{4,11},{12,5},{5,12},... | collective-permute-start | bytes 122888 | tf_op jit(solution)/shard_map/ppermute | solution.py:406
  36.4 3.1 %collective-permute-start.1 = (bf16[80,256]{1,0:T(8,128)(2,1)S(1)}, bf16[80,256]{1,0:T(8,128)(2,1)S(1)}, u32[]{:S(2)}, u32[]{:S(2)}) collective-permute-start(bf16[80,256]{1,0:T(8,128)(2,1)S(1)} %shard_map.57.own_ref), channel_id=1, source_target_pairs={{0,8},{8,0},{16,24},{24,16},{32,40},{40,32},{48,56},{56,48},{64,72... | collective-permute-start | bytes 122888 | tf_op jit(solution)/shard_map/ppermute | solution.py:396
  39.6 5.8 %collective-permute-start.4 = (bf16[80,512]{1,0:T(8,128)(2,1)S(1)}, bf16[80,512]{1,0:T(8,128)(2,1)S(1)}, u32[]{:S(2)}, u32[]{:S(2)}) collective-permute-start(bf16[80,512]{1,0:T(8,128)(2,1)S(1)} %shard_map.58.here_ref), channel_id=1, source_target_pairs={{16,0},{24,8},{32,16},{40,24},{48,32},{56,40},{64,48},{72,56},{80,... | collective-permute-start | bytes 245768 | tf_op jit(solution)/shard_map/ppermute | solution.py:412
  42.5 7.3 %collective-permute-start.3 = (bf16[80,512]{1,0:T(8,128)(2,1)S(1)}, bf16[80,512]{1,0:T(8,128)(2,1)S(1)}, u32[]{:S(2)}, u32[]{:S(2)}) collective-permute-start(bf16[80,512]{1,0:T(8,128)(2,1)S(1)} %shard_map.58.here_ref), channel_id=1, source_target_pairs={{0,16},{8,24},{16,32},{24,40},{32,48},{40,56},{48,64},{56,72},{64,... | collective-permute-start | bytes 245768 | tf_op jit(solution)/shard_map/ppermute | solution.py:412

commit v3 on v2

--- a/solution.py
+++ b/solution.py
@@ -1,3 +1,5 @@
+import functools
+
 import jax
 import jax.numpy as jnp
 from jax import lax
@@ -18,7 +20,7 @@
 STRIPS = HALF // STRIP
 REACH = 8
 CHUNK = 64
-SITE_CHUNK = 128
+SITE_CHUNK = 160
 FACTS = 16
 PACKET = MEMBERS + FACTS
 BATCH_LANES = 4 * SLOTS
@@ -108,30 +110,37 @@
         jnp.where(lane < SLOTS, pltpu.roll(first, SLOTS, 1), second),
     )
     place = lax.broadcasted_iota(jnp.int32, (HALF, 2 * SLOTS), 0)
+    choosers, lines = [], []
+    for facts in batches:
+        col = (facts[6:7] * 128.0 + facts[7:8]).astype(jnp.int32) - place_ref[4]
+        lines.append((facts[9:10] * ROWS + facts[8:9]).astype(jnp.int32) - place_ref[3])
+        choosers.append(jnp.where(place == col, 1.0, 0.0).astype(BF16))
+    values = jnp.dot(field_ref[...], jnp.concatenate(choosers, axis=1), preferred_element_type=F32)
     for batch in range(2):
-        facts = batches[batch]
-        col = (facts[6:7] * 128.0 + facts[7:8]).astype(jnp.int32) - place_ref[4]
-        line = (facts[9:10] * ROWS + facts[8:9]).astype(jnp.int32) - place_ref[3]
-        chooser = jnp.where(place == col, 1.0, 0.0).astype(BF16)
-        scratch[...] = jnp.dot(field_ref[...], chooser, preferred_element_type=F32)
+        lanes = pl.ds(batch * 2 * SLOTS, 2 * SLOTS)
+        scratch[batch] = values[:, batch * 2 * SLOTS : (batch + 1) * 2 * SLOTS]
         total = jnp.zeros((MEMBERS, 2 * SLOTS), F32)
         for index in range(LINES):
-            block = scratch[pl.ds(index, MEMBERS, stride=LINES), :]
-            total = total + jnp.where(line == index, block, 0.0)
-        lanes = pl.ds(batch * 2 * SLOTS, 2 * SLOTS)
+            block = scratch[batch, pl.ds(index, MEMBERS, stride=LINES), :]
+            total = total + jnp.where(lines[batch] == index, block, 0.0)
         packet_ref[pl.ds(0, MEMBERS), lanes] = total.astype(BF16)
-        packet_ref[pl.ds(MEMBERS, FACTS), lanes] = facts.astype(BF16)
+        packet_ref[pl.ds(MEMBERS, FACTS), lanes] = batches[batch].astype(BF16)
 
 
 def merge_kernel(own_ref, other_ref, beyond_ref, cat_ref):
+    lane = lax.broadcasted_iota(jnp.int32, (PACKET, 2 * SLOTS), 1)
     for batch in range(2):
         lanes = pl.ds(batch * 2 * SLOTS, 2 * SLOTS)
-        here = pl.ds(batch * BATCH_LANES, 2 * SLOTS)
         members = pl.ds(0, MEMBERS)
-        facts = pl.ds(MEMBERS, FACTS)
-        cat_ref[members, here] = own_ref[members, lanes] + other_ref[members, lanes]
-        cat_ref[facts, here] = own_ref[facts, lanes]
-        cat_ref[:, pl.ds(batch * BATCH_LANES + 2 * SLOTS, 2 * SLOTS)] = beyond_ref[:, lanes]
+        here = jnp.concatenate(
+            [own_ref[members, lanes] + other_ref[members, lanes], own_ref[pl.ds(MEMBERS, FACTS), lanes]],
+            axis=0,
+        ).astype(F32)
+        beyond = beyond_ref[:, lanes].astype(F32)
+        first = jnp.where(lane < SLOTS, here, pltpu.roll(beyond, SLOTS, 1))
+        second = jnp.where(lane < SLOTS, pltpu.roll(here, SLOTS, 1), beyond)
+        cat_ref[:, pl.ds(batch * BATCH_LANES, 2 * SLOTS)] = first.astype(BF16)
+        cat_ref[:, pl.ds(batch * BATCH_LANES + 2 * SLOTS, 2 * SLOTS)] = second.astype(BF16)
 
 
 def weights_of(columns, datum, noise, live):
@@ -160,14 +169,14 @@
 
 def taper(square):
     inverse = lax.rsqrt(jnp.maximum(square, 1.0))
-    s = square * inverse * 0.25
-    inside = (((-0.25 * s + 0.5) * s + 0.625) * s - 5.0 / 3.0) * s * s + 1.0
-    outside = (
-        ((((s * (1.0 / 12.0) - 0.5) * s + 0.625) * s + 5.0 / 3.0) * s - 5.0) * s
-        + 4.0
-        - (8.0 / 3.0) * inverse
-    )
-    return jnp.where(square <= 16.0, inside, jnp.where(square < 64.0, outside, 0.0))
+    distance = square * inverse
+    inside = ((distance * (-0.25 / 1024.0) + 0.5 / 256.0) * distance + 0.625 / 64.0) * distance
+    inside = (inside - 5.0 / 48.0) * square + 1.0
+    left = jnp.maximum(8.0 - distance, 0.0)
+    left = left * left
+    outside = (distance * (0.125 / 1536.0) + 1.0 / 1536.0) * distance - 1.0 / 1536.0
+    outside = outside * inverse * (left * left)
+    return jnp.where(square <= 16.0, inside, outside)
 
 
 def table_of(pert, mean_weight, pert_weight, row, col, level):
@@ -179,9 +188,12 @@
     return jnp.concatenate([high, low, stack_rows(tail, 16).astype(BF16)], axis=0)
 
 
-def chosen_records(ranks, base, count, table):
-    place = lax.broadcasted_iota(jnp.int32, (count, 1), 0).astype(F32) + base
-    chooser = jnp.where(ranks == place, 1.0, 0.0).astype(BF16)
+def chosen_records(ranks, bases, counts, table):
+    parts = []
+    for index, (base, count) in enumerate(zip(bases, counts)):
+        place = lax.broadcasted_iota(jnp.int32, (count, 1), 0).astype(F32) + base
+        parts.append(jnp.where(ranks[index : index + 1] == place, 1.0, 0.0).astype(BF16))
+    chooser = jnp.concatenate(parts, axis=0)
     return lax.dot_general(chooser, table, (((1,), (1,)), ((), ())), preferred_element_type=F32)
 
 
@@ -194,59 +206,68 @@
     mean_weight = tail[:, 4:5] + tail[:, 5:6]
     pert_weight = tail[:, 6:7] + tail[:, 7:8]
     step = mean_weight - pert_weight * (records[:, :MEMBERS] + records[:, MEMBERS : 2 * MEMBERS])
+    return pert, row, col, level, step * (1.0 / (MEMBERS - 1))
+
+
+def halves(gain):
+    high, low = split(gain)
+    return jnp.concatenate([high, high, low], axis=0)
+
+
+def advance(step, gain):
     high, low = split(step)
-    return pert, row, col, level, jnp.concatenate([high, low, high], axis=0)
-
-
-def advance(step, gain):
-    high, low = split(gain)
     return lax.dot_general(
-        step,
-        jnp.concatenate([high, high, low], axis=0),
+        jnp.concatenate([high, low, high], axis=0),
+        gain,
         (((0,), (0,)), ((), ())),
         preferred_element_type=F32,
     )
 
 
-def level_factor(level, target):
-    return (1.0 / (MEMBERS - 1)) / (1.0 + jnp.abs(level - target))
-
-
-def update_region(ranks, total, table, source, state, wide_state):
-    chunks = (jnp.max(total).astype(jnp.int32) + (CHUNK - 1)) // CHUNK
-
-    def one(index, carry):
-        base = (index * CHUNK).astype(F32)
-        for strip in range(STRIPS):
-            records = chosen_records(ranks[strip : strip + 1], base, CHUNK, table)
-            pert, row, col, level, step = open_records(records)
-            lane = lax.broadcasted_iota(jnp.int32, (1, STRIP), 1).astype(F32) + strip * STRIP
-            across = col - lane
-            across = across * across
-            tile = jnp.floor(row * (1.0 / SPAN_NORTH))
-            beside = [
-                jnp.where(jnp.abs(tile - target) <= 1.0, 1.0, 0.0) for target in range(ROWS // SPAN_NORTH)
-            ]
-            tapers = []
-            for line in range(ROWS):
-                down = row - float(line)
-                tapers.append(taper(across + down * down) * beside[line // SPAN_NORTH])
-            if wide_state:
-                pert = jnp.concatenate([pert, pert[:, :MEMBERS]], axis=1)
-            for target in range(LEVELS):
-                lanes = pl.ds(target * ROWS * STRIP, ROWS * STRIP)
-                factor = level_factor(level, float(target))
-                weight = jnp.concatenate([t * factor for t in tapers], axis=1)
-                covariance = jnp.dot(pert, source[strip, :, lanes], preferred_element_type=F32)
-                state[strip, :, lanes] = state[strip, :, lanes] + advance(step, weight * covariance)
-        return carry
-
-    lax.fori_loop(0, chunks, one, 0)
+def region_step(records, strip, matched):
+    pert, row, col, level, step = open_records(records)
+    lane = lax.broadcasted_iota(jnp.int32, (1, STRIP), 1).astype(F32) + strip * STRIP
+    across = col - lane
+    across = across * across
+    tile = jnp.floor(row * (1.0 / SPAN_NORTH))
+    tapers = []
+    for line in range(ROWS):
+        down = row - float(line)
+        tapers.append(taper(across + down * down))
+    for target in range(LEVELS):
+        factor = jnp.where(level == target, 1.0, 0.5)
+        factors = [
+            jnp.where(jnp.abs(tile - part) <= 1.0, factor, 0.0) for part in range(ROWS // SPAN_NORTH)
+        ]
+        weight = jnp.concatenate(
+            [tapers[line] * factors[line // SPAN_NORTH] for line in range(ROWS)], axis=1
+        )
+        lanes = pl.ds(target * ROWS * STRIP, ROWS * STRIP)
+        cells = matched(strip, lanes)
+        if cells.shape[0] > 2 * MEMBERS:
+            three = jnp.concatenate([pert, pert[:, :MEMBERS]], axis=1)
+            covariance = jnp.dot(three, cells, preferred_element_type=F32)
+        else:
+            covariance = jnp.dot(pert, cells, preferred_element_type=F32)
+        yield lanes, advance(step, halves(weight * covariance))
+
+
+def chunks_of(total, size):
+    return (jnp.max(total).astype(jnp.int32) + (size - 1)) // size
+
+
+def rows_of(cats, rows, batch):
+    parts = []
+    for index, cat in enumerate(cats):
+        start, count = batch * BATCH_LANES, BATCH_LANES
+        if batch == 1 and index != 1:
+            start, count = start + (2 * SLOTS if index == 0 else 0), 2 * SLOTS
+        parts.append(cat[rows, pl.ds(start, count)])
+    return jnp.concatenate(parts, axis=1)
 
 
 def facts_of(cats, batch, place_ref):
-    lanes = pl.ds(batch * BATCH_LANES, BATCH_LANES)
-    facts = jnp.concatenate([c[pl.ds(MEMBERS, FACTS), lanes] for c in cats], axis=1).astype(F32)
+    facts = rows_of(cats, pl.ds(MEMBERS, FACTS), batch).astype(F32)
     datum = facts[0:1] + facts[1:2] + facts[2:3]
     noise = facts[3:4] + facts[4:5] + facts[5:6]
     col = (facts[6:7] * 128.0 + facts[7:8]).astype(jnp.int32) - place_ref[4]
@@ -266,69 +287,122 @@
     return stack_rows(masks, 8)
 
 
-def analysis_kernel(
-    place_ref, field_ref, north_ref, here_ref, south_ref, message_ref, wide, state, narrow, source, site_state
-):
-    cats = (north_ref, here_ref, south_ref)
-    for part in range(STRIPS):
-        wide[part] = field_ref[:, part * STRIP : (part + 1) * STRIP].astype(F32)
-    for strip in range(STRIPS):
-        for line in range(LINES):
-            piece = wide[strip, pl.ds(line, MEMBERS, stride=LINES), :]
-            lanes = pl.ds(line * STRIP, STRIP)
-            state[strip, :, lanes] = piece
-            low = piece.astype(BF16)
-            narrow[strip, :MEMBERS, lanes] = low
-            narrow[strip, MEMBERS:, lanes] = low
-
-    first, sites = (
-        jnp.concatenate([c[pl.ds(0, MEMBERS), pl.ds(b * BATCH_LANES, BATCH_LANES)] for c in cats], axis=1)
-        for b in range(2)
-    )
+def arrange_kernel(strip, field_ref, cells_ref, wide):
+    wide[...] = field_ref[:, strip * STRIP : (strip + 1) * STRIP].astype(F32)
+    for line in range(LINES):
+        piece = wide[pl.ds(line, MEMBERS, stride=LINES), :]
+        cells_ref[:, pl.ds(line * STRIP, STRIP)] = piece.astype(BF16)
+
+
+def analysis_kernel(place_ref, west_ref, east_ref, north_ref, here_ref, south_ref, message_ref, *scratch):
+    refs = (place_ref, (west_ref, east_ref), (north_ref, here_ref, south_ref), message_ref, *scratch)
+    more = analysis(False, *refs)
+
+    @pl.when(more)
+    def _():
+        analysis(True, *refs)
+
+
+def analysis(loops, place_ref, cells, cats, message_ref, wide, state, source, site_state):
+    sizes = [CHUNK] * STRIPS
+    pieces = [slice(strip * CHUNK, (strip + 1) * CHUNK) for strip in range(STRIPS)]
+    members = pl.ds(0, MEMBERS)
+
     datum, noise, col, row, level, live = facts_of(cats, 0, place_ref)
-    pert, mean_weight, pert_weight = weights_of(first.astype(F32), datum, noise, live)
+    datum_1, noise_1, col_1, row_1, level_1, live_1 = facts_of(cats, 1, place_ref)
+    ranks, total = positions(masks_of(col, row, live))
+    ranks_1, total_1 = positions(masks_of(col_1, row_1, live_1))
+    chunks = chunks_of(total[:STRIPS], CHUNK)
+    chunks_1 = chunks_of(total_1[:STRIPS], CHUNK)
+    site_chunks = chunks_of(total[STRIPS : STRIPS + 1], SITE_CHUNK)
+
+    first = rows_of(cats, members, 0).astype(F32)
+    pert, mean_weight, pert_weight = weights_of(first, datum, noise, live)
     table = table_of(pert, mean_weight, pert_weight, row, col, level)
-    ranks, total = positions(masks_of(col, row, live))
-    update_region(ranks, total[:STRIPS], table, narrow, state, False)
-
-    site_state[...] = sites.astype(F32)
-    datum_1, noise_1, col_1, row_1, level_1, live_1 = facts_of(cats, 1, place_ref)
+    records = chosen_records(ranks, [0.0] * (STRIPS + 1), sizes + [SITE_CHUNK], table)
+
+    sites = rows_of(cats, members, 1)
     site_row = row_1.astype(F32)
     site_col = col_1.astype(F32)
     site_tile = (row_1 >> 2).astype(F32)
-    doubled = jnp.concatenate([sites, sites], axis=0)
-
-    def one(index, carry):
-        base = (index * SITE_CHUNK).astype(F32)
-        records = chosen_records(ranks[STRIPS : STRIPS + 1], base, SITE_CHUNK, table)
+
+    def site_step(records):
         obs, obs_row, obs_col, obs_level, step = open_records(records)
         down = obs_row - site_row
         across = obs_col - site_col
-        weight = taper(down * down + across * across) * level_factor(obs_level, level_1)
+        weight = taper(down * down + across * across)
+        weight = weight * jnp.where(obs_level == level_1, 1.0, 0.5)
         obs_tile = jnp.floor(obs_row * (1.0 / SPAN_NORTH))
         weight = jnp.where(jnp.abs(obs_tile - site_tile) <= 1.0, weight, 0.0)
-        covariance = jnp.dot(obs, doubled, preferred_element_type=F32)
-        site_state[...] = site_state[...] + advance(step, weight * covariance)
+        covariance = jnp.dot(obs, jnp.concatenate([sites, sites], axis=0), preferred_element_type=F32)
+        return advance(step, halves(weight * covariance))
+
+    after = sites.astype(F32) + site_step(records[STRIPS * CHUNK :])
+
+    def more_sites(index, carry):
+        base = (index * SITE_CHUNK).astype(F32)
+        more = chosen_records(ranks[STRIPS : STRIPS + 1], [base], [SITE_CHUNK], table)
+        site_state[...] = site_state[...] + site_step(more)
         return carry
 
-    chunks = (jnp.max(total[STRIPS : STRIPS + 1]).astype(jnp.int32) + (SITE_CHUNK - 1)) // SITE_CHUNK
-    lax.fori_loop(0, chunks, one, 0)
-
-    pert, mean_weight, pert_weight = weights_of(site_state[...], datum_1, noise_1, live_1)
+    if loops:
+        site_state[...] = after
+        lax.fori_loop(1, site_chunks, more_sites, 0)
+        after = site_state[...]
+
+    def more_cells(ranks, table, matched):
+        def one(index, carry):
+            base = (index * CHUNK).astype(F32)
+            more = chosen_records(ranks, [base] * STRIPS, sizes, table)
+            for strip in range(STRIPS):
+                for lanes, moved in region_step(more[pieces[strip]], strip, matched):
+                    state[strip, :, lanes] = state[strip, :, lanes] + moved
+            return carry
+
+        return one
+
+    def cells_of(strip, lanes):
+        once = cells[strip][:, lanes]
+        return jnp.concatenate([once, once], axis=0)
+
+    for strip in range(STRIPS):
+        for lanes, moved in region_step(records[pieces[strip]], strip, cells_of):
+            state[strip, :, lanes] = cells[strip][:, lanes].astype(F32) + moved
+    if loops:
+        lax.fori_loop(1, chunks, more_cells(ranks, table, cells_of), 0)
+
+    pert, mean_weight, pert_weight = weights_of(after, datum_1, noise_1, live_1)
     table_1 = table_of(pert, mean_weight, pert_weight, row_1, col_1, level_1)
-    ranks_1, total_1 = positions(masks_of(col_1, row_1, live_1))
+    records_1 = chosen_records(ranks_1, [0.0] * STRIPS, sizes, table_1)
+
+    def split_cells(strip, lanes):
+        high, low = split(state[strip, :, lanes])
+        if loops:
+            source[strip, :MEMBERS, lanes] = high
+            source[strip, MEMBERS:, lanes] = low
+        return jnp.concatenate([high, high, low], axis=0)
+
+    def source_of(strip, lanes):
+        high = source[strip, :MEMBERS, lanes]
+        return jnp.concatenate([high, high, source[strip, MEMBERS:, lanes]], axis=0)
+
     for strip in range(STRIPS):
-        high, low = split(state[strip])
-        source[strip, :MEMBERS, :] = high
-        source[strip, MEMBERS : 2 * MEMBERS, :] = high
-        source[strip, 2 * MEMBERS :, :] = low
-    update_region(ranks_1, total_1[:STRIPS], table_1, source, state, True)
-
-    for strip in range(STRIPS):
-        for line in range(LINES):
-            wide[strip, pl.ds(line, MEMBERS, stride=LINES), :] = state[strip, :, pl.ds(line * STRIP, STRIP)]
+        for lanes, moved in region_step(records_1[pieces[strip]], strip, split_cells):
+            if loops:
+                state[strip, :, lanes] = state[strip, :, lanes] + moved
+                continue
+            done = state[strip, :, lanes] + moved
+            for line in range(ROWS):
+                place = pl.ds(lanes.start // STRIP + line, MEMBERS, stride=LINES)
+                wide[strip, place, :] = done[:, line * STRIP : (line + 1) * STRIP]
+    if loops:
+        lax.fori_loop(1, chunks_1, more_cells(ranks_1, table_1, source_of), 0)
+        for strip in range(STRIPS):
+            for line in range(LINES):
+                wide[strip, pl.ds(line, MEMBERS, stride=LINES), :] = state[strip, :, pl.ds(line * STRIP, STRIP)]
     for part in range(STRIPS):
         message_ref[:, part * STRIP : (part + 1) * STRIP] = wide[part].astype(BF16)
+    return (jnp.maximum(chunks, chunks_1) > 1) | (site_chunks > 1)
 
 
 def call(kernel, shape, operands, scratch=(), scalars=0, flops=0, moved=1 << 18):
@@ -369,7 +443,7 @@
 
 
 def pick(place, field, own, other):
-    scratch = [pltpu.VMEM((MEMBERS * LINES, 2 * SLOTS), F32)]
+    scratch = [pltpu.VMEM((2, MEMBERS * LINES, 2 * SLOTS), F32)]
     return call(
         pick_kernel, (PACKET, 4 * SLOTS), (place, field, own, other), scratch, 1, 1 << 27, 1 << 19
     )
@@ -379,16 +453,21 @@
     return call(merge_kernel, (PACKET, 2 * BATCH_LANES), (own, other, beyond))
 
 
-def analyse(place, field, north, here, south):
+def arrange(field, strip):
+    kernel = functools.partial(arrange_kernel, strip)
+    scratch = [pltpu.VMEM((MEMBERS * LINES, STRIP), F32)]
+    return call(kernel, (MEMBERS, LINES * STRIP), (field,), scratch, moved=1 << 19)
+
+
+def analyse(place, west, east, north, here, south):
     scratch = [
         pltpu.VMEM((STRIPS, MEMBERS * LINES, STRIP), F32),
         pltpu.VMEM((STRIPS, MEMBERS, LINES * STRIP), F32),
         pltpu.VMEM((STRIPS, 2 * MEMBERS, LINES * STRIP), BF16),
-        pltpu.VMEM((STRIPS, 3 * MEMBERS, LINES * STRIP), BF16),
-        pltpu.VMEM((MEMBERS, 3 * BATCH_LANES), F32),
+        pltpu.VMEM((MEMBERS, 2 * BATCH_LANES), F32),
     ]
     return call(
-        analysis_kernel, MESSAGE, (place, field, north, here, south), scratch, 1, 1 << 30, 1 << 20
+        analysis_kernel, MESSAGE, (place, west, east, north, here, south), scratch, 1, 1 << 30, 1 << 20
     )
 
 
@@ -423,9 +502,15 @@
     field = lax.all_to_all(message, "mem", split_axis=0, concat_axis=0, tiled=True)
     facts = state_facts(place, datum, noise, point, count.reshape(2))
     packet = pick(place, field, facts, swap_cores(facts))
-    here = merge(packet, swap_cores(packet), swap_beyond(packet))
-    north, south = from_behind(here, 2), from_behind(here, -2)
-    message = analyse(place, field, north, here, south)
+    field, packet = lax.optimization_barrier((field, packet))
+    other = swap_cores(packet)
+    west, packet = lax.optimization_barrier((arrange(field, 0), packet))
+    here = merge(packet, other, swap_beyond(packet))
+    field, here = lax.optimization_barrier((field, here))
+    north = from_behind(here, 2)
+    east, here = lax.optimization_barrier((arrange(field, 1), here))
+    south = from_behind(here, -2)
+    message = analyse(place, west, east, north, here, south)
     message = lax.all_to_all(message, "mem", split_axis=0, concat_axis=0, tiled=True)
     return unpack(message)[None]
 

time: 84.4 us -> 81.7 us (0.968)
  the two profiles are of different devices: /device:TPU:199 before, /device:TPU:263 now
where the time goes in v3:
time: 81.7 us; the launch traced here: 81.3 us
  blocking collectives  26.4 us (32%)
  starting transfers between devices  24.1 us (29%)
  waiting for transfers between devices  20.3 us (25%)
  Pallas kernels  8.56 us (10%)
  local copies, waits for them, and re-layouts  1.81 us (2%)
    all_to_all x1, blocking collectives, on_device(): lax.all_to_all(message, 'mem', split_axis=0, concat_axis=0, tiled=True)  26.4 us
    all_to_all x1, waiting for transfers between devices, on_device(): lax.all_to_all(message, 'mem', split_axis=0, concat_axis=0, tiled=True)  12.6 us
    all_to_all x1, starting transfers between devices, on_device(): lax.all_to_all(message, 'mem', split_axis=0, concat_axis=0, tiled=True)  11.1 us
    pallas_call x7, Pallas kernels, call(): pl.pallas_call(kernel, out_shape=jax.ShapeDtypeStruct(shape, BF16), in_sp...  7.93 us
    ppermute x2, starting transfers between devices, from_behind(): return lax.ppermute(block, 'mem', route)  5.28 us
    ppermute x2, waiting for transfers between devices, from_behind(): return lax.ppermute(block, 'mem', route)  5.05 us
    ppermute x2, starting transfers between devices, swap_cores(): lax.ppermute(block, 'mem', [(i, i ^ 1) for i in range(lax.axis_size('mem'...  4.19 us
    ppermute x1, starting transfers between devices, swap_beyond(): return lax.ppermute(block, ('mem', 'tile'), route)  3.48 us
  transfers between devices with their start and end apart: 6, of which 4 were waited for; matrix products, arithmetic and copies ran while one was open for 0% of the time, Pallas kernels for 1%

profile of v3, /device:TPU:263, one launch (start us, length us, event | category | flops | bytes accessed | tf_op | source)
XLA Modules:
  0.0 81.3 jit_solution(10505173020494401410)
XLA Ops:
  0.0 0.0 copy-start
  0.0 1.0 %copy-done = bf16[1,2,256,512]{3,2,1,0:T(8,128)(2,1)S(1)} copy-done((bf16[1,2,256,512]{3,2,1,0:T(8,128)(2,1)S(1)}, bf16[1,2,256,512]{3,2,1,0:T(8,128)(2,1)}, u32[]{:S(2)}) %copy-start) | copy-done | bytes 524312
  1.0 0.8 %shard_map.55 = bf16[1024,256]{1,0:T(8,128)(2,1)} custom-call(bf16[2,256,512]{2,1,0:T(8,128)(2,1)S(1)} %bitcast.16), custom_call_target="tpu_custom_call" | custom-call | bytes 1048576 | tf_op jit(solution)/shard_map/pallas_call | solution.py:411
  1.9 11.1 %all-to-all-start = ((bf16[64,16,256]{2,1,0:T(8,128)(2,1)}), bf16[64,16,256]{2,1,0:T(8,128)(2,1)S(1)}, u32[]{:S(2)}, u32[]{:S(2)}) async-start(bf16[64,16,256]{2,1,0:T(8,128)(2,1)} %bitcast.6), calls=%async_computation | async-start | bytes 1048576 | tf_op jit(solution)/shard_map/all_to_all | solution.py:502
  13.0 0.0 copy-start.2
  13.0 0.0 copy-start.3
  13.0 0.1 stack.23.place_ref
  13.1 0.0 copy-start.1
  13.1 0.0 copy-start.4
  13.1 0.6 copy-done.2
  13.7 0.0 copy-done.3
  13.7 0.1 copy-done.1
  13.8 0.0 copy-done.4
  13.8 0.6 shard_map.56.own_ref
  14.4 2.3 %collective-permute-start = (bf16[16,128]{1,0:T(8,128)(2,1)S(1)}, bf16[16,128]{1,0:T(8,128)(2,1)S(1)}, u32[]{:S(2)}, u32[]{:S(2)}) collective-permute-start(bf16[16,128]{1,0:T(8,128)(2,1)S(1)} %shard_map.56.own_ref), channel_id=1, source_target_pairs={{0,8},{8,0},{16,24},{24,16},{32,40},{40,32},{48,56},{56,48},{64,72... | collective-permute-start | bytes 12296 | tf_op jit(solution)/shard_map/ppermute | solution.py:475
  16.7 0.8 collective-permute-done.other_ref
  17.5 12.6 %all-to-all-done = bf16[64,16,256]{2,1,0:T(8,128)(2,1)S(1)} async-done(((bf16[64,16,256]{2,1,0:T(8,128)(2,1)}), bf16[64,16,256]{2,1,0:T(8,128)(2,1)S(1)}, u32[]{:S(2)}, u32[]{:S(2)}) %all-to-all-start) | async-done | bytes 524320 | tf_op jit(solution)/shard_map/all_to_all | solution.py:502
  30.2 1.2 %shard_map.57.own_ref = bf16[80,256]{1,0:T(8,128)(2,1)S(1)} custom-call(s32[5]{0:T(128)S(1)} %stack.23.place_ref, bf16[1024,256]{1,0:T(8,128)(2,1)S(1)} %bitcast.12, bf16[16,128]{1,0:T(8,128)(2,1)S(1)} %shard_map.56.own_ref, bf16[16,128]{1,0:T(8,128)(2,1)S(1)} %collective-permute-done.other_ref), custom_call_target="tpu_custom_call" | custom-call | flops 134217728 | bytes 524288 | tf_op jit(solution)/shard_map/pallas_call | solution.py:411
  31.4 1.9 %collective-permute-start.1 = (bf16[80,256]{1,0:T(8,128)(2,1)S(1)}, bf16[80,256]{1,0:T(8,128)(2,1)S(1)}, u32[]{:S(2)}, u32[]{:S(2)}) collective-permute-start(bf16[80,256]{1,0:T(8,128)(2,1)S(1)} %shard_map.57.own_ref), channel_id=1, source_target_pairs={{0,8},{8,0},{16,24},{24,16},{32,40},{40,32},{48,56},{56,48},{64,72... | collective-permute-start | bytes 122888 | tf_op jit(solution)/shard_map/ppermute | solution.py:475
  33.3 0.2 shard_map.58.west_ref
  33.5 3.5 %collective-permute-start.2 = (bf16[80,256]{1,0:T(8,128)(2,1)S(1)}, bf16[80,256]{1,0:T(8,128)(2,1)S(1)}, u32[]{:S(2)}, u32[]{:S(2)}) collective-permute-start(bf16[80,256]{1,0:T(8,128)(2,1)S(1)} %shard_map.57.own_ref), channel_id=1, source_target_pairs={{8,1},{1,8},{9,2},{2,9},{10,3},{3,10},{11,4},{4,11},{12,5},{5,12},... | collective-permute-start | bytes 122888 | tf_op jit(solution)/shard_map/ppermute | solution.py:485
  37.0 0.0 collective-permute-done.1.other_ref
  37.0 1.8 %collective-permute-done.2.beyond_ref = bf16[80,256]{1,0:T(8,128)(2,1)S(1)} collective-permute-done((bf16[80,256]{1,0:T(8,128)(2,1)S(1)}, bf16[80,256]{1,0:T(8,128)(2,1)S(1)}, u32[]{:S(2)}, u32[]{:S(2)}) %collective-permute-start.2) | collective-permute-done | bytes 40992 | tf_op jit(solution)/shard_map/ppermute | solution.py:485
  38.9 0.1 shard_map.59.here_ref
  39.0 0.2 shard_map.60.east_ref
  39.2 3.0 %collective-permute-start.4 = (bf16[80,512]{1,0:T(8,128)(2,1)S(1)}, bf16[80,512]{1,0:T(8,128)(2,1)S(1)}, u32[]{:S(2)}, u32[]{:S(2)}) collective-permute-start(bf16[80,512]{1,0:T(8,128)(2,1)S(1)} %shard_map.59.here_ref), channel_id=1, source_target_pairs={{16,0},{24,8},{32,16},{40,24},{48,32},{56,40},{64,48},{72,56},{80,... | collective-permute-start | bytes 245768 | tf_op jit(solution)/shard_map/ppermute | solution.py:491
  42.2 2.2 %collective-permute-start.3 = (bf16[80,512]{1,0:T(8,128)(2,1)S(1)}, bf16[80,512]{1,0:T(8,128)(2,1)S(1)}, u32[]{:S(2)}, u32[]{:S(2)}) collective-permute-start(bf16[80,512]{1,0:T(8,128)(2,1)S(1)} %shard_map.59.here_ref), channel_id=1, source_target_pairs={{0,16},{8,24},{16,32},{24,40},{32,48},{40,56},{48,64},{56,72},{64,... | collective-permute-start | bytes 245768 | tf_op jit(solution)/shard_map/ppermute | solution.py:491
  44.5 0.0 collective-permute-done.4.south_ref
  44.5 5.0 %collective-permute-done.3.north_ref = bf16[80,512]{1,0:T(8,128)(2,1)S(1)} collective-permute-done((bf16[80,512]{1,0:T(8,128)(2,1)S(1)}, bf16[80,512]{1,0:T(8,128)(2,1)S(1)}, u32[]{:S(2)}, u32[]{:S(2)}) %collective-permute-start.3) | collective-permute-done | bytes 81952 | tf_op jit(solution)/shard_map/ppermute | solution.py:491
  49.5 4.5 %shard_map.61 = bf16[1024,256]{1,0:T(8,128)(2,1)S(1)} custom-call(s32[5]{0:T(128)S(1)} %stack.23.place_ref, bf16[64,2048]{1,0:T(8,128)(2,1)S(1)} %shard_map.58.west_ref, bf16[64,2048]{1,0:T(8,128)(2,1)S(1)} %shard_map.60.east_ref, bf16[80,512]{1,0:T(8,128)(2,1)S(1)} %collective-permute-done.3.north_ref, bf16[80,512]{1,0:T(8,128)(2,1)S(1)} %shard_map.59.here_ref, ...), custom_call_target="tpu_custom_call" | custom-call | flops 1073741824 | bytes 1048576 | tf_op jit(solution)/shard_map/pallas_call | solution.py:411
  54.1 26.4 %all_to_all.22 = bf16[64,16,256]{2,1,0:T(8,128)(2,1)S(1)} all-to-all(bf16[64,16,256]{2,1,0:T(8,128)(2,1)S(1)} %bitcast.17), channel_id=1, replica_groups=mesh['mem'=64,'tile'=8] {'mem'}, dimensions={0} | all-to-all | bytes 1048576 | tf_op jit(solution)/shard_map/all_to_all | solution.py:514
  80.5 0.8 %shard_map.62 = bf16[2,256,512]{2,1,0:T(8,128)(2,1)} custom-call(bf16[1024,256]{1,0:T(8,128)(2,1)S(1)} %bitcast.15), custom_call_target="tpu_custom_call" | custom-call | bytes 1048576 | tf_op jit(solution)/shard_map/pallas_call | solution.py:411
Async XLA Ops:
  0.0 1.0 %copy-start = (bf16[1,2,256,512]{3,2,1,0:T(8,128)(2,1)S(1)}, bf16[1,2,256,512]{3,2,1,0:T(8,128)(2,1)}, u32[]{:S(2)}) copy-start(bf16[1,2,256,512]{3,2,1,0:T(8,128)(2,1)} %param.5) | copy-start | bytes 1572868
  1.9 28.3 %all-to-all-start = ((bf16[64,16,256]{2,1,0:T(8,128)(2,1)}), bf16[64,16,256]{2,1,0:T(8,128)(2,1)S(1)}, u32[]{:S(2)}, u32[]{:S(2)}) async-start(bf16[64,16,256]{2,1,0:T(8,128)(2,1)} %bitcast.6), calls=%async_computation | async-start | bytes 1048576 | tf_op jit(solution)/shard_map/all_to_all | solution.py:502
  13.0 0.7 copy-start.2
  13.0 0.7 copy-start.3
  13.1 0.7 copy-start.1
  13.1 0.7 copy-start.4
  14.4 3.1 %collective-permute-start = (bf16[16,128]{1,0:T(8,128)(2,1)S(1)}, bf16[16,128]{1,0:T(8,128)(2,1)S(1)}, u32[]{:S(2)}, u32[]{:S(2)}) collective-permute-start(bf16[16,128]{1,0:T(8,128)(2,1)S(1)} %shard_map.56.own_ref), channel_id=1, source_target_pairs={{0,8},{8,0},{16,24},{24,16},{32,40},{40,32},{48,56},{56,48},{64,72... | collective-permute-start | bytes 12296 | tf_op jit(solution)/shard_map/ppermute | solution.py:475
  31.4 5.6 %collective-permute-start.1 = (bf16[80,256]{1,0:T(8,128)(2,1)S(1)}, bf16[80,256]{1,0:T(8,128)(2,1)S(1)}, u32[]{:S(2)}, u32[]{:S(2)}) collective-permute-start(bf16[80,256]{1,0:T(8,128)(2,1)S(1)} %shard_map.57.own_ref), channel_id=1, source_target_pairs={{0,8},{8,0},{16,24},{24,16},{32,40},{40,32},{48,56},{56,48},{64,72... | collective-permute-start | bytes 122888 | tf_op jit(solution)/shard_map/ppermute | solution.py:475
  33.5 5.3 %collective-permute-start.2 = (bf16[80,256]{1,0:T(8,128)(2,1)S(1)}, bf16[80,256]{1,0:T(8,128)(2,1)S(1)}, u32[]{:S(2)}, u32[]{:S(2)}) collective-permute-start(bf16[80,256]{1,0:T(8,128)(2,1)S(1)} %shard_map.57.own_ref), channel_id=1, source_target_pairs={{8,1},{1,8},{9,2},{2,9},{10,3},{3,10},{11,4},{4,11},{12,5},{5,12},... | collective-permute-start | bytes 122888 | tf_op jit(solution)/shard_map/ppermute | solution.py:485
  39.2 5.3 %collective-permute-start.4 = (bf16[80,512]{1,0:T(8,128)(2,1)S(1)}, bf16[80,512]{1,0:T(8,128)(2,1)S(1)}, u32[]{:S(2)}, u32[]{:S(2)}) collective-permute-start(bf16[80,512]{1,0:T(8,128)(2,1)S(1)} %shard_map.59.here_ref), channel_id=1, source_target_pairs={{16,0},{24,8},{32,16},{40,24},{48,32},{56,40},{64,48},{72,56},{80,... | collective-permute-start | bytes 245768 | tf_op jit(solution)/shard_map/ppermute | solution.py:491
  42.2 7.3 %collective-permute-start.3 = (bf16[80,512]{1,0:T(8,128)(2,1)S(1)}, bf16[80,512]{1,0:T(8,128)(2,1)S(1)}, u32[]{:S(2)}, u32[]{:S(2)}) collective-permute-start(bf16[80,512]{1,0:T(8,128)(2,1)S(1)} %shard_map.59.here_ref), channel_id=1, source_target_pairs={{0,16},{8,24},{16,32},{24,40},{32,48},{40,56},{48,64},{56,72},{64,... | collective-permute-start | bytes 245768 | tf_op jit(solution)/shard_map/ppermute | solution.py:491

commit v4 on v3

--- a/solution.py
+++ b/solution.py
@@ -13,6 +13,7 @@
 SPAN_EAST = 512
 SLOTS = 64
 CHIPS = 32
+CHIP_LINE = 8
 ROWS = 2 * SPAN_NORTH
 LINES = LEVELS * ROWS
 HALF = SPAN_EAST // 2
@@ -29,6 +30,11 @@
 VMEM_LIMIT = 48 * 1024 * 1024
 
 
+def chip_of(region):
+    line, place = divmod(region, CHIP_LINE)
+    return line * CHIP_LINE + (CHIP_LINE - 1 - place if line % 2 else place)
+
+
 def split(values):
     high = values.astype(BF16)
     return high, (values - high.astype(F32)).astype(BF16)
@@ -43,7 +49,7 @@
             rows = slice(chip * ROWS, (chip + 1) * ROWS)
             for half in range(2):
                 lanes = slice(half * HALF, (half + 1) * HALF)
-                place = (2 * (2 * group + chip) + half) * LINES
+                place = (2 * chip_of(2 * group + chip) + half) * LINES
                 message_ref[pl.ds(place, LINES), :] = jnp.concatenate(
                     [upper[rows, lanes], lower[rows, lanes]], axis=0
                 ).astype(BF16)
@@ -54,7 +60,7 @@
         for half in range(2):
             lanes = pl.ds(half * HALF, HALF)
             first, second = (
-                message_ref[pl.ds((2 * (2 * group + chip) + half) * LINES, LINES), :].astype(F32)
+                message_ref[pl.ds((2 * chip_of(2 * group + chip) + half) * LINES, LINES), :].astype(F32)
                 for chip in range(2)
             )
             for level in range(LEVELS):
@@ -256,18 +262,19 @@
     return (jnp.max(total).astype(jnp.int32) + (size - 1)) // size
 
 
-def rows_of(cats, rows, batch):
+def rows_of(cats, rows, batch, place_ref):
     parts = []
     for index, cat in enumerate(cats):
         start, count = batch * BATCH_LANES, BATCH_LANES
         if batch == 1 and index != 1:
-            start, count = start + (2 * SLOTS if index == 0 else 0), 2 * SLOTS
+            north = place_ref[5] if index == 0 else 1 - place_ref[5]
+            start, count = pl.multiple_of(start + north * (2 * SLOTS), 2 * SLOTS), 2 * SLOTS
         parts.append(cat[rows, pl.ds(start, count)])
     return jnp.concatenate(parts, axis=1)
 
 
 def facts_of(cats, batch, place_ref):
-    facts = rows_of(cats, pl.ds(MEMBERS, FACTS), batch).astype(F32)
+    facts = rows_of(cats, pl.ds(MEMBERS, FACTS), batch, place_ref).astype(F32)
     datum = facts[0:1] + facts[1:2] + facts[2:3]
     noise = facts[3:4] + facts[4:5] + facts[5:6]
     col = (facts[6:7] * 128.0 + facts[7:8]).astype(jnp.int32) - place_ref[4]
@@ -294,8 +301,8 @@
         cells_ref[:, pl.ds(line * STRIP, STRIP)] = piece.astype(BF16)
 
 
-def analysis_kernel(place_ref, west_ref, east_ref, north_ref, here_ref, south_ref, message_ref, *scratch):
-    refs = (place_ref, (west_ref, east_ref), (north_ref, here_ref, south_ref), message_ref, *scratch)
+def analysis_kernel(place_ref, west_ref, east_ref, next_ref, here_ref, last_ref, message_ref, *scratch):
+    refs = (place_ref, (west_ref, east_ref), (next_ref, here_ref, last_ref), message_ref, *scratch)
     more = analysis(False, *refs)
 
     @pl.when(more)
@@ -316,12 +323,12 @@
     chunks_1 = chunks_of(total_1[:STRIPS], CHUNK)
     site_chunks = chunks_of(total[STRIPS : STRIPS + 1], SITE_CHUNK)
 
-    first = rows_of(cats, members, 0).astype(F32)
+    first = rows_of(cats, members, 0, place_ref).astype(F32)
     pert, mean_weight, pert_weight = weights_of(first, datum, noise, live)
     table = table_of(pert, mean_weight, pert_weight, row, col, level)
     records = chosen_records(ranks, [0.0] * (STRIPS + 1), sizes + [SITE_CHUNK], table)
 
-    sites = rows_of(cats, members, 1)
+    sites = rows_of(cats, members, 1, place_ref)
     site_row = row_1.astype(F32)
     site_col = col_1.astype(F32)
     site_tile = (row_1 >> 2).astype(F32)
@@ -459,7 +466,7 @@
     return call(kernel, (MEMBERS, LINES * STRIP), (field,), scratch, moved=1 << 19)
 
 
-def analyse(place, west, east, north, here, south):
+def analyse(place, west, east, first, here, second):
     scratch = [
         pltpu.VMEM((STRIPS, MEMBERS * LINES, STRIP), F32),
         pltpu.VMEM((STRIPS, MEMBERS, LINES * STRIP), F32),
@@ -467,12 +474,17 @@
         pltpu.VMEM((MEMBERS, 2 * BATCH_LANES), F32),
     ]
     return call(
-        analysis_kernel, MESSAGE, (place, west, east, north, here, south), scratch, 1, 1 << 30, 1 << 20
+        analysis_kernel, MESSAGE, (place, west, east, first, here, second), scratch, 1, 1 << 30, 1 << 20
     )
 
 
 def swap_cores(block):
     return lax.ppermute(block, "mem", [(i, i ^ 1) for i in range(lax.axis_size("mem"))])
+
+
+def to_region(block, change):
+    route = [(2 * k + h, 2 * chip_of(k) + (h ^ change)) for k in range(CHIPS) for h in range(2)]
+    return lax.ppermute(block, "mem", route)
 
 
 def swap_beyond(block):
@@ -485,9 +497,12 @@
     return lax.ppermute(block, ("mem", "tile"), route)
 
 
-def from_behind(block, distance):
-    size = lax.axis_size("mem")
-    route = [(i - distance, i) for i in range(size) if 0 <= i - distance < size]
+def swap_regions(block, start):
+    route = []
+    for region in range(start, CHIPS - 1, 2):
+        for half in range(2):
+            one, two = 2 * chip_of(region) + half, 2 * chip_of(region + 1) + half
+            route += [(one, two), (two, one)]
     return lax.ppermute(block, "mem", route)
 
 
@@ -495,22 +510,31 @@
     row = lax.axis_index("mem")
     column = lax.axis_index("tile")
     half = row % 2
+    line, place = row // 2 // CHIP_LINE, row // 2 % CHIP_LINE
+    region = line * CHIP_LINE + jnp.where(line % 2 == 1, CHIP_LINE - 1 - place, place)
     place = jnp.stack(
-        [row * SPAN_NORTH, column * SPAN_EAST, half, (row // 2) * ROWS, column * SPAN_EAST + half * HALF]
+        [
+            row * SPAN_NORTH,
+            column * SPAN_EAST,
+            half,
+            region * ROWS,
+            column * SPAN_EAST + half * HALF,
+            region % 2,
+        ]
     ).astype(jnp.int32)
     message = pack(members[0])
     field = lax.all_to_all(message, "mem", split_axis=0, concat_axis=0, tiled=True)
     facts = state_facts(place, datum, noise, point, count.reshape(2))
-    packet = pick(place, field, facts, swap_cores(facts))
+    packet = pick(place, field, to_region(facts, 0), to_region(facts, 1))
     field, packet = lax.optimization_barrier((field, packet))
     other = swap_cores(packet)
     west, packet = lax.optimization_barrier((arrange(field, 0), packet))
     here = merge(packet, other, swap_beyond(packet))
     field, here = lax.optimization_barrier((field, here))
-    north = from_behind(here, 2)
+    first = swap_regions(here, 0)
     east, here = lax.optimization_barrier((arrange(field, 1), here))
-    south = from_behind(here, -2)
-    message = analyse(place, west, east, north, here, south)
+    second = swap_regions(here, 1)
+    message = analyse(place, west, east, first, here, second)
     message = lax.all_to_all(message, "mem", split_axis=0, concat_axis=0, tiled=True)
     return unpack(message)[None]
 

time: 81.7 us -> 80.6 us (0.987)
  waiting for transfers between devices: 20.3 us -> 12.7 us
  starting transfers between devices: 24.1 us -> 28.6 us
  blocking collectives: 26.4 us -> 28.2 us
    all_to_all x1, waiting for transfers between devices: 12.6 us -> 3.49 us  [on_device(): lax.all_to_all(message, 'mem', split_axis=0, concat_axis=0, tiled=True)]
    ppermute x2 -> x4, starting transfers between devices: 5.28 us -> 12.1 us  [the longest x2 6.74 us: to_region(): return lax.ppermute(block, 'mem', route)]
    ppermute x2 -> x4, waiting for transfers between devices: 5.05 us -> 7.41 us  [the longest x2 5.6 us: to_region(): return lax.ppermute(block, 'mem', route)]
    ppermute x2 -> x1, starting transfers between devices: 4.19 us -> 1.92 us  [swap_cores(): lax.ppermute(block, 'mem', [(i, i ^ 1) for i in range(lax.axis_size('mem'...]
    all_to_all x1, blocking collectives: 26.4 us -> 28.2 us  [on_device(): lax.all_to_all(message, 'mem', split_axis=0, concat_axis=0, tiled=True)]
  transfers between devices with their start and end apart: 6 -> 7, of which waited for: 4 -> 4; matrix products, arithmetic and copies ran while one was open for 0% -> 0% of each run, Pallas kernels for 1% -> 1%
where the time goes in v4:
time: 80.6 us; the launch traced here: 80.2 us
  starting transfers between devices  28.6 us (35%)
  blocking collectives  28.2 us (35%)
  waiting for transfers between devices  12.7 us (16%)
  Pallas kernels  8.57 us (11%)
  local copies, waits for them, and re-layouts  1.82 us (2%)
    all_to_all x1, blocking collectives, on_device(): lax.all_to_all(message, 'mem', split_axis=0, concat_axis=0, tiled=True)  28.2 us
    all_to_all x1, starting transfers between devices, on_device(): lax.all_to_all(message, 'mem', split_axis=0, concat_axis=0, tiled=True)  11.1 us
    pallas_call x7, Pallas kernels, call(): pl.pallas_call(kernel, out_shape=jax.ShapeDtypeStruct(shape, BF16), in_sp...  7.94 us
    ppermute x2, starting transfers between devices, to_region(): return lax.ppermute(block, 'mem', route)  6.74 us
    ppermute x2, waiting for transfers between devices, to_region(): return lax.ppermute(block, 'mem', route)  5.6 us
    ppermute x2, starting transfers between devices, swap_regions(): return lax.ppermute(block, 'mem', route)  5.37 us
    all_to_all x1, waiting for transfers between devices, on_device(): lax.all_to_all(message, 'mem', split_axis=0, concat_axis=0, tiled=True)  3.49 us
    ppermute x1, starting transfers between devices, swap_beyond(): return lax.ppermute(block, ('mem', 'tile'), route)  3.48 us
  transfers between devices with their start and end apart: 7, of which 4 were waited for; matrix products, arithmetic and copies ran while one was open for 0% of the time, Pallas kernels for 1%

profile of v4, /device:TPU:263, one launch (start us, length us, event | category | flops | bytes accessed | tf_op | source)
XLA Modules:
  0.0 80.2 jit_solution(8806947573447371492)
XLA Ops:
  0.0 0.0 copy-start
  0.0 1.0 %copy-done = bf16[1,2,256,512]{3,2,1,0:T(8,128)(2,1)S(1)} copy-done((bf16[1,2,256,512]{3,2,1,0:T(8,128)(2,1)S(1)}, bf16[1,2,256,512]{3,2,1,0:T(8,128)(2,1)}, u32[]{:S(2)}) %copy-start) | copy-done | bytes 524312
  1.0 0.8 %shard_map.55 = bf16[1024,256]{1,0:T(8,128)(2,1)} custom-call(bf16[2,256,512]{2,1,0:T(8,128)(2,1)S(1)} %bitcast.17), custom_call_target="tpu_custom_call" | custom-call | bytes 1048576 | tf_op jit(solution)/shard_map/pallas_call | solution.py:418
  1.9 11.1 %all-to-all-start = ((bf16[64,16,256]{2,1,0:T(8,128)(2,1)}), bf16[64,16,256]{2,1,0:T(8,128)(2,1)S(1)}, u32[]{:S(2)}, u32[]{:S(2)}) async-start(bf16[64,16,256]{2,1,0:T(8,128)(2,1)} %bitcast.7), calls=%async_computation | async-start | bytes 1048576 | tf_op jit(solution)/shard_map/all_to_all | solution.py:526
  13.1 0.0 copy-start.2
  13.1 0.0 copy-start.3
  13.1 0.1 stack.27.place_ref
  13.2 0.0 copy-start.1
  13.2 0.0 copy-start.4
  13.2 0.6 copy-done.2
  13.8 0.0 copy-done.3
  13.8 0.1 copy-done.1
  13.9 0.0 copy-done.4
  13.9 0.6 shard_map.56
  14.5 4.6 %collective-permute-start.1 = (bf16[16,128]{1,0:T(8,128)(2,1)S(1)}, bf16[16,128]{1,0:T(8,128)(2,1)S(1)}, u32[]{:S(2)}, u32[]{:S(2)}) collective-permute-start(bf16[16,128]{1,0:T(8,128)(2,1)S(1)} %shard_map.56), channel_id=1, source_target_pairs={{0,8},{8,0},{16,24},{24,16},{32,40},{40,32},{48,56},{56,48},{64,72... | collective-permute-start | bytes 12296 | tf_op jit(solution)/shard_map/ppermute | solution.py:487
  19.2 2.1 %collective-permute-start = (bf16[16,128]{1,0:T(8,128)(2,1)S(1)}, bf16[16,128]{1,0:T(8,128)(2,1)S(1)}, u32[]{:S(2)}, u32[]{:S(2)}) collective-permute-start(bf16[16,128]{1,0:T(8,128)(2,1)S(1)} %shard_map.56), channel_id=1, source_target_pairs={{0,0},{8,8},{16,16},{24,24},{32,32},{40,40},{48,48},{56,56},{64,64... | collective-permute-start | bytes 12296 | tf_op jit(solution)/shard_map/ppermute | solution.py:487
  21.3 5.6 %collective-permute-done.1.other_ref = bf16[16,128]{1,0:T(8,128)(2,1)S(1)} collective-permute-done((bf16[16,128]{1,0:T(8,128)(2,1)S(1)}, bf16[16,128]{1,0:T(8,128)(2,1)S(1)}, u32[]{:S(2)}, u32[]{:S(2)}) %collective-permute-start.1) | collective-permute-done | bytes 4128 | tf_op jit(solution)/shard_map/ppermute | solution.py:487
  26.9 0.0 collective-permute-done.own_ref
  26.9 3.5 %all-to-all-done = bf16[64,16,256]{2,1,0:T(8,128)(2,1)S(1)} async-done(((bf16[64,16,256]{2,1,0:T(8,128)(2,1)}), bf16[64,16,256]{2,1,0:T(8,128)(2,1)S(1)}, u32[]{:S(2)}, u32[]{:S(2)}) %all-to-all-start) | async-done | bytes 524320 | tf_op jit(solution)/shard_map/all_to_all | solution.py:526
  30.3 1.2 %shard_map.57.own_ref = bf16[80,256]{1,0:T(8,128)(2,1)S(1)} custom-call(s32[6]{0:T(128)S(1)} %stack.27.place_ref, bf16[1024,256]{1,0:T(8,128)(2,1)S(1)} %bitcast.13, bf16[16,128]{1,0:T(8,128)(2,1)S(1)} %collective-permute-done.own_ref, bf16[16,128]{1,0:T(8,128)(2,1)S(1)} %collective-permute-done.1.other_ref), custom_call_target="tpu_custom_call" | custom-call | flops 134217728 | bytes 524288 | tf_op jit(solution)/shard_map/pallas_call | solution.py:418
  31.6 1.9 %collective-permute-start.2 = (bf16[80,256]{1,0:T(8,128)(2,1)S(1)}, bf16[80,256]{1,0:T(8,128)(2,1)S(1)}, u32[]{:S(2)}, u32[]{:S(2)}) collective-permute-start(bf16[80,256]{1,0:T(8,128)(2,1)S(1)} %shard_map.57.own_ref), channel_id=1, source_target_pairs={{0,8},{8,0},{16,24},{24,16},{32,40},{40,32},{48,56},{56,48},{64,72... | collective-permute-start | bytes 122888 | tf_op jit(solution)/shard_map/ppermute | solution.py:482
  33.5 0.2 shard_map.58.west_ref
  33.7 3.5 %collective-permute-start.3 = (bf16[80,256]{1,0:T(8,128)(2,1)S(1)}, bf16[80,256]{1,0:T(8,128)(2,1)S(1)}, u32[]{:S(2)}, u32[]{:S(2)}) collective-permute-start(bf16[80,256]{1,0:T(8,128)(2,1)S(1)} %shard_map.57.own_ref), channel_id=1, source_target_pairs={{8,1},{1,8},{9,2},{2,9},{10,3},{3,10},{11,4},{4,11},{12,5},{5,12},... | collective-permute-start | bytes 122888 | tf_op jit(solution)/shard_map/ppermute | solution.py:497
  37.2 0.0 collective-permute-done.2.other_ref
  37.2 1.8 %collective-permute-done.3.beyond_ref = bf16[80,256]{1,0:T(8,128)(2,1)S(1)} collective-permute-done((bf16[80,256]{1,0:T(8,128)(2,1)S(1)}, bf16[80,256]{1,0:T(8,128)(2,1)S(1)}, u32[]{:S(2)}, u32[]{:S(2)}) %collective-permute-start.3) | collective-permute-done | bytes 40992 | tf_op jit(solution)/shard_map/ppermute | solution.py:497
  39.0 0.1 shard_map.59.here_ref
  39.1 0.2 shard_map.60.east_ref
  39.3 0.7 collective-permute-start.5
  40.0 4.7 %collective-permute-start.4 = (bf16[80,512]{1,0:T(8,128)(2,1)S(1)}, bf16[80,512]{1,0:T(8,128)(2,1)S(1)}, u32[]{:S(2)}, u32[]{:S(2)}) collective-permute-start(bf16[80,512]{1,0:T(8,128)(2,1)S(1)} %shard_map.59.here_ref), channel_id=1, source_target_pairs={{0,16},{16,0},{8,24},{24,8},{32,48},{48,32},{40,56},{56,40},{64,80... | collective-permute-start | bytes 245768 | tf_op jit(solution)/shard_map/ppermute | solution.py:506
  44.7 0.0 collective-permute-done.5.last_ref
  44.7 1.8 %collective-permute-done.4.next_ref = bf16[80,512]{1,0:T(8,128)(2,1)S(1)} collective-permute-done((bf16[80,512]{1,0:T(8,128)(2,1)S(1)}, bf16[80,512]{1,0:T(8,128)(2,1)S(1)}, u32[]{:S(2)}, u32[]{:S(2)}) %collective-permute-start.4) | collective-permute-done | bytes 81952 | tf_op jit(solution)/shard_map/ppermute | solution.py:506
  46.6 4.5 %shard_map.61 = bf16[1024,256]{1,0:T(8,128)(2,1)S(1)} custom-call(s32[6]{0:T(128)S(1)} %stack.27.place_ref, bf16[64,2048]{1,0:T(8,128)(2,1)S(1)} %shard_map.58.west_ref, bf16[64,2048]{1,0:T(8,128)(2,1)S(1)} %shard_map.60.east_ref, bf16[80,512]{1,0:T(8,128)(2,1)S(1)} %collective-permute-done.4.next_ref, bf16[80,512]{1,0:T(8,128)(2,1)S(1)} %shard_map.59.here_ref, ...), custom_call_target="tpu_custom_call" | custom-call | flops 1073741824 | bytes 1048576 | tf_op jit(solution)/shard_map/pallas_call | solution.py:418
  51.1 28.2 %all_to_all.22 = bf16[64,16,256]{2,1,0:T(8,128)(2,1)S(1)} all-to-all(bf16[64,16,256]{2,1,0:T(8,128)(2,1)S(1)} %bitcast.18), channel_id=1, replica_groups=mesh['mem'=64,'tile'=8] {'mem'}, dimensions={0} | all-to-all | bytes 1048576 | tf_op jit(solution)/shard_map/all_to_all | solution.py:538
  79.4 0.8 %shard_map.62 = bf16[2,256,512]{2,1,0:T(8,128)(2,1)} custom-call(bf16[1024,256]{1,0:T(8,128)(2,1)S(1)} %bitcast.16), custom_call_target="tpu_custom_call" | custom-call | bytes 1048576 | tf_op jit(solution)/shard_map/pallas_call | solution.py:418
Async XLA Ops:
  0.0 1.0 %copy-start = (bf16[1,2,256,512]{3,2,1,0:T(8,128)(2,1)S(1)}, bf16[1,2,256,512]{3,2,1,0:T(8,128)(2,1)}, u32[]{:S(2)}) copy-start(bf16[1,2,256,512]{3,2,1,0:T(8,128)(2,1)} %param.5) | copy-start | bytes 1572868
  1.9 28.5 %all-to-all-start = ((bf16[64,16,256]{2,1,0:T(8,128)(2,1)}), bf16[64,16,256]{2,1,0:T(8,128)(2,1)S(1)}, u32[]{:S(2)}, u32[]{:S(2)}) async-start(bf16[64,16,256]{2,1,0:T(8,128)(2,1)} %bitcast.7), calls=%async_computation | async-start | bytes 1048576 | tf_op jit(solution)/shard_map/all_to_all | solution.py:526
  13.1 0.7 copy-start.2
  13.1 0.7 copy-start.3
  13.2 0.7 copy-start.1
  13.2 0.7 copy-start.4
  14.5 12.4 %collective-permute-start.1 = (bf16[16,128]{1,0:T(8,128)(2,1)S(1)}, bf16[16,128]{1,0:T(8,128)(2,1)S(1)}, u32[]{:S(2)}, u32[]{:S(2)}) collective-permute-start(bf16[16,128]{1,0:T(8,128)(2,1)S(1)} %shard_map.56), channel_id=1, source_target_pairs={{0,8},{8,0},{16,24},{24,16},{32,40},{40,32},{48,56},{56,48},{64,72... | collective-permute-start | bytes 12296 | tf_op jit(solution)/shard_map/ppermute | solution.py:487
  19.2 7.7 %collective-permute-start = (bf16[16,128]{1,0:T(8,128)(2,1)S(1)}, bf16[16,128]{1,0:T(8,128)(2,1)S(1)}, u32[]{:S(2)}, u32[]{:S(2)}) collective-permute-start(bf16[16,128]{1,0:T(8,128)(2,1)S(1)} %shard_map.56), channel_id=1, source_target_pairs={{0,0},{8,8},{16,16},{24,24},{32,32},{40,40},{48,48},{56,56},{64,64... | collective-permute-start | bytes 12296 | tf_op jit(solution)/shard_map/ppermute | solution.py:487
  31.6 5.6 %collective-permute-start.2 = (bf16[80,256]{1,0:T(8,128)(2,1)S(1)}, bf16[80,256]{1,0:T(8,128)(2,1)S(1)}, u32[]{:S(2)}, u32[]{:S(2)}) collective-permute-start(bf16[80,256]{1,0:T(8,128)(2,1)S(1)} %shard_map.57.own_ref), channel_id=1, source_target_pairs={{0,8},{8,0},{16,24},{24,16},{32,40},{40,32},{48,56},{56,48},{64,72... | collective-permute-start | bytes 122888 | tf_op jit(solution)/shard_map/ppermute | solution.py:482
  33.7 5.3 %collective-permute-start.3 = (bf16[80,256]{1,0:T(8,128)(2,1)S(1)}, bf16[80,256]{1,0:T(8,128)(2,1)S(1)}, u32[]{:S(2)}, u32[]{:S(2)}) collective-permute-start(bf16[80,256]{1,0:T(8,128)(2,1)S(1)} %shard_map.57.own_ref), channel_id=1, source_target_pairs={{8,1},{1,8},{9,2},{2,9},{10,3},{3,10},{11,4},{4,11},{12,5},{5,12},... | collective-permute-start | bytes 122888 | tf_op jit(solution)/shard_map/ppermute | solution.py:497
  39.3 5.4 %collective-permute-start.5 = (bf16[80,512]{1,0:T(8,128)(2,1)S(1)}, bf16[80,512]{1,0:T(8,128)(2,1)S(1)}, u32[]{:S(2)}, u32[]{:S(2)}) collective-permute-start(bf16[80,512]{1,0:T(8,128)(2,1)S(1)} %shard_map.59.here_ref), channel_id=1, source_target_pairs={{16,32},{32,16},{24,40},{40,24},{48,64},{64,48},{56,72},{72,56},{8... | collective-permute-start | bytes 245768 | tf_op jit(solution)/shard_map/ppermute | solution.py:506
  40.0 6.5 %collective-permute-start.4 = (bf16[80,512]{1,0:T(8,128)(2,1)S(1)}, bf16[80,512]{1,0:T(8,128)(2,1)S(1)}, u32[]{:S(2)}, u32[]{:S(2)}) collective-permute-start(bf16[80,512]{1,0:T(8,128)(2,1)S(1)} %shard_map.59.here_ref), channel_id=1, source_target_pairs={{0,16},{16,0},{8,24},{24,8},{32,48},{48,32},{40,56},{56,40},{64,80... | collective-permute-start | bytes 245768 | tf_op jit(solution)/shard_map/ppermute | solution.py:506

commit v5 on v3

--- a/solution.py
+++ b/solution.py
@@ -1,5 +1,3 @@
-import functools
-
 import jax
 import jax.numpy as jnp
 from jax import lax
@@ -43,7 +41,7 @@
             rows = slice(chip * ROWS, (chip + 1) * ROWS)
             for half in range(2):
                 lanes = slice(half * HALF, (half + 1) * HALF)
-                place = (2 * (2 * group + chip) + half) * LINES
+                place = (4 * group + 2 * chip + half) * LINES
                 message_ref[pl.ds(place, LINES), :] = jnp.concatenate(
                     [upper[rows, lanes], lower[rows, lanes]], axis=0
                 ).astype(BF16)
@@ -54,7 +52,7 @@
         for half in range(2):
             lanes = pl.ds(half * HALF, HALF)
             first, second = (
-                message_ref[pl.ds((2 * (2 * group + chip) + half) * LINES, LINES), :].astype(F32)
+                message_ref[pl.ds((4 * group + 2 * chip + half) * LINES, LINES), :].astype(F32)
                 for chip in range(2)
             )
             for level in range(LEVELS):
@@ -127,8 +125,9 @@
         packet_ref[pl.ds(MEMBERS, FACTS), lanes] = batches[batch].astype(BF16)
 
 
-def merge_kernel(own_ref, other_ref, beyond_ref, cat_ref):
+def merge_kernel(place_ref, own_ref, other_ref, beyond_ref, here_ref, first_ref, second_ref):
     lane = lax.broadcasted_iota(jnp.int32, (PACKET, 2 * SLOTS), 1)
+    odd = place_ref[5]
     for batch in range(2):
         lanes = pl.ds(batch * 2 * SLOTS, 2 * SLOTS)
         members = pl.ds(0, MEMBERS)
@@ -137,10 +136,18 @@
             axis=0,
         ).astype(F32)
         beyond = beyond_ref[:, lanes].astype(F32)
-        first = jnp.where(lane < SLOTS, here, pltpu.roll(beyond, SLOTS, 1))
-        second = jnp.where(lane < SLOTS, pltpu.roll(here, SLOTS, 1), beyond)
-        cat_ref[:, pl.ds(batch * BATCH_LANES, 2 * SLOTS)] = first.astype(BF16)
-        cat_ref[:, pl.ds(batch * BATCH_LANES + 2 * SLOTS, 2 * SLOTS)] = second.astype(BF16)
+        upper = jnp.where(lane < SLOTS, here, pltpu.roll(beyond, SLOTS, 1))
+        lower = jnp.where(lane < SLOTS, pltpu.roll(here, SLOTS, 1), beyond)
+        start = batch * BATCH_LANES
+        here_ref[:, pl.ds(start, 2 * SLOTS)] = upper.astype(BF16)
+        here_ref[:, pl.ds(start + 2 * SLOTS, 2 * SLOTS)] = lower.astype(BF16)
+        if batch == 0:
+            for ref in (first_ref, second_ref):
+                ref[:, pl.ds(0, 2 * SLOTS)] = upper.astype(BF16)
+                ref[:, pl.ds(2 * SLOTS, 2 * SLOTS)] = lower.astype(BF16)
+        else:
+            first_ref[:, pl.ds(start, 2 * SLOTS)] = jnp.where(odd == 0, lower, upper).astype(BF16)
+            second_ref[:, pl.ds(start, 2 * SLOTS)] = jnp.where(odd == 0, upper, lower).astype(BF16)
 
 
 def weights_of(columns, datum, noise, live):
@@ -259,10 +266,8 @@
 def rows_of(cats, rows, batch):
     parts = []
     for index, cat in enumerate(cats):
-        start, count = batch * BATCH_LANES, BATCH_LANES
-        if batch == 1 and index != 1:
-            start, count = start + (2 * SLOTS if index == 0 else 0), 2 * SLOTS
-        parts.append(cat[rows, pl.ds(start, count)])
+        count = 2 * SLOTS if batch == 1 and index != 1 else BATCH_LANES
+        parts.append(cat[rows, pl.ds(batch * BATCH_LANES, count)])
     return jnp.concatenate(parts, axis=1)
 
 
@@ -287,15 +292,17 @@
     return stack_rows(masks, 8)
 
 
-def arrange_kernel(strip, field_ref, cells_ref, wide):
-    wide[...] = field_ref[:, strip * STRIP : (strip + 1) * STRIP].astype(F32)
-    for line in range(LINES):
-        piece = wide[pl.ds(line, MEMBERS, stride=LINES), :]
-        cells_ref[:, pl.ds(line * STRIP, STRIP)] = piece.astype(BF16)
-
-
-def analysis_kernel(place_ref, west_ref, east_ref, north_ref, here_ref, south_ref, message_ref, *scratch):
-    refs = (place_ref, (west_ref, east_ref), (north_ref, here_ref, south_ref), message_ref, *scratch)
+def arrange_kernel(field_ref, cells_ref, wide):
+    for strip in range(STRIPS):
+        wide[strip] = field_ref[:, strip * STRIP : (strip + 1) * STRIP].astype(F32)
+    for strip in range(STRIPS):
+        for line in range(LINES):
+            piece = wide[strip, pl.ds(line, MEMBERS, stride=LINES), :]
+            cells_ref[strip, :, pl.ds(line * STRIP, STRIP)] = piece.astype(BF16)
+
+
+def analysis_kernel(place_ref, cells_ref, next_ref, here_ref, last_ref, message_ref, *scratch):
+    refs = (place_ref, cells_ref, (next_ref, here_ref, last_ref), message_ref, *scratch)
     more = analysis(False, *refs)
 
     @pl.when(more)
@@ -361,19 +368,20 @@
 
         return one
 
-    def cells_of(strip, lanes):
-        once = cells[strip][:, lanes]
-        return jnp.concatenate([once, once], axis=0)
-
-    for strip in range(STRIPS):
-        for lanes, moved in region_step(records[pieces[strip]], strip, cells_of):
-            state[strip, :, lanes] = cells[strip][:, lanes].astype(F32) + moved
-    if loops:
-        lax.fori_loop(1, chunks, more_cells(ranks, table, cells_of), 0)
-
     pert, mean_weight, pert_weight = weights_of(after, datum_1, noise_1, live_1)
     table_1 = table_of(pert, mean_weight, pert_weight, row_1, col_1, level_1)
     records_1 = chosen_records(ranks_1, [0.0] * STRIPS, sizes, table_1)
+
+    def cells_of(strip, lanes):
+        once = cells[strip, :, lanes]
+        return jnp.concatenate([once, once], axis=0)
+
+    for strip in range(STRIPS):
+        for lanes, moved in region_step(records[pieces[strip]], strip, cells_of):
+            state[strip, :, lanes] = cells[strip, :, lanes].astype(F32) + moved
+    if loops:
+        lax.fori_loop(1, chunks, more_cells(ranks, table, cells_of), 0)
+
 
     def split_cells(strip, lanes):
         high, low = split(state[strip, :, lanes])
@@ -395,13 +403,14 @@
             for line in range(ROWS):
                 place = pl.ds(lanes.start // STRIP + line, MEMBERS, stride=LINES)
                 wide[strip, place, :] = done[:, line * STRIP : (line + 1) * STRIP]
+        if not loops:
+            message_ref[:, strip * STRIP : (strip + 1) * STRIP] = wide[strip].astype(BF16)
     if loops:
         lax.fori_loop(1, chunks_1, more_cells(ranks_1, table_1, source_of), 0)
         for strip in range(STRIPS):
             for line in range(LINES):
                 wide[strip, pl.ds(line, MEMBERS, stride=LINES), :] = state[strip, :, pl.ds(line * STRIP, STRIP)]
-    for part in range(STRIPS):
-        message_ref[:, part * STRIP : (part + 1) * STRIP] = wide[part].astype(BF16)
+            message_ref[:, strip * STRIP : (strip + 1) * STRIP] = wide[strip].astype(BF16)
     return (jnp.maximum(chunks, chunks_1) > 1) | (site_chunks > 1)
 
 
@@ -449,17 +458,26 @@
     )
 
 
-def merge(own, other, beyond):
-    return call(merge_kernel, (PACKET, 2 * BATCH_LANES), (own, other, beyond))
-
-
-def arrange(field, strip):
-    kernel = functools.partial(arrange_kernel, strip)
-    scratch = [pltpu.VMEM((MEMBERS * LINES, STRIP), F32)]
-    return call(kernel, (MEMBERS, LINES * STRIP), (field,), scratch, moved=1 << 19)
-
-
-def analyse(place, west, east, north, here, south):
+def merge(place, own, other, beyond):
+    smem = pl.BlockSpec(memory_space=pltpu.SMEM)
+    vmem = pl.BlockSpec(memory_space=pltpu.VMEM)
+    lanes = (2 * BATCH_LANES, BATCH_LANES + 2 * SLOTS, BATCH_LANES + 2 * SLOTS)
+    return pl.pallas_call(
+        merge_kernel,
+        out_shape=[jax.ShapeDtypeStruct((PACKET, count), BF16) for count in lanes],
+        in_specs=[smem, vmem, vmem, vmem],
+        out_specs=[vmem, vmem, vmem],
+        compiler_params=pltpu.CompilerParams(vmem_limit_bytes=VMEM_LIMIT),
+        cost_estimate=pl.CostEstimate(flops=0, bytes_accessed=1 << 18, transcendentals=0),
+    )(place, own, other, beyond)
+
+
+def arrange(field):
+    scratch = [pltpu.VMEM((STRIPS, MEMBERS * LINES, STRIP), F32)]
+    return call(arrange_kernel, (STRIPS, MEMBERS, LINES * STRIP), (field,), scratch, moved=1 << 20)
+
+
+def analyse(place, cells, first, here, second):
     scratch = [
         pltpu.VMEM((STRIPS, MEMBERS * LINES, STRIP), F32),
         pltpu.VMEM((STRIPS, MEMBERS, LINES * STRIP), F32),
@@ -467,7 +485,7 @@
         pltpu.VMEM((MEMBERS, 2 * BATCH_LANES), F32),
     ]
     return call(
-        analysis_kernel, MESSAGE, (place, west, east, north, here, south), scratch, 1, 1 << 30, 1 << 20
+        analysis_kernel, MESSAGE, (place, cells, first, here, second), scratch, 1, 1 << 30, 1 << 20
     )
 
 
@@ -485,9 +503,12 @@
     return lax.ppermute(block, ("mem", "tile"), route)
 
 
-def from_behind(block, distance):
-    size = lax.axis_size("mem")
-    route = [(i - distance, i) for i in range(size) if 0 <= i - distance < size]
+def swap_regions(block, start):
+    route = []
+    for region in range(start, CHIPS - 1, 2):
+        for half in range(2):
+            one, two = 2 * region + half, 2 * region + 2 + half
+            route += [(one, two), (two, one)]
     return lax.ppermute(block, "mem", route)
 
 
@@ -495,22 +516,28 @@
     row = lax.axis_index("mem")
     column = lax.axis_index("tile")
     half = row % 2
+    region = row // 2
     place = jnp.stack(
-        [row * SPAN_NORTH, column * SPAN_EAST, half, (row // 2) * ROWS, column * SPAN_EAST + half * HALF]
+        [
+            row * SPAN_NORTH,
+            column * SPAN_EAST,
+            half,
+            region * ROWS,
+            column * SPAN_EAST + half * HALF,
+            region % 2,
+        ]
     ).astype(jnp.int32)
     message = pack(members[0])
     field = lax.all_to_all(message, "mem", split_axis=0, concat_axis=0, tiled=True)
     facts = state_facts(place, datum, noise, point, count.reshape(2))
     packet = pick(place, field, facts, swap_cores(facts))
     field, packet = lax.optimization_barrier((field, packet))
+    beyond = swap_beyond(packet)
     other = swap_cores(packet)
-    west, packet = lax.optimization_barrier((arrange(field, 0), packet))
-    here = merge(packet, other, swap_beyond(packet))
-    field, here = lax.optimization_barrier((field, here))
-    north = from_behind(here, 2)
-    east, here = lax.optimization_barrier((arrange(field, 1), here))
-    south = from_behind(here, -2)
-    message = analyse(place, west, east, north, here, south)
+    cells, other, beyond = lax.optimization_barrier((arrange(field), other, beyond))
+    here, first, second = merge(place, packet, other, beyond)
+    first, second = swap_regions(first, 0), swap_regions(second, 1)
+    message = analyse(place, cells, first, here, second)
     message = lax.all_to_all(message, "mem", split_axis=0, concat_axis=0, tiled=True)
     return unpack(message)[None]
 

time: 81.7 us -> 80 us (0.979)
  the two profiles are of different devices: /device:TPU:263 before, /device:TPU:199 now
where the time goes in v5:
time: 80 us; the launch traced here: 79.6 us
  starting transfers between devices  26 us (32%)
  blocking collectives  24.5 us (31%)
  waiting for transfers between devices  18.3 us (23%)
  Pallas kernels  8.89 us (11%)
  local copies, waits for them, and re-layouts  1.82 us (2%)
    all_to_all x1, blocking collectives, on_device(): lax.all_to_all(message, 'mem', split_axis=0, concat_axis=0, tiled=True)  24.5 us
    all_to_all x1, waiting for transfers between devices, on_device(): lax.all_to_all(message, 'mem', split_axis=0, concat_axis=0, tiled=True)  12.6 us
    all_to_all x1, starting transfers between devices, on_device(): lax.all_to_all(message, 'mem', split_axis=0, concat_axis=0, tiled=True)  11.1 us
    pallas_call x5, Pallas kernels, call(): pl.pallas_call(kernel, out_shape=jax.ShapeDtypeStruct(shape, BF16), in_sp...  7.62 us
    ppermute x2, starting transfers between devices, swap_regions(): return lax.ppermute(block, 'mem', route)  5.68 us
    ppermute x1, starting transfers between devices, swap_beyond(): return lax.ppermute(block, ('mem', 'tile'), route)  4.99 us
    ppermute x2, starting transfers between devices, swap_cores(): lax.ppermute(block, 'mem', [(i, i ^ 1) for i in range(lax.axis_size('mem'...  4.19 us
    ppermute x2, waiting for transfers between devices, swap_regions(): return lax.ppermute(block, 'mem', route)  4.08 us
  transfers between devices with their start and end apart: 6, of which 4 were waited for; matrix products, arithmetic and copies ran while one was open for 0% of the time, Pallas kernels for 1%

profile of v5, /device:TPU:199, one launch (start us, length us, event | category | flops | bytes accessed | tf_op | source)
XLA Modules:
  0.0 79.6 jit_solution(12586551219243361473)
XLA Ops:
  0.0 0.0 copy-start
  0.0 1.0 %copy-done = bf16[1,2,256,512]{3,2,1,0:T(8,128)(2,1)S(1)} copy-done((bf16[1,2,256,512]{3,2,1,0:T(8,128)(2,1)S(1)}, bf16[1,2,256,512]{3,2,1,0:T(8,128)(2,1)}, u32[]{:S(2)}) %copy-start) | copy-done | bytes 524312
  1.0 0.8 %shard_map.55 = bf16[1024,256]{1,0:T(8,128)(2,1)} custom-call(bf16[2,256,512]{2,1,0:T(8,128)(2,1)S(1)} %bitcast.16), custom_call_target="tpu_custom_call" | custom-call | bytes 1048576 | tf_op jit(solution)/shard_map/pallas_call | solution.py:420
  1.9 11.1 %all-to-all-start = ((bf16[64,16,256]{2,1,0:T(8,128)(2,1)}), bf16[64,16,256]{2,1,0:T(8,128)(2,1)S(1)}, u32[]{:S(2)}, u32[]{:S(2)}) async-start(bf16[64,16,256]{2,1,0:T(8,128)(2,1)} %bitcast.7), calls=%async_computation | async-start | bytes 1048576 | tf_op jit(solution)/shard_map/all_to_all | solution.py:531
  13.0 0.0 copy-start.2
  13.0 0.0 copy-start.3
  13.1 0.1 stack.27.place_ref
  13.1 0.0 copy-start.1
  13.1 0.0 copy-start.4
  13.1 0.6 copy-done.2
  13.7 0.0 copy-done.3
  13.7 0.1 copy-done.1
  13.8 0.0 copy-done.4
  13.8 0.6 shard_map.56.own_ref
  14.5 2.3 %collective-permute-start = (bf16[16,128]{1,0:T(8,128)(2,1)S(1)}, bf16[16,128]{1,0:T(8,128)(2,1)S(1)}, u32[]{:S(2)}, u32[]{:S(2)}) collective-permute-start(bf16[16,128]{1,0:T(8,128)(2,1)S(1)} %shard_map.56.own_ref), channel_id=1, source_target_pairs={{0,8},{8,0},{16,24},{24,16},{32,40},{40,32},{48,56},{56,48},{64,72... | collective-permute-start | bytes 12296 | tf_op jit(solution)/shard_map/ppermute | solution.py:493
  16.7 0.8 %collective-permute-done.other_ref = bf16[16,128]{1,0:T(8,128)(2,1)S(1)} collective-permute-done((bf16[16,128]{1,0:T(8,128)(2,1)S(1)}, bf16[16,128]{1,0:T(8,128)(2,1)S(1)}, u32[]{:S(2)}, u32[]{:S(2)}) %collective-permute-start) | collective-permute-done | bytes 4128 | tf_op jit(solution)/shard_map/ppermute | solution.py:493
  17.5 12.6 %all-to-all-done = bf16[64,16,256]{2,1,0:T(8,128)(2,1)S(1)} async-done(((bf16[64,16,256]{2,1,0:T(8,128)(2,1)}), bf16[64,16,256]{2,1,0:T(8,128)(2,1)S(1)}, u32[]{:S(2)}, u32[]{:S(2)}) %all-to-all-start) | async-done | bytes 524320 | tf_op jit(solution)/shard_map/all_to_all | solution.py:531
  30.2 1.2 %shard_map.57.own_ref = bf16[80,256]{1,0:T(8,128)(2,1)S(1)} custom-call(s32[6]{0:T(128)S(1)} %stack.27.place_ref, bf16[1024,256]{1,0:T(8,128)(2,1)S(1)} %bitcast.13, bf16[16,128]{1,0:T(8,128)(2,1)S(1)} %shard_map.56.own_ref, bf16[16,128]{1,0:T(8,128)(2,1)S(1)} %collective-permute-done.other_ref), custom_call_target="tpu_custom_call" | custom-call | flops 134217728 | bytes 524288 | tf_op jit(solution)/shard_map/pallas_call | solution.py:420
  31.4 5.0 %collective-permute-start.2 = (bf16[80,256]{1,0:T(8,128)(2,1)S(1)}, bf16[80,256]{1,0:T(8,128)(2,1)S(1)}, u32[]{:S(2)}, u32[]{:S(2)}) collective-permute-start(bf16[80,256]{1,0:T(8,128)(2,1)S(1)} %shard_map.57.own_ref), channel_id=1, source_target_pairs={{8,1},{1,8},{9,2},{2,9},{10,3},{3,10},{11,4},{4,11},{12,5},{5,12},... | collective-permute-start | bytes 122888 | tf_op jit(solution)/shard_map/ppermute | solution.py:503
  36.4 1.9 %collective-permute-start.1 = (bf16[80,256]{1,0:T(8,128)(2,1)S(1)}, bf16[80,256]{1,0:T(8,128)(2,1)S(1)}, u32[]{:S(2)}, u32[]{:S(2)}) collective-permute-start(bf16[80,256]{1,0:T(8,128)(2,1)S(1)} %shard_map.57.own_ref), channel_id=1, source_target_pairs={{0,8},{8,0},{16,24},{24,16},{32,40},{40,32},{48,56},{56,48},{64,72... | collective-permute-start | bytes 122888 | tf_op jit(solution)/shard_map/ppermute | solution.py:493
  38.3 0.4 shard_map.58.cells_ref
  38.7 0.0 collective-permute-done.2.beyond_ref
  38.7 0.8 collective-permute-done.1.other_ref
  39.5 0.6 shard_map.59
  40.2 2.7 %collective-permute-start.3 = (bf16[80,384]{1,0:T(8,128)(2,1)S(1)}, bf16[80,384]{1,0:T(8,128)(2,1)S(1)}, u32[]{:S(2)}, u32[]{:S(2)}) collective-permute-start(bf16[80,384]{1,0:T(8,128)(2,1)S(1)} %get-tuple-element.18), channel_id=1, source_target_pairs={{0,16},{16,0},{8,24},{24,8},{32,48},{48,32},{40,56},{56,40},{64,80... | collective-permute-start | bytes 184328 | tf_op jit(solution)/shard_map/ppermute | solution.py:512
  42.9 3.0 %collective-permute-start.4 = (bf16[80,384]{1,0:T(8,128)(2,1)S(1)}, bf16[80,384]{1,0:T(8,128)(2,1)S(1)}, u32[]{:S(2)}, u32[]{:S(2)}) collective-permute-start(bf16[80,384]{1,0:T(8,128)(2,1)S(1)} %get-tuple-element.20), channel_id=1, source_target_pairs={{16,32},{32,16},{24,40},{40,24},{48,64},{64,48},{56,72},{72,56},{8... | collective-permute-start | bytes 184328 | tf_op jit(solution)/shard_map/ppermute | solution.py:512
  45.8 0.0 collective-permute-done.3.next_ref
  45.9 4.1 %collective-permute-done.4.last_ref = bf16[80,384]{1,0:T(8,128)(2,1)S(1)} collective-permute-done((bf16[80,384]{1,0:T(8,128)(2,1)S(1)}, bf16[80,384]{1,0:T(8,128)(2,1)S(1)}, u32[]{:S(2)}, u32[]{:S(2)}) %collective-permute-start.4) | collective-permute-done | bytes 61472 | tf_op jit(solution)/shard_map/ppermute | solution.py:512
  49.9 4.3 %shard_map.60 = bf16[1024,256]{1,0:T(8,128)(2,1)S(1)} custom-call(s32[6]{0:T(128)S(1)} %stack.27.place_ref, bf16[2,64,2048]{2,1,0:T(8,128)(2,1)S(1)} %shard_map.58.cells_ref, bf16[80,384]{1,0:T(8,128)(2,1)S(1)} %collective-permute-done.3.next_ref, bf16[80,512]{1,0:T(8,128)(2,1)S(1)} %get-tuple-element.19.here_ref, ...), custom_call_target="tpu_custom_call" | custom-call | flops 1073741824 | bytes 1048576 | tf_op jit(solution)/shard_map/pallas_call | solution.py:420
  54.3 24.5 %all_to_all.22 = bf16[64,16,256]{2,1,0:T(8,128)(2,1)S(1)} all-to-all(bf16[64,16,256]{2,1,0:T(8,128)(2,1)S(1)} %bitcast.17), channel_id=1, replica_groups=mesh['mem'=64,'tile'=8] {'mem'}, dimensions={0} | all-to-all | bytes 1048576 | tf_op jit(solution)/shard_map/all_to_all | solution.py:541
  78.8 0.8 %shard_map.61 = bf16[2,256,512]{2,1,0:T(8,128)(2,1)} custom-call(bf16[1024,256]{1,0:T(8,128)(2,1)S(1)} %bitcast.15), custom_call_target="tpu_custom_call" | custom-call | bytes 1048576 | tf_op jit(solution)/shard_map/pallas_call | solution.py:420
Async XLA Ops:
  0.0 1.0 %copy-start = (bf16[1,2,256,512]{3,2,1,0:T(8,128)(2,1)S(1)}, bf16[1,2,256,512]{3,2,1,0:T(8,128)(2,1)}, u32[]{:S(2)}) copy-start(bf16[1,2,256,512]{3,2,1,0:T(8,128)(2,1)} %param.5) | copy-start | bytes 1572868
  1.9 28.3 %all-to-all-start = ((bf16[64,16,256]{2,1,0:T(8,128)(2,1)}), bf16[64,16,256]{2,1,0:T(8,128)(2,1)S(1)}, u32[]{:S(2)}, u32[]{:S(2)}) async-start(bf16[64,16,256]{2,1,0:T(8,128)(2,1)} %bitcast.7), calls=%async_computation | async-start | bytes 1048576 | tf_op jit(solution)/shard_map/all_to_all | solution.py:531
  13.0 0.7 copy-start.2
  13.0 0.7 copy-start.3
  13.1 0.7 copy-start.1
  13.1 0.7 copy-start.4
  14.5 3.1 %collective-permute-start = (bf16[16,128]{1,0:T(8,128)(2,1)S(1)}, bf16[16,128]{1,0:T(8,128)(2,1)S(1)}, u32[]{:S(2)}, u32[]{:S(2)}) collective-permute-start(bf16[16,128]{1,0:T(8,128)(2,1)S(1)} %shard_map.56.own_ref), channel_id=1, source_target_pairs={{0,8},{8,0},{16,24},{24,16},{32,40},{40,32},{48,56},{56,48},{64,72... | collective-permute-start | bytes 12296 | tf_op jit(solution)/shard_map/ppermute | solution.py:493
  31.4 7.3 %collective-permute-start.2 = (bf16[80,256]{1,0:T(8,128)(2,1)S(1)}, bf16[80,256]{1,0:T(8,128)(2,1)S(1)}, u32[]{:S(2)}, u32[]{:S(2)}) collective-permute-start(bf16[80,256]{1,0:T(8,128)(2,1)S(1)} %shard_map.57.own_ref), channel_id=1, source_target_pairs={{8,1},{1,8},{9,2},{2,9},{10,3},{3,10},{11,4},{4,11},{12,5},{5,12},... | collective-permute-start | bytes 122888 | tf_op jit(solution)/shard_map/ppermute | solution.py:503
  36.4 3.1 %collective-permute-start.1 = (bf16[80,256]{1,0:T(8,128)(2,1)S(1)}, bf16[80,256]{1,0:T(8,128)(2,1)S(1)}, u32[]{:S(2)}, u32[]{:S(2)}) collective-permute-start(bf16[80,256]{1,0:T(8,128)(2,1)S(1)} %shard_map.57.own_ref), channel_id=1, source_target_pairs={{0,8},{8,0},{16,24},{24,16},{32,40},{40,32},{48,56},{56,48},{64,72... | collective-permute-start | bytes 122888 | tf_op jit(solution)/shard_map/ppermute | solution.py:493
  40.2 5.7 %collective-permute-start.3 = (bf16[80,384]{1,0:T(8,128)(2,1)S(1)}, bf16[80,384]{1,0:T(8,128)(2,1)S(1)}, u32[]{:S(2)}, u32[]{:S(2)}) collective-permute-start(bf16[80,384]{1,0:T(8,128)(2,1)S(1)} %get-tuple-element.18), channel_id=1, source_target_pairs={{0,16},{16,0},{8,24},{24,8},{32,48},{48,32},{40,56},{56,40},{64,80... | collective-permute-start | bytes 184328 | tf_op jit(solution)/shard_map/ppermute | solution.py:512
  42.9 7.1 %collective-permute-start.4 = (bf16[80,384]{1,0:T(8,128)(2,1)S(1)}, bf16[80,384]{1,0:T(8,128)(2,1)S(1)}, u32[]{:S(2)}, u32[]{:S(2)}) collective-permute-start(bf16[80,384]{1,0:T(8,128)(2,1)S(1)} %get-tuple-element.20), channel_id=1, source_target_pairs={{16,32},{32,16},{24,40},{40,24},{48,64},{64,48},{56,72},{72,56},{8... | collective-permute-start | bytes 184328 | tf_op jit(solution)/shard_map/ppermute | solution.py:512

commit v6 on v5

--- a/solution.py
+++ b/solution.py
@@ -18,7 +18,7 @@
 STRIPS = HALF // STRIP
 REACH = 8
 CHUNK = 64
-SITE_CHUNK = 160
+SITE_CHUNK = 192
 FACTS = 16
 PACKET = MEMBERS + FACTS
 BATCH_LANES = 4 * SLOTS

time: 80 us -> 81.5 us (1.019)
  the two profiles are of different devices: /device:TPU:199 before, /device:TPU:71 now
where the time goes in v6:
time: 81.5 us; the launch traced here: 82.5 us
  blocking collectives  28.6 us (35%)
  starting transfers between devices  24.8 us (30%)
  waiting for transfers between devices  18.3 us (22%)
  Pallas kernels  8.87 us (11%)
  local copies, waits for them, and re-layouts  1.82 us (2%)
    all_to_all x1, blocking collectives, on_device(): lax.all_to_all(message, 'mem', split_axis=0, concat_axis=0, tiled=True)  28.6 us
    all_to_all x1, waiting for transfers between devices, on_device(): lax.all_to_all(message, 'mem', split_axis=0, concat_axis=0, tiled=True)  12.6 us
    all_to_all x1, starting transfers between devices, on_device(): lax.all_to_all(message, 'mem', split_axis=0, concat_axis=0, tiled=True)  11.1 us
    pallas_call x5, Pallas kernels, call(): pl.pallas_call(kernel, out_shape=jax.ShapeDtypeStruct(shape, BF16), in_sp...  7.6 us
    ppermute x2, starting transfers between devices, swap_regions(): return lax.ppermute(block, 'mem', route)  5.66 us
    ppermute x2, starting transfers between devices, swap_cores(): lax.ppermute(block, 'mem', [(i, i ^ 1) for i in range(lax.axis_size('mem'...  4.19 us
    ppermute x2, waiting for transfers between devices, swap_regions(): return lax.ppermute(block, 'mem', route)  4.09 us
    ppermute x1, starting transfers between devices, swap_beyond(): return lax.ppermute(block, ('mem', 'tile'), route)  3.78 us
  transfers between devices with their start and end apart: 6, of which 4 were waited for; matrix products, arithmetic and copies ran while one was open for 0% of the time, Pallas kernels for 1%

profile of v6, /device:TPU:71, one launch (start us, length us, event | category | flops | bytes accessed | tf_op | source)
XLA Modules:
  0.0 82.5 jit_solution(7966042497358977375)
XLA Ops:
  0.0 0.0 copy-start
  0.0 1.0 %copy-done = bf16[1,2,256,512]{3,2,1,0:T(8,128)(2,1)S(1)} copy-done((bf16[1,2,256,512]{3,2,1,0:T(8,128)(2,1)S(1)}, bf16[1,2,256,512]{3,2,1,0:T(8,128)(2,1)}, u32[]{:S(2)}) %copy-start) | copy-done | bytes 524312
  1.0 0.8 %shard_map.55 = bf16[1024,256]{1,0:T(8,128)(2,1)} custom-call(bf16[2,256,512]{2,1,0:T(8,128)(2,1)S(1)} %bitcast.16), custom_call_target="tpu_custom_call" | custom-call | bytes 1048576 | tf_op jit(solution)/shard_map/pallas_call | solution.py:420
  1.9 11.1 %all-to-all-start = ((bf16[64,16,256]{2,1,0:T(8,128)(2,1)}), bf16[64,16,256]{2,1,0:T(8,128)(2,1)S(1)}, u32[]{:S(2)}, u32[]{:S(2)}) async-start(bf16[64,16,256]{2,1,0:T(8,128)(2,1)} %bitcast.7), calls=%async_computation | async-start | bytes 1048576 | tf_op jit(solution)/shard_map/all_to_all | solution.py:531
  13.0 0.0 copy-start.2
  13.0 0.0 copy-start.3
  13.1 0.1 stack.27.place_ref
  13.1 0.0 copy-start.1
  13.1 0.0 copy-start.4
  13.1 0.6 copy-done.2
  13.7 0.0 copy-done.3
  13.7 0.1 copy-done.1
  13.8 0.0 copy-done.4
  13.8 0.6 shard_map.56.own_ref
  14.5 2.3 %collective-permute-start = (bf16[16,128]{1,0:T(8,128)(2,1)S(1)}, bf16[16,128]{1,0:T(8,128)(2,1)S(1)}, u32[]{:S(2)}, u32[]{:S(2)}) collective-permute-start(bf16[16,128]{1,0:T(8,128)(2,1)S(1)} %shard_map.56.own_ref), channel_id=1, source_target_pairs={{0,8},{8,0},{16,24},{24,16},{32,40},{40,32},{48,56},{56,48},{64,72... | collective-permute-start | bytes 12296 | tf_op jit(solution)/shard_map/ppermute | solution.py:493
  16.7 0.8 collective-permute-done.other_ref
  17.5 12.6 %all-to-all-done = bf16[64,16,256]{2,1,0:T(8,128)(2,1)S(1)} async-done(((bf16[64,16,256]{2,1,0:T(8,128)(2,1)}), bf16[64,16,256]{2,1,0:T(8,128)(2,1)S(1)}, u32[]{:S(2)}, u32[]{:S(2)}) %all-to-all-start) | async-done | bytes 524320 | tf_op jit(solution)/shard_map/all_to_all | solution.py:531
  30.2 1.2 %shard_map.57.own_ref = bf16[80,256]{1,0:T(8,128)(2,1)S(1)} custom-call(s32[6]{0:T(128)S(1)} %stack.27.place_ref, bf16[1024,256]{1,0:T(8,128)(2,1)S(1)} %bitcast.13, bf16[16,128]{1,0:T(8,128)(2,1)S(1)} %shard_map.56.own_ref, bf16[16,128]{1,0:T(8,128)(2,1)S(1)} %collective-permute-done.other_ref), custom_call_target="tpu_custom_call" | custom-call | flops 134217728 | bytes 524288 | tf_op jit(solution)/shard_map/pallas_call | solution.py:420
  31.4 3.8 %collective-permute-start.2 = (bf16[80,256]{1,0:T(8,128)(2,1)S(1)}, bf16[80,256]{1,0:T(8,128)(2,1)S(1)}, u32[]{:S(2)}, u32[]{:S(2)}) collective-permute-start(bf16[80,256]{1,0:T(8,128)(2,1)S(1)} %shard_map.57.own_ref), channel_id=1, source_target_pairs={{8,1},{1,8},{9,2},{2,9},{10,3},{3,10},{11,4},{4,11},{12,5},{5,12},... | collective-permute-start | bytes 122888 | tf_op jit(solution)/shard_map/ppermute | solution.py:503
  35.2 1.9 %collective-permute-start.1 = (bf16[80,256]{1,0:T(8,128)(2,1)S(1)}, bf16[80,256]{1,0:T(8,128)(2,1)S(1)}, u32[]{:S(2)}, u32[]{:S(2)}) collective-permute-start(bf16[80,256]{1,0:T(8,128)(2,1)S(1)} %shard_map.57.own_ref), channel_id=1, source_target_pairs={{0,8},{8,0},{16,24},{24,16},{32,40},{40,32},{48,56},{56,48},{64,72... | collective-permute-start | bytes 122888 | tf_op jit(solution)/shard_map/ppermute | solution.py:493
  37.1 0.4 shard_map.58.cells_ref
  37.5 0.0 collective-permute-done.2.beyond_ref
  37.5 0.8 collective-permute-done.1.other_ref
  38.3 0.6 shard_map.59
  38.9 2.7 %collective-permute-start.3 = (bf16[80,384]{1,0:T(8,128)(2,1)S(1)}, bf16[80,384]{1,0:T(8,128)(2,1)S(1)}, u32[]{:S(2)}, u32[]{:S(2)}) collective-permute-start(bf16[80,384]{1,0:T(8,128)(2,1)S(1)} %get-tuple-element.18), channel_id=1, source_target_pairs={{0,16},{16,0},{8,24},{24,8},{32,48},{48,32},{40,56},{56,40},{64,80... | collective-permute-start | bytes 184328 | tf_op jit(solution)/shard_map/ppermute | solution.py:512
  41.6 3.0 %collective-permute-start.4 = (bf16[80,384]{1,0:T(8,128)(2,1)S(1)}, bf16[80,384]{1,0:T(8,128)(2,1)S(1)}, u32[]{:S(2)}, u32[]{:S(2)}) collective-permute-start(bf16[80,384]{1,0:T(8,128)(2,1)S(1)} %get-tuple-element.20), channel_id=1, source_target_pairs={{16,32},{32,16},{24,40},{40,24},{48,64},{64,48},{56,72},{72,56},{8... | collective-permute-start | bytes 184328 | tf_op jit(solution)/shard_map/ppermute | solution.py:512
  44.6 0.0 collective-permute-done.3.next_ref
  44.6 4.1 %collective-permute-done.4.last_ref = bf16[80,384]{1,0:T(8,128)(2,1)S(1)} collective-permute-done((bf16[80,384]{1,0:T(8,128)(2,1)S(1)}, bf16[80,384]{1,0:T(8,128)(2,1)S(1)}, u32[]{:S(2)}, u32[]{:S(2)}) %collective-permute-start.4) | collective-permute-done | bytes 61472 | tf_op jit(solution)/shard_map/ppermute | solution.py:512
  48.7 4.3 %shard_map.60 = bf16[1024,256]{1,0:T(8,128)(2,1)S(1)} custom-call(s32[6]{0:T(128)S(1)} %stack.27.place_ref, bf16[2,64,2048]{2,1,0:T(8,128)(2,1)S(1)} %shard_map.58.cells_ref, bf16[80,384]{1,0:T(8,128)(2,1)S(1)} %collective-permute-done.3.next_ref, bf16[80,512]{1,0:T(8,128)(2,1)S(1)} %get-tuple-element.19.here_ref, ...), custom_call_target="tpu_custom_call" | custom-call | flops 1073741824 | bytes 1048576 | tf_op jit(solution)/shard_map/pallas_call | solution.py:420
  53.0 28.6 %all_to_all.22 = bf16[64,16,256]{2,1,0:T(8,128)(2,1)S(1)} all-to-all(bf16[64,16,256]{2,1,0:T(8,128)(2,1)S(1)} %bitcast.17), channel_id=1, replica_groups=mesh['mem'=64,'tile'=8] {'mem'}, dimensions={0} | all-to-all | bytes 1048576 | tf_op jit(solution)/shard_map/all_to_all | solution.py:541
  81.7 0.8 %shard_map.61 = bf16[2,256,512]{2,1,0:T(8,128)(2,1)} custom-call(bf16[1024,256]{1,0:T(8,128)(2,1)S(1)} %bitcast.15), custom_call_target="tpu_custom_call" | custom-call | bytes 1048576 | tf_op jit(solution)/shard_map/pallas_call | solution.py:420
Async XLA Ops:
  0.0 1.0 %copy-start = (bf16[1,2,256,512]{3,2,1,0:T(8,128)(2,1)S(1)}, bf16[1,2,256,512]{3,2,1,0:T(8,128)(2,1)}, u32[]{:S(2)}) copy-start(bf16[1,2,256,512]{3,2,1,0:T(8,128)(2,1)} %param.5) | copy-start | bytes 1572868
  1.9 28.3 %all-to-all-start = ((bf16[64,16,256]{2,1,0:T(8,128)(2,1)}), bf16[64,16,256]{2,1,0:T(8,128)(2,1)S(1)}, u32[]{:S(2)}, u32[]{:S(2)}) async-start(bf16[64,16,256]{2,1,0:T(8,128)(2,1)} %bitcast.7), calls=%async_computation | async-start | bytes 1048576 | tf_op jit(solution)/shard_map/all_to_all | solution.py:531
  13.0 0.7 copy-start.2
  13.0 0.7 copy-start.3
  13.1 0.7 copy-start.1
  13.1 0.7 copy-start.4
  14.5 3.1 %collective-permute-start = (bf16[16,128]{1,0:T(8,128)(2,1)S(1)}, bf16[16,128]{1,0:T(8,128)(2,1)S(1)}, u32[]{:S(2)}, u32[]{:S(2)}) collective-permute-start(bf16[16,128]{1,0:T(8,128)(2,1)S(1)} %shard_map.56.own_ref), channel_id=1, source_target_pairs={{0,8},{8,0},{16,24},{24,16},{32,40},{40,32},{48,56},{56,48},{64,72... | collective-permute-start | bytes 12296 | tf_op jit(solution)/shard_map/ppermute | solution.py:493
  31.4 6.1 %collective-permute-start.2 = (bf16[80,256]{1,0:T(8,128)(2,1)S(1)}, bf16[80,256]{1,0:T(8,128)(2,1)S(1)}, u32[]{:S(2)}, u32[]{:S(2)}) collective-permute-start(bf16[80,256]{1,0:T(8,128)(2,1)S(1)} %shard_map.57.own_ref), channel_id=1, source_target_pairs={{8,1},{1,8},{9,2},{2,9},{10,3},{3,10},{11,4},{4,11},{12,5},{5,12},... | collective-permute-start | bytes 122888 | tf_op jit(solution)/shard_map/ppermute | solution.py:503
  35.2 3.1 %collective-permute-start.1 = (bf16[80,256]{1,0:T(8,128)(2,1)S(1)}, bf16[80,256]{1,0:T(8,128)(2,1)S(1)}, u32[]{:S(2)}, u32[]{:S(2)}) collective-permute-start(bf16[80,256]{1,0:T(8,128)(2,1)S(1)} %shard_map.57.own_ref), channel_id=1, source_target_pairs={{0,8},{8,0},{16,24},{24,16},{32,40},{40,32},{48,56},{56,48},{64,72... | collective-permute-start | bytes 122888 | tf_op jit(solution)/shard_map/ppermute | solution.py:493
  38.9 5.7 %collective-permute-start.3 = (bf16[80,384]{1,0:T(8,128)(2,1)S(1)}, bf16[80,384]{1,0:T(8,128)(2,1)S(1)}, u32[]{:S(2)}, u32[]{:S(2)}) collective-permute-start(bf16[80,384]{1,0:T(8,128)(2,1)S(1)} %get-tuple-element.18), channel_id=1, source_target_pairs={{0,16},{16,0},{8,24},{24,8},{32,48},{48,32},{40,56},{56,40},{64,80... | collective-permute-start | bytes 184328 | tf_op jit(solution)/shard_map/ppermute | solution.py:512
  41.6 7.1 %collective-permute-start.4 = (bf16[80,384]{1,0:T(8,128)(2,1)S(1)}, bf16[80,384]{1,0:T(8,128)(2,1)S(1)}, u32[]{:S(2)}, u32[]{:S(2)}) collective-permute-start(bf16[80,384]{1,0:T(8,128)(2,1)S(1)} %get-tuple-element.20), channel_id=1, source_target_pairs={{16,32},{32,16},{24,40},{40,24},{48,64},{64,48},{56,72},{72,56},{8... | collective-permute-start | bytes 184328 | tf_op jit(solution)/shard_map/ppermute | solution.py:512

commit v7 on v6

--- a/solution.py
+++ b/solution.py
@@ -96,7 +96,7 @@
     facts_ref[...] = stack_rows(lines, FACTS).astype(BF16)
 
 
-def pick_kernel(place_ref, field_ref, own_ref, other_ref, packet_ref, scratch):
+def choose_kernel(place_ref, own_ref, other_ref, chooser_ref, facts_ref):
     own = own_ref[...].astype(F32)
     other = other_ref[...].astype(F32)
     half = place_ref[2]
@@ -108,21 +108,26 @@
         jnp.where(lane < SLOTS, pltpu.roll(first, SLOTS, 1), second),
     )
     place = lax.broadcasted_iota(jnp.int32, (HALF, 2 * SLOTS), 0)
-    choosers, lines = [], []
-    for facts in batches:
+    for batch, facts in enumerate(batches):
+        lanes = pl.ds(batch * 2 * SLOTS, 2 * SLOTS)
         col = (facts[6:7] * 128.0 + facts[7:8]).astype(jnp.int32) - place_ref[4]
-        lines.append((facts[9:10] * ROWS + facts[8:9]).astype(jnp.int32) - place_ref[3])
-        choosers.append(jnp.where(place == col, 1.0, 0.0).astype(BF16))
-    values = jnp.dot(field_ref[...], jnp.concatenate(choosers, axis=1), preferred_element_type=F32)
+        chooser_ref[:, lanes] = jnp.where(place == col, 1.0, 0.0).astype(BF16)
+        facts_ref[:, lanes] = facts.astype(BF16)
+
+
+def pick_kernel(place_ref, field_ref, chooser_ref, facts_ref, packet_ref, scratch):
+    facts = facts_ref[...].astype(F32)
+    line = (facts[9:10] * ROWS + facts[8:9]).astype(jnp.int32) - place_ref[3]
+    values = jnp.dot(field_ref[...], chooser_ref[...], preferred_element_type=F32)
     for batch in range(2):
-        lanes = pl.ds(batch * 2 * SLOTS, 2 * SLOTS)
-        scratch[batch] = values[:, batch * 2 * SLOTS : (batch + 1) * 2 * SLOTS]
+        part = slice(batch * 2 * SLOTS, (batch + 1) * 2 * SLOTS)
+        scratch[batch] = values[:, part]
         total = jnp.zeros((MEMBERS, 2 * SLOTS), F32)
         for index in range(LINES):
             block = scratch[batch, pl.ds(index, MEMBERS, stride=LINES), :]
-            total = total + jnp.where(lines[batch] == index, block, 0.0)
-        packet_ref[pl.ds(0, MEMBERS), lanes] = total.astype(BF16)
-        packet_ref[pl.ds(MEMBERS, FACTS), lanes] = batches[batch].astype(BF16)
+            total = total + jnp.where(line[:, part] == index, block, 0.0)
+        packet_ref[pl.ds(0, MEMBERS), pl.ds(batch * 2 * SLOTS, 2 * SLOTS)] = total.astype(BF16)
+    packet_ref[pl.ds(MEMBERS, FACTS), :] = facts_ref[...]
 
 
 def merge_kernel(place_ref, own_ref, other_ref, beyond_ref, here_ref, first_ref, second_ref):
@@ -451,10 +456,22 @@
     )(place, datum, noise, point, count)
 
 
-def pick(place, field, own, other):
+def choose(place, own, other):
+    smem = pl.BlockSpec(memory_space=pltpu.SMEM)
+    vmem = pl.BlockSpec(memory_space=pltpu.VMEM)
+    return pl.pallas_call(
+        choose_kernel,
+        out_shape=[jax.ShapeDtypeStruct((rows, 4 * SLOTS), BF16) for rows in (HALF, FACTS)],
+        in_specs=[smem, vmem, vmem],
+        out_specs=[vmem, vmem],
+        compiler_params=pltpu.CompilerParams(vmem_limit_bytes=VMEM_LIMIT),
+    )(place, own, other)
+
+
+def pick(place, field, chooser, facts):
     scratch = [pltpu.VMEM((2, MEMBERS * LINES, 2 * SLOTS), F32)]
     return call(
-        pick_kernel, (PACKET, 4 * SLOTS), (place, field, own, other), scratch, 1, 1 << 27, 1 << 19
+        pick_kernel, (PACKET, 4 * SLOTS), (place, field, chooser, facts), scratch, 1, 1 << 27, 1 << 19
     )
 
 
@@ -530,7 +547,8 @@
     message = pack(members[0])
     field = lax.all_to_all(message, "mem", split_axis=0, concat_axis=0, tiled=True)
     facts = state_facts(place, datum, noise, point, count.reshape(2))
-    packet = pick(place, field, facts, swap_cores(facts))
+    chooser, facts = choose(place, facts, swap_cores(facts))
+    packet = pick(place, field, chooser, facts)
     field, packet = lax.optimization_barrier((field, packet))
     beyond = swap_beyond(packet)
     other = swap_cores(packet)

time: 81.5 us -> 79.9 us (0.980)
  the two profiles are of different devices: /device:TPU:71 before, /device:TPU:199 now
where the time goes in v7:
time: 79.9 us; the launch traced here: 79.5 us
  starting transfers between devices  26 us (33%)
  blocking collectives  24.5 us (31%)
  waiting for transfers between devices  17.6 us (22%)
  Pallas kernels  9.45 us (12%)
  local copies, waits for them, and re-layouts  1.82 us (2%)
    all_to_all x1, blocking collectives, on_device(): lax.all_to_all(message, 'mem', split_axis=0, concat_axis=0, tiled=True)  24.5 us
    all_to_all x1, waiting for transfers between devices, on_device(): lax.all_to_all(message, 'mem', split_axis=0, concat_axis=0, tiled=True)  12 us
    all_to_all x1, starting transfers between devices, on_device(): lax.all_to_all(message, 'mem', split_axis=0, concat_axis=0, tiled=True)  11.1 us
    pallas_call x5, Pallas kernels, call(): pl.pallas_call(kernel, out_shape=jax.ShapeDtypeStruct(shape, BF16), in_sp...  7.52 us
    ppermute x2, starting transfers between devices, swap_regions(): return lax.ppermute(block, 'mem', route)  5.68 us
    ppermute x1, starting transfers between devices, swap_beyond(): return lax.ppermute(block, ('mem', 'tile'), route)  4.99 us
    ppermute x2, starting transfers between devices, swap_cores(): lax.ppermute(block, 'mem', [(i, i ^ 1) for i in range(lax.axis_size('mem'...  4.19 us
    ppermute x2, waiting for transfers between devices, swap_regions(): return lax.ppermute(block, 'mem', route)  4.08 us
  transfers between devices with their start and end apart: 6, of which 4 were waited for; matrix products, arithmetic and copies ran while one was open for 0% of the time, Pallas kernels for 2%

profile of v7, /device:TPU:199, one launch (start us, length us, event | category | flops | bytes accessed | tf_op | source)
XLA Modules:
  0.0 79.5 jit_solution(13747348421412454385)
XLA Ops:
  0.0 0.0 copy-start
  0.0 1.0 %copy-done = bf16[1,2,256,512]{3,2,1,0:T(8,128)(2,1)S(1)} copy-done((bf16[1,2,256,512]{3,2,1,0:T(8,128)(2,1)S(1)}, bf16[1,2,256,512]{3,2,1,0:T(8,128)(2,1)}, u32[]{:S(2)}) %copy-start) | copy-done | bytes 524312
  1.0 0.8 %shard_map.55 = bf16[1024,256]{1,0:T(8,128)(2,1)} custom-call(bf16[2,256,512]{2,1,0:T(8,128)(2,1)S(1)} %bitcast.16), custom_call_target="tpu_custom_call" | custom-call | bytes 1048576 | tf_op jit(solution)/shard_map/pallas_call | solution.py:425
  1.9 11.1 %all-to-all-start = ((bf16[64,16,256]{2,1,0:T(8,128)(2,1)}), bf16[64,16,256]{2,1,0:T(8,128)(2,1)S(1)}, u32[]{:S(2)}, u32[]{:S(2)}) async-start(bf16[64,16,256]{2,1,0:T(8,128)(2,1)} %bitcast.7), calls=%async_computation | async-start | bytes 1048576 | tf_op jit(solution)/shard_map/all_to_all | solution.py:548
  13.0 0.0 copy-start.2
  13.0 0.0 copy-start.3
  13.1 0.1 stack.27.place_ref
  13.1 0.0 copy-start.1
  13.1 0.0 copy-start.4
  13.1 0.6 copy-done.2
  13.7 0.0 copy-done.3
  13.7 0.1 copy-done.1
  13.8 0.0 copy-done.4
  13.8 0.6 shard_map.56.own_ref
  14.5 2.3 %collective-permute-start = (bf16[16,128]{1,0:T(8,128)(2,1)S(1)}, bf16[16,128]{1,0:T(8,128)(2,1)S(1)}, u32[]{:S(2)}, u32[]{:S(2)}) collective-permute-start(bf16[16,128]{1,0:T(8,128)(2,1)S(1)} %shard_map.56.own_ref), channel_id=1, source_target_pairs={{0,8},{8,0},{16,24},{24,16},{32,40},{40,32},{48,56},{56,48},{64,72... | collective-permute-start | bytes 12296 | tf_op jit(solution)/shard_map/ppermute | solution.py:510
  16.7 0.8 %collective-permute-done.other_ref = bf16[16,128]{1,0:T(8,128)(2,1)S(1)} collective-permute-done((bf16[16,128]{1,0:T(8,128)(2,1)S(1)}, bf16[16,128]{1,0:T(8,128)(2,1)S(1)}, u32[]{:S(2)}, u32[]{:S(2)}) %collective-permute-start) | collective-permute-done | bytes 4128 | tf_op jit(solution)/shard_map/ppermute | solution.py:510
  17.5 0.7 shard_map.57
  18.2 12.0 %all-to-all-done = bf16[64,16,256]{2,1,0:T(8,128)(2,1)S(1)} async-done(((bf16[64,16,256]{2,1,0:T(8,128)(2,1)}), bf16[64,16,256]{2,1,0:T(8,128)(2,1)S(1)}, u32[]{:S(2)}, u32[]{:S(2)}) %all-to-all-start) | async-done | bytes 524320 | tf_op jit(solution)/shard_map/all_to_all | solution.py:548
  30.2 1.1 %shard_map.58.own_ref = bf16[80,256]{1,0:T(8,128)(2,1)S(1)} custom-call(s32[6]{0:T(128)S(1)} %stack.27.place_ref, bf16[1024,256]{1,0:T(8,128)(2,1)S(1)} %bitcast.13, bf16[256,256]{1,0:T(8,128)(2,1)S(1)} %get-tuple-element.15.chooser_ref, bf16[16,256]{1,0:T(8,128)(2,1)S(1)} %get-tuple-element.16.facts_ref), custom_call_target="tpu_custom_call" | custom-call | flops 134217728 | bytes 524288 | tf_op jit(solution)/shard_map/pallas_call | solution.py:425
  31.3 5.0 %collective-permute-start.2 = (bf16[80,256]{1,0:T(8,128)(2,1)S(1)}, bf16[80,256]{1,0:T(8,128)(2,1)S(1)}, u32[]{:S(2)}, u32[]{:S(2)}) collective-permute-start(bf16[80,256]{1,0:T(8,128)(2,1)S(1)} %shard_map.58.own_ref), channel_id=1, source_target_pairs={{8,1},{1,8},{9,2},{2,9},{10,3},{3,10},{11,4},{4,11},{12,5},{5,12},... | collective-permute-start | bytes 122888 | tf_op jit(solution)/shard_map/ppermute | solution.py:520
  36.3 1.9 %collective-permute-start.1 = (bf16[80,256]{1,0:T(8,128)(2,1)S(1)}, bf16[80,256]{1,0:T(8,128)(2,1)S(1)}, u32[]{:S(2)}, u32[]{:S(2)}) collective-permute-start(bf16[80,256]{1,0:T(8,128)(2,1)S(1)} %shard_map.58.own_ref), channel_id=1, source_target_pairs={{0,8},{8,0},{16,24},{24,16},{32,40},{40,32},{48,56},{56,48},{64,72... | collective-permute-start | bytes 122888 | tf_op jit(solution)/shard_map/ppermute | solution.py:510
  38.2 0.4 shard_map.59.cells_ref
  38.7 0.0 collective-permute-done.2.beyond_ref
  38.7 0.8 collective-permute-done.1.other_ref
  39.4 0.6 shard_map.60
  40.1 2.7 %collective-permute-start.3 = (bf16[80,384]{1,0:T(8,128)(2,1)S(1)}, bf16[80,384]{1,0:T(8,128)(2,1)S(1)}, u32[]{:S(2)}, u32[]{:S(2)}) collective-permute-start(bf16[80,384]{1,0:T(8,128)(2,1)S(1)} %get-tuple-element.22), channel_id=1, source_target_pairs={{0,16},{16,0},{8,24},{24,8},{32,48},{48,32},{40,56},{56,40},{64,80... | collective-permute-start | bytes 184328 | tf_op jit(solution)/shard_map/ppermute | solution.py:529
  42.8 3.0 %collective-permute-start.4 = (bf16[80,384]{1,0:T(8,128)(2,1)S(1)}, bf16[80,384]{1,0:T(8,128)(2,1)S(1)}, u32[]{:S(2)}, u32[]{:S(2)}) collective-permute-start(bf16[80,384]{1,0:T(8,128)(2,1)S(1)} %get-tuple-element.24), channel_id=1, source_target_pairs={{16,32},{32,16},{24,40},{40,24},{48,64},{64,48},{56,72},{72,56},{8... | collective-permute-start | bytes 184328 | tf_op jit(solution)/shard_map/ppermute | solution.py:529
  45.8 0.0 collective-permute-done.3.next_ref
  45.8 4.1 %collective-permute-done.4.last_ref = bf16[80,384]{1,0:T(8,128)(2,1)S(1)} collective-permute-done((bf16[80,384]{1,0:T(8,128)(2,1)S(1)}, bf16[80,384]{1,0:T(8,128)(2,1)S(1)}, u32[]{:S(2)}, u32[]{:S(2)}) %collective-permute-start.4) | collective-permute-done | bytes 61472 | tf_op jit(solution)/shard_map/ppermute | solution.py:529
  49.9 4.3 %shard_map.61 = bf16[1024,256]{1,0:T(8,128)(2,1)S(1)} custom-call(s32[6]{0:T(128)S(1)} %stack.27.place_ref, bf16[2,64,2048]{2,1,0:T(8,128)(2,1)S(1)} %shard_map.59.cells_ref, bf16[80,384]{1,0:T(8,128)(2,1)S(1)} %collective-permute-done.3.next_ref, bf16[80,512]{1,0:T(8,128)(2,1)S(1)} %get-tuple-element.23.here_ref, ...), custom_call_target="tpu_custom_call" | custom-call | flops 1073741824 | bytes 1048576 | tf_op jit(solution)/shard_map/pallas_call | solution.py:425
  54.2 24.5 %all_to_all.22 = bf16[64,16,256]{2,1,0:T(8,128)(2,1)S(1)} all-to-all(bf16[64,16,256]{2,1,0:T(8,128)(2,1)S(1)} %bitcast.17), channel_id=1, replica_groups=mesh['mem'=64,'tile'=8] {'mem'}, dimensions={0} | all-to-all | bytes 1048576 | tf_op jit(solution)/shard_map/all_to_all | solution.py:559
  78.7 0.8 %shard_map.62 = bf16[2,256,512]{2,1,0:T(8,128)(2,1)} custom-call(bf16[1024,256]{1,0:T(8,128)(2,1)S(1)} %bitcast.15), custom_call_target="tpu_custom_call" | custom-call | bytes 1048576 | tf_op jit(solution)/shard_map/pallas_call | solution.py:425
Async XLA Ops:
  0.0 1.0 %copy-start = (bf16[1,2,256,512]{3,2,1,0:T(8,128)(2,1)S(1)}, bf16[1,2,256,512]{3,2,1,0:T(8,128)(2,1)}, u32[]{:S(2)}) copy-start(bf16[1,2,256,512]{3,2,1,0:T(8,128)(2,1)} %param.5) | copy-start | bytes 1572868
  1.9 28.3 %all-to-all-start = ((bf16[64,16,256]{2,1,0:T(8,128)(2,1)}), bf16[64,16,256]{2,1,0:T(8,128)(2,1)S(1)}, u32[]{:S(2)}, u32[]{:S(2)}) async-start(bf16[64,16,256]{2,1,0:T(8,128)(2,1)} %bitcast.7), calls=%async_computation | async-start | bytes 1048576 | tf_op jit(solution)/shard_map/all_to_all | solution.py:548
  13.0 0.7 copy-start.2
  13.0 0.7 copy-start.3
  13.1 0.7 copy-start.1
  13.1 0.7 copy-start.4
  14.5 3.1 %collective-permute-start = (bf16[16,128]{1,0:T(8,128)(2,1)S(1)}, bf16[16,128]{1,0:T(8,128)(2,1)S(1)}, u32[]{:S(2)}, u32[]{:S(2)}) collective-permute-start(bf16[16,128]{1,0:T(8,128)(2,1)S(1)} %shard_map.56.own_ref), channel_id=1, source_target_pairs={{0,8},{8,0},{16,24},{24,16},{32,40},{40,32},{48,56},{56,48},{64,72... | collective-permute-start | bytes 12296 | tf_op jit(solution)/shard_map/ppermute | solution.py:510
  31.3 7.3 %collective-permute-start.2 = (bf16[80,256]{1,0:T(8,128)(2,1)S(1)}, bf16[80,256]{1,0:T(8,128)(2,1)S(1)}, u32[]{:S(2)}, u32[]{:S(2)}) collective-permute-start(bf16[80,256]{1,0:T(8,128)(2,1)S(1)} %shard_map.58.own_ref), channel_id=1, source_target_pairs={{8,1},{1,8},{9,2},{2,9},{10,3},{3,10},{11,4},{4,11},{12,5},{5,12},... | collective-permute-start | bytes 122888 | tf_op jit(solution)/shard_map/ppermute | solution.py:520
  36.3 3.1 %collective-permute-start.1 = (bf16[80,256]{1,0:T(8,128)(2,1)S(1)}, bf16[80,256]{1,0:T(8,128)(2,1)S(1)}, u32[]{:S(2)}, u32[]{:S(2)}) collective-permute-start(bf16[80,256]{1,0:T(8,128)(2,1)S(1)} %shard_map.58.own_ref), channel_id=1, source_target_pairs={{0,8},{8,0},{16,24},{24,16},{32,40},{40,32},{48,56},{56,48},{64,72... | collective-permute-start | bytes 122888 | tf_op jit(solution)/shard_map/ppermute | solution.py:510
  40.1 5.7 %collective-permute-start.3 = (bf16[80,384]{1,0:T(8,128)(2,1)S(1)}, bf16[80,384]{1,0:T(8,128)(2,1)S(1)}, u32[]{:S(2)}, u32[]{:S(2)}) collective-permute-start(bf16[80,384]{1,0:T(8,128)(2,1)S(1)} %get-tuple-element.22), channel_id=1, source_target_pairs={{0,16},{16,0},{8,24},{24,8},{32,48},{48,32},{40,56},{56,40},{64,80... | collective-permute-start | bytes 184328 | tf_op jit(solution)/shard_map/ppermute | solution.py:529
  42.8 7.1 %collective-permute-start.4 = (bf16[80,384]{1,0:T(8,128)(2,1)S(1)}, bf16[80,384]{1,0:T(8,128)(2,1)S(1)}, u32[]{:S(2)}, u32[]{:S(2)}) collective-permute-start(bf16[80,384]{1,0:T(8,128)(2,1)S(1)} %get-tuple-element.24), channel_id=1, source_target_pairs={{16,32},{32,16},{24,40},{40,24},{48,64},{64,48},{56,72},{72,56},{8... | collective-permute-start | bytes 184328 | tf_op jit(solution)/shard_map/ppermute | solution.py:529
